TPU v7x, 256 devices: a whole 4x4x8 slice. The times are simulated.
256 devices in a mesh: replica: 8 (over y, x_hi), fsdp: 32 (over x_lo, z, core).
Axes of the slice: x: 4 (x_hi: 2, x_lo: 2; x = x_hi * 2 + x_lo), y: 4, z: 8, core: 2. Of those that a mesh axis runs over, the one named last changes fastest.
Arguments:
- token_ids: int32 [32768], P(('replica', 'fsdp')), may hold values from 0 to 128000, as said below
- inputs: bfloat16 [32768, 8192], P(('replica', 'fsdp')), may hold values from -24 to 24
- key_cotangent: bfloat16 [32768, 768], P(('replica', 'fsdp')), may hold values from -6 to 6
- key_weight: float32 [8, 8192, 768], P('replica', 'fsdp'), may hold values from -0.0625 to 0.0625
- adam_m: float32 [8, 8192, 768], P('replica', 'fsdp'), may hold values from -0.25 to 0.25
- adam_v: float32 [8, 8192, 768], P('replica', 'fsdp'), may hold values from 2.4414063e-05 to 0.0024414062
- frag_local: float32 [8, 3, 8192, 512], P('replica', None, 'fsdp'), may hold values from -0.0625 to 0.0625
- frag_global: float32 [8, 8192, 512], P('replica', 'fsdp'), may hold values from -0.0625 to 0.0625
- outer_mom: float32 [8, 8192, 512], P('replica', 'fsdp'), may hold values from -0.15625 to 0.15625
- owner: int32 [32], P('fsdp'), may hold values from 0 to 7
- fragment: int32 [8], P('replica'), may hold values from 0 to 2
Outputs:
- input_cotangent: bfloat16 [32768, 8192], P(('replica', 'fsdp'))
- new_weight: float32 [8, 8192, 768], P('replica', 'fsdp')
- new_m: float32 [8, 8192, 768], P('replica', 'fsdp')
- new_v: float32 [8, 8192, 768], P('replica', 'fsdp')
- synced: float32 [8, 8192, 512], P('replica', 'fsdp')
- new_outer_mom: float32 [8, 8192, 512], P('replica', 'fsdp')
Inputs may be any that keep to these rules, and one draw needn't show every extreme that they name: `token_ids`: token 0 of every replica's sequence of 4096 tokens is 128000, the id that begins a document; the same id begins every later document.
All inputs are finite; a program needn't handle non-finite values.
Results may differ from a plain program's by a relative error of at most 0.0095.
Values may be sent and summed in bfloat16 or wider, within the bound.
No kernel may reach another device: no remote copies, remote signals or barrier semaphores. Data moves between devices by JAX's collectives and lax.ppermute only.
A program may use at most 128 MiB of HBM per device.

v0:
```python
import jax
import jax.numpy as jnp
from jax import lax
from jax.sharding import PartitionSpec as P

HEAD = 128


begin_token = 128000
rope_base = 500000.0
beta_one = 0.9
beta_two = 0.95
adam_lr = 0.001
adam_eps = 1e-08
adam_step = 10.0
weight_decay = 0.1
outer_lr = 0.7
outer_momentum = 0.9


def prefix(part, axis, combine, identity):
    place = lax.axis_index(axis)
    gathered = lax.all_gather(part, axis)
    state = jnp.zeros_like(part) + jnp.asarray(identity, part.dtype)

    def one(step, state):
        return combine(state, lax.dynamic_index_in_dim(gathered, step, 0, False))

    return lax.fori_loop(0, place, one, state)


def from_root(value, axis, source):
    kept = jnp.where(lax.axis_index(axis) == source, value, 0).astype(value.dtype)
    return lax.psum(kept, axis)


def unrotate(cotangent, positions):
    row_count = cotangent.shape[0]
    head_count = cotangent.shape[1] // HEAD
    half_head = HEAD // 2
    frequency = jnp.float32(rope_base) ** (
        -(jnp.arange(half_head, dtype=jnp.float32) * (2.0 / HEAD))
    )
    angles = positions.astype(jnp.float32)[:, None] * frequency[None, :]
    cosine = jnp.cos(angles)[:, None, :]
    sine_part = jnp.sin(angles)[:, None, :]
    per_head = cotangent.astype(jnp.float32).reshape(row_count, head_count, HEAD)
    front_half = per_head[..., :half_head]
    back_half = per_head[..., half_head:]
    turned = jnp.concatenate(
        [front_half * cosine + back_half * sine_part, back_half * cosine - front_half * sine_part],
        axis=-1,
    )
    return turned.reshape(row_count, head_count * HEAD).astype(jnp.bfloat16)


def on_device(
    token_ids,
    inputs,
    key_cotangent,
    key_weight,
    adam_m,
    adam_v,
    frag_local,
    frag_global,
    outer_mom,
    owner,
    fragment,
):
    rows_here = inputs.shape[0]
    fsdp_size = lax.axis_size("fsdp")
    seq_len = rows_here * fsdp_size
    first_row = lax.axis_index("fsdp") * rows_here
    token_index = first_row + jnp.arange(rows_here, dtype=jnp.int32)
    starts = jnp.where(token_ids == begin_token, token_index, -1)
    earlier = prefix(jnp.max(starts), "fsdp", jnp.maximum, jnp.int32(-1))
    latest = jnp.maximum(lax.cummax(starts, axis=0), earlier)
    key_grad = unrotate(key_cotangent, token_index - latest)
    weight_bf = key_weight[0].astype(jnp.bfloat16)
    input_cotangent = lax.dot_general(
        key_grad,
        lax.all_gather(weight_bf, "fsdp", axis=0, tiled=True),
        (((1,), (1,)), ((), ())),
        preferred_element_type=jnp.float32,
    ).astype(jnp.bfloat16)
    weight_sum = lax.psum_scatter(
        lax.dot_general(
            inputs, key_grad, (((0,), (0,)), ((), ())), preferred_element_type=jnp.float32
        ).astype(jnp.bfloat16),
        "fsdp",
        scatter_dimension=0,
        tiled=True,
    ).astype(jnp.float32)
    weight_grad = (weight_sum / seq_len)[None]
    moment_mean = beta_one * adam_m + (1.0 - beta_one) * weight_grad
    moment_square = beta_two * adam_v + (1.0 - beta_two) * weight_grad * weight_grad
    mean_hat = moment_mean / (1.0 - beta_one**adam_step)
    square_hat = moment_square / (1.0 - beta_two**adam_step)
    new_weight = key_weight - adam_lr * (
        mean_hat / (jnp.sqrt(square_hat) + adam_eps) + weight_decay * key_weight
    )
    owner_rank = owner[0]
    replica_count = lax.axis_size("replica")
    replica_rank = lax.axis_index("replica")
    is_owner = replica_rank == owner_rank
    local_slot = lax.dynamic_index_in_dim(frag_local[0], fragment[0], 0, keepdims=False)
    state_global, state_mom = (
        from_root(frag_global[0].astype(jnp.bfloat16), "replica", owner_rank).astype(jnp.float32),
        from_root(outer_mom[0].astype(jnp.bfloat16), "replica", owner_rank).astype(jnp.float32),
    )
    replica_total = lax.psum(local_slot.astype(jnp.bfloat16), "replica").astype(jnp.float32)
    outer_grad = state_global - replica_total / replica_count
    mom_next = outer_momentum * state_mom + outer_grad
    synced = state_global - outer_lr * (outer_grad + outer_momentum * mom_next)
    new_outer_mom = jnp.where(is_owner, mom_next, outer_mom[0])[None]
    return (input_cotangent, new_weight, moment_mean, moment_square, synced[None], new_outer_mom)


def solution(mesh):
    in_specs = (
        P(("replica", "fsdp")),
        P(("replica", "fsdp"), None),
        P(("replica", "fsdp"), None),
        P("replica", "fsdp", None),
        P("replica", "fsdp", None),
        P("replica", "fsdp", None),
        P("replica", None, "fsdp", None),
        P("replica", "fsdp", None),
        P("replica", "fsdp", None),
        P("fsdp"),
        P("replica"),
    )
    out_specs = (
        P(("replica", "fsdp"), None),
        P("replica", "fsdp", None),
        P("replica", "fsdp", None),
        P("replica", "fsdp", None),
        P("replica", "fsdp", None),
        P("replica", "fsdp", None),
    )
    return jax.shard_map(
        on_device, mesh=mesh, in_specs=in_specs, out_specs=out_specs, check_vma=False
    )
```

profile of v0, /device:TPU:1, one launch (start us, length us, event | category | flops | bytes accessed | tf_op | source)
XLA Modules:
  0.0 271.1 jit_solution(17986854767635538785)
XLA Ops:
  8.0 0.0 copy-start
  8.0 0.0 copy-start.3
  8.0 0.0 copy-start.1
  8.0 0.0 copy-start.2
  8.0 0.0 all-reduce.4.cloned.1.call-start
  8.9 1.8 select_bitcast_fusion
  10.7 1.8 fusion.14
  13.1 1.8 fusion.13
  14.9 0.0 all-reduce.4.cloned.1.call-update
  14.9 0.0 all-gather.3.cloned.1.call-start
  14.9 1.9 convert_element_type.57
  16.9 0.0 all-gather.3.cloned.1.call-update
  16.9 0.0 reduce-scatter.2.cloned.1.call-start
  16.9 0.0 copy-done.1
  17.0 0.2 copy.25
  17.2 0.0 copy-done.2
  17.2 0.6 fusion.15
  17.8 0.1 copy.26
  17.9 0.2 reduce-window.8
  18.1 0.0 copy-done.3
  18.1 0.6 dynamic-slice.1
  18.7 1.3 dynamic-update-slice
  20.0 17.3 %all-reduce = s32[32]{0:T(128)S(1)} all-reduce(s32[32]{0:T(128)S(1)} %dynamic-update-slice), channel_id=1, replica_groups=mesh['replica'=8,'fsdp'=32] {'fsdp'}, use_global_device_ids=true, to_apply=%add | all-reduce | flops 32 | bytes 256
  37.3 1.2 while.10
  37.3 0.6 dynamic_slice.13
  38.6 0.1 maximum_reduce_fusion
  38.7 0.2 multiply_cosine_fusion
  38.9 0.1 add_convert_fusion
  39.0 0.0 copy-done
  39.0 6.4 %fusion.2 = bf16[8192,768]{0,1:T(8,128)(2,1)} fusion(bf16[128,768]{0,1:T(8,128)(2,1)S(1)} %bitcast.51, bf16[128,8192]{1,0:T(8,128)(2,1)S(1)} %copy-done), kind=kOutput, calls=%fused_computation.3 | convolution fusion | flops 1616904192 | bytes 14876672 | tf_op jit(solution)/shard_map/dot_general | solution.py:87
  45.4 0.0 reduce-scatter.2.cloned.1.call-update
  45.4 1.4 copy.30
  46.8 2.3 copy.27
  49.1 2.3 copy.28
  51.4 83.1 %all-reduce.4.cloned.1.call-done = (bf16[256,512]{1,0:T(8,128)(2,1)}, bf16[256,512]{1,0:T(8,128)(2,1)}, bf16[256,512]{1,0:T(8,128)(2,1)}) async-done(((bf16[256,512]{1,0:T(8,128)(2,1)}, bf16[256,512]{1,0:T(8,128)(2,1)}, bf16[256,512]{1,0:T(8,128)(2,1)}), (bf16[256,512]{1,0:T(8,128)(2,1)}, bf16[256,512]{1,0:T(8,128)(2,1)}, bf16[256,512]{1,0:T(8,128)(2,1)})) %all-reduce.4.cloned.1.call-update) | async-done | bytes 786448 | tf_op jit(solution)/shard_map/psum | solution.py:34
  134.4 2.4 fusion.12
  136.9 0.0 all-gather.3.cloned.1.call-done
  136.9 10.3 %fusion.3 = bf16[128,8192]{1,0:T(8,128)(2,1)} fusion(bf16[128,768]{0,1:T(8,128)(2,1)S(1)} %bitcast.52, bf16[1,8192,768]{2,1,0:T(8,128)(2,1)} %all-gather.3.cloned.1.call-done), kind=kOutput, calls=%fused_computation.4 | convolution fusion | flops 1611661312 | bytes 14876672 | tf_op jit(solution)/shard_map/dot_general | solution.py:80
  147.2 106.4 %reduce-scatter.2.cloned.1.call-done = bf16[256,768]{0,1:T(8,128)(2,1)} async-done(((bf16[8192,768]{0,1:T(8,128)(2,1)}), bf16[256,768]{0,1:T(8,128)(2,1)}) %reduce-scatter.2.cloned.1.call-update) | async-done | bytes 393232 | tf_op jit(solution)/shard_map/reduce_scatter | solution.py:86
  253.5 3.3 %multiply_subtract_fusion = (f32[1,256,768]{1,2,0:T(8,128)}, f32[1,256,768]{1,2,0:T(8,128)}, f32[1,256,768]{1,2,0:T(8,128)}) fusion(f32[1,256,768]{1,2,0:T(8,128)S(1)} %copy.30, bf16[256,768]{0,1:T(8,128)(2,1)} %reduce-scatter.2.cloned.1.call-done, f32[1,256,768]{1,2,0:T(8,128)} %copy.27, f32[1,256,768]{1,2,0:T(8,128)} %copy.28), kind=kLoop, calls=%fused_computation.13 | loop fusion | flops 3342336 | bytes 5111808 | tf_op jit(solution)/shard_map/sub | solution.py:99
  256.8 2.3 copy.31
  259.1 2.3 copy.32
  261.4 2.3 copy.33
  (5 shorter events, 0.1 us)
Async XLA Ops:
  8.0 31.0 %copy-start = (bf16[128,8192]{1,0:T(8,128)(2,1)S(1)}, bf16[128,8192]{1,0:T(8,128)(2,1)}, u32[]{:S(2)}) copy-start(bf16[128,8192]{1,0:T(8,128)(2,1)} %param.14) | copy-start | bytes 6291460
  8.0 10.1 %copy-start.3 = (u32[256]{0:T(256)S(1)}, u32[256]{0:T(256)}, u32[]{:S(2)}) copy-start(u32[256]{0:T(256)} %constant.84) | copy-start | bytes 3076
  8.0 8.9 %copy-start.1 = (bf16[128,768]{1,0:T(8,128)(2,1)S(1)}, bf16[128,768]{1,0:T(8,128)(2,1)}, u32[]{:S(2)}) copy-start(bf16[128,768]{1,0:T(8,128)(2,1)} %param.15) | copy-start | bytes 589828
  8.0 9.1 %copy-start.2 = (s32[128]{0:T(128)S(1)}, s32[128]{0:T(128)}, u32[]{:S(2)}) copy-start(s32[128]{0:T(128)} %param.13) | copy-start | bytes 1540
  8.0 126.4 %all-reduce.4.cloned.1.call-start = ((), (), s32[]{:S(2)}) async-start(), calls=%async_computation.3 | async-start | bytes 1572864 | tf_op jit(solution)/shard_map/psum | solution.py:34
  14.9 122.0 %all-gather.3.cloned.1.call-start = ((), (), s32[]{:S(2)}) async-start(), calls=%async_computation.2 | async-start | bytes 12976128 | tf_op jit(solution)/shard_map/all_gather | solution.py:82
  16.9 236.6 %reduce-scatter.2.cloned.1.call-start = ((), (), s32[]{:S(2)}) async-start(), calls=%async_computation.1 | async-start | bytes 12976128 | tf_op jit(solution)/shard_map/reduce_scatter | solution.py:86
Sparse Core Ops, SparseCore 0:
  15.0 119.3 all-reduce.3
Sparse Core Ops, SparseCore 1:
  17.8 101.4 all-gather.2
  121.7 131.8 reduce-scatter.1
where the time goes:
time: 275 us; the launch traced here: 271 us
  waiting for transfers between devices  189 us (69%)
  local copies, waits for them, and re-layouts  17.3 us (6%)
  blocking collectives  17.3 us (6%)
  between operations  17.1 us (6%)
  matrix products  16.7 us (6%)
  other arithmetic  12.4 us (5%)
    reduce_scatter x1, waiting for transfers between devices, on_device(): lax.psum_scatter(lax.dot_general(inputs, key_grad, (((0,), (0,)), ((), ()...  106 us
    psum x1, waiting for transfers between devices, from_root(): return lax.psum(kept, axis)  83.1 us
    unnamed x1, blocking collectives  17.3 us
    unnamed x18, local copies, waits for them, and re-layouts  14.9 us
    dot_general x1, matrix products, on_device(): lax.dot_general(key_grad, lax.all_gather(weight_bf, 'fsdp', axis=0, tiled...  10.3 us
    dot_general x1, matrix products, on_device(): lax.dot_general(inputs, key_grad, (((0,), (0,)), ((), ())), preferred_ele...  6.38 us
  transfers between devices with their start and end apart: 3, of which 2 were waited for; matrix products, arithmetic and copies ran while one was open for 11% of the time, Pallas kernels for 0%

commit v1 on v0

v1 whole, which is shorter than its diff:
```python
import jax
import jax.numpy as jnp
from jax import lax
from jax.experimental import pallas as pl
from jax.experimental.pallas import tpu as pltpu
from jax.sharding import PartitionSpec as P

HEAD = 128
N_X, N_Z, N_CORE = 2, 8, 2

begin_token = 128000
rope_base = 500000.0
beta_one = 0.9
beta_two = 0.95
adam_lr = 0.001
adam_eps = 1e-08
adam_step = 10.0
weight_decay = 0.1
outer_lr = 0.7
outer_momentum = 0.9

PLACES = [(x, z, c) for x in range(N_X) for z in range(N_Z) for c in range(N_CORE)]
PEERS = [(0, 0), (0, 1), (1, 0), (1, 1)]


def place(x, z, c):
    return (x * N_Z + z % N_Z) * N_CORE + c


def along_z(value, distance):
    pairs = [(place(x, z, c), place(x, z + distance, c)) for x, z, c in PLACES]
    return lax.ppermute(value, "fsdp", pairs)


def with_peer(value, peer):
    flip_x, flip_c = PEERS[peer]
    pairs = [(place(x, z, c), place(x ^ flip_x, z, c ^ flip_c)) for x, z, c in PLACES]
    return lax.ppermute(value, "fsdp", pairs)


def unrotate_angles(positions):
    half_head = HEAD // 2
    frequency = jnp.float32(rope_base) ** (
        -(jnp.arange(half_head, dtype=jnp.float32) * (2.0 / HEAD))
    )
    return positions.astype(jnp.float32)[:, None] * frequency[None, :]


def place_index(x, z, c, peer):
    flip_x, flip_c = PEERS[peer]
    return ((x ^ flip_x) * N_Z + z) * N_CORE + (c ^ flip_c)


def peer_positions(token_ids, x, z, c):
    rows = token_ids.shape[0]
    ids = jnp.stack([token_ids] + [with_peer(token_ids, p) for p in (1, 2, 3)])
    indices = jnp.stack([place_index(x, z, c, p) for p in range(4)])
    token_index = indices[:, None] * rows + jnp.arange(rows, dtype=jnp.int32)[None, :]
    starts = jnp.where(ids == begin_token, token_index, -1)
    rank = jnp.arange(N_Z, dtype=jnp.int32)
    newest = jnp.where((rank == z)[:, None], jnp.max(starts, axis=1)[None, :], -1)
    for distance in (1, 2, 4):
        newest = jnp.maximum(newest, along_z(newest, distance))
    all_indices = jnp.stack([place_index(x, rank, c, p) for p in range(4)], axis=1)
    before = all_indices[None, :, :] < indices[:, None, None]
    earlier = jnp.max(jnp.where(before, newest[None], -1), axis=(1, 2))
    lane = jnp.arange(rows, dtype=jnp.int32)
    upto = lane[None, :] <= lane[:, None]
    latest = jnp.max(jnp.where(upto[None], starts[:, None, :], -1), axis=2)
    return token_index - jnp.maximum(latest, earlier[:, None])


def unrotate(cotangent, positions):
    row_count = cotangent.shape[0]
    head_count = cotangent.shape[1] // HEAD
    half_head = HEAD // 2
    angles = unrotate_angles(positions)
    cosine = jnp.cos(angles)[:, None, :]
    sine_part = jnp.sin(angles)[:, None, :]
    per_head = cotangent.astype(jnp.float32).reshape(row_count, head_count, HEAD)
    front_half = per_head[..., :half_head]
    back_half = per_head[..., half_head:]
    turned = jnp.concatenate(
        [front_half * cosine + back_half * sine_part, back_half * cosine - front_half * sine_part],
        axis=-1,
    )
    return turned.reshape(row_count, head_count * HEAD).astype(jnp.bfloat16)


NEAR = (0, 1, -1, 2, -2)
FAR = (3, -3, 4)


def column_of(base_ref, peer, ahead, width):
    step = lax.rem(base_ref[4] + (ahead + N_Z), N_Z)
    return pl.multiple_of(base_ref[peer] + step * (N_CORE * width), width)


def pack_columns(inputs, bases, width):
    tokens = inputs.shape[0]

    def kernel(base_ref, in_ref, *refs):
        outs, sem = refs[:8], refs[8]
        copies = []
        for part, steps in enumerate((NEAR, FAR)):
            for peer in range(4):
                for at, ahead in enumerate(steps):
                    copies.append(
                        pltpu.make_async_copy(
                            in_ref.at[:, pl.ds(column_of(base_ref, peer, ahead, width), width)],
                            outs[part * 4 + peer].at[:, pl.ds(at * width, width)],
                            sem.at[len(copies)],
                        )
                    )
        for copy in copies:
            copy.start()
        for copy in copies:
            copy.wait()

    shapes = [(tokens, len(steps) * width) for steps in (NEAR, FAR) for _ in range(4)]
    packed = pl.pallas_call(
        kernel,
        out_shape=[jax.ShapeDtypeStruct(shape, inputs.dtype) for shape in shapes],
        in_specs=[pl.BlockSpec(memory_space=pltpu.SMEM), pl.BlockSpec(memory_space=pl.ANY)],
        out_specs=[pl.BlockSpec(memory_space=pltpu.VMEM)] * 8,
        scratch_shapes=[pltpu.SemaphoreType.DMA((4 * N_Z,))],
        cost_estimate=pl.CostEstimate(flops=0, bytes_accessed=4 * inputs.size, transcendentals=0),
    )(bases, inputs)
    return packed[:4], packed[4:]


def unpack_columns(near, far, bases, width):
    tokens = near[0].shape[0]
    columns = 4 * N_Z * width

    def kernel(base_ref, *refs):
        ins, out_ref, sem = refs[:8], refs[8], refs[9]
        copies = []
        for part, steps in enumerate((NEAR, FAR)):
            for peer in range(4):
                for at, ahead in enumerate(steps):
                    copies.append(
                        pltpu.make_async_copy(
                            ins[part * 4 + peer].at[:, pl.ds(at * width, width)],
                            out_ref.at[:, pl.ds(column_of(base_ref, peer, ahead, width), width)],
                            sem.at[len(copies)],
                        )
                    )
        for copy in copies:
            copy.start()
        for copy in copies:
            copy.wait()

    return pl.pallas_call(
        kernel,
        out_shape=jax.ShapeDtypeStruct((tokens, columns), near[0].dtype),
        in_specs=[pl.BlockSpec(memory_space=pltpu.SMEM)] + [pl.BlockSpec(memory_space=pltpu.VMEM)] * 8,
        out_specs=pl.BlockSpec(memory_space=pl.ANY),
        scratch_shapes=[pltpu.SemaphoreType.DMA((4 * N_Z,))],
        cost_estimate=pl.CostEstimate(flops=0, bytes_accessed=4 * tokens * columns, transcendentals=0),
    )(bases, *near, *far)


def back_products(grads, weights):
    tokens, depth = grads.shape[1:]
    rows = weights[0].shape[0]
    count = len(weights)

    def kernel(g_ref, *refs):
        w_refs, outs = refs[:count], refs[count:]
        grad = g_ref[...].reshape(4 * tokens, depth)
        for at, w_ref in enumerate(w_refs):
            product = lax.dot_general(
                grad, w_ref[...], (((1,), (1,)), ((), ())), preferred_element_type=jnp.float32
            ).astype(jnp.bfloat16)
            for peer in range(4):
                outs[peer][:, at * rows : (at + 1) * rows] = product[peer * tokens : (peer + 1) * tokens]

    return pl.pallas_call(
        kernel,
        out_shape=[jax.ShapeDtypeStruct((tokens, count * rows), jnp.bfloat16)] * 4,
        in_specs=[pl.BlockSpec(memory_space=pltpu.VMEM)] * (1 + count),
        out_specs=[pl.BlockSpec(memory_space=pltpu.VMEM)] * 4,
        cost_estimate=pl.CostEstimate(
            flops=8 * tokens * depth * count * rows,
            bytes_accessed=2 * (4 * tokens * depth + count * rows * depth + 4 * tokens * count * rows),
            transcendentals=0,
        ),
    )(grads, *weights)


def weight_products(rows_in, grads, blocks):
    tokens, depth = grads.shape[1:]
    rows = rows_in[0].shape[1] // blocks

    def kernel(g_ref, *refs):
        ins, outs = refs[:4], refs[4:]
        for at, out in enumerate(outs):
            total = None
            for peer in range(4):
                term = lax.dot_general(
                    ins[peer][:, at * rows : (at + 1) * rows],
                    g_ref[peer],
                    (((0,), (0,)), ((), ())),
                    preferred_element_type=jnp.float32,
                )
                total = term if total is None else total + term
            out[...] = total.astype(jnp.bfloat16)

    return pl.pallas_call(
        kernel,
        out_shape=[jax.ShapeDtypeStruct((rows, depth), jnp.bfloat16)] * blocks,
        in_specs=[pl.BlockSpec(memory_space=pltpu.VMEM)] * 5,
        out_specs=[pl.BlockSpec(memory_space=pltpu.VMEM)] * blocks,
        cost_estimate=pl.CostEstimate(
            flops=8 * tokens * depth * blocks * rows,
            bytes_accessed=2 * (4 * tokens * depth + blocks * rows * depth + 4 * tokens * blocks * rows),
            transcendentals=0,
        ),
    )(grads, *rows_in)


def adam(forward, backward, own, key_weight, adam_m, adam_v, seq_len):
    rows, columns = own.shape
    step_rows = rows // 4

    def kernel(f_ref, b_ref, o_ref, w_ref, m_ref, v_ref, nw_ref, nm_ref, nv_ref):
        total = (
            f_ref[...].astype(jnp.float32)
            + b_ref[...].astype(jnp.float32)
            + o_ref[...].astype(jnp.float32)
        )
        grad = total / seq_len
        weight = w_ref[0]
        mean = beta_one * m_ref[0] + (1.0 - beta_one) * grad
        square = beta_two * v_ref[0] + (1.0 - beta_two) * grad * grad
        mean_hat = mean / (1.0 - beta_one**adam_step)
        square_hat = square / (1.0 - beta_two**adam_step)
        nm_ref[0] = mean
        nv_ref[0] = square
        nw_ref[0] = weight - adam_lr * (
            mean_hat / (jnp.sqrt(square_hat) + adam_eps) + weight_decay * weight
        )

    flat = pl.BlockSpec((step_rows, columns), lambda i: (i, 0))
    deep = pl.BlockSpec((1, step_rows, columns), lambda i: (0, i, 0))
    return pl.pallas_call(
        kernel,
        grid=(4,),
        out_shape=[jax.ShapeDtypeStruct((1, rows, columns), jnp.float32)] * 3,
        in_specs=[flat] * 3 + [deep] * 3,
        out_specs=[deep] * 3,
        cost_estimate=pl.CostEstimate(flops=20 * own.size, bytes_accessed=30 * own.size, transcendentals=own.size),
    )(forward, backward, own, key_weight, adam_m, adam_v)


def ring_gather(block):
    half = block.shape[0] // 2
    held = {0: block}
    behind = ahead = block
    for step in (1, 2, 3):
        behind, ahead = along_z(behind, 1), along_z(ahead, -1)
        held[-step], held[step] = behind, ahead
    held[4] = jnp.concatenate([along_z(behind[:half], 1), along_z(ahead[half:], -1)])
    return held


def added(arrived, term):
    return (arrived.astype(jnp.float32) + term.astype(jnp.float32)).astype(jnp.bfloat16)


def ring_reduce_far(blocks):
    half = blocks[4].shape[0] // 2
    forward = along_z(blocks[4][:half], 1)
    backward = along_z(blocks[4][half:], -1)
    term = blocks[3]
    forward = along_z(jnp.concatenate([added(forward, term[:half]), term[half:]]), 1)
    term = blocks[-3]
    backward = along_z(jnp.concatenate([term[:half], added(backward, term[half:])]), -1)
    return forward, backward


def ring_reduce_near(forward, backward, blocks):
    for ahead in (2, 1):
        forward = along_z(added(forward, blocks[ahead]), 1)
        backward = along_z(added(backward, blocks[-ahead]), -1)
    return forward, backward, blocks[0]


def outer_sync(frag_local, frag_global, outer_mom, owner, fragment):
    replica_count = lax.axis_size("replica")
    is_owner = lax.axis_index("replica") == owner[0]
    gain = outer_lr * (1.0 + outer_momentum)
    mom_gain = outer_lr * outer_momentum * outer_momentum
    local_slot = lax.dynamic_index_in_dim(frag_local[0], fragment[0], 0, keepdims=False)
    state_global, state_mom = frag_global[0], outer_mom[0]
    synced = (gain / replica_count) * local_slot + jnp.where(
        is_owner, (1.0 - gain) * state_global - mom_gain * state_mom, 0.0
    )
    for flip in (1, 2, 4):
        pairs = [(r, r ^ flip) for r in range(replica_count)]
        arrived = lax.ppermute(synced.astype(jnp.bfloat16), "replica", pairs)
        synced = synced + arrived.astype(jnp.float32)
    outer_grad = (state_global - mom_gain * state_mom - synced) / gain
    mom_next = outer_momentum * state_mom + outer_grad
    return synced[None], jnp.where(is_owner, mom_next, state_mom)[None]


def on_device(
    token_ids,
    inputs,
    key_cotangent,
    key_weight,
    adam_m,
    adam_v,
    frag_local,
    frag_global,
    outer_mom,
    owner,
    fragment,
):
    rows_here = inputs.shape[0]
    width = key_weight.shape[1]
    seq_len = rows_here * lax.axis_size("fsdp")
    index = lax.axis_index("fsdp")
    x, z, c = index // (N_Z * N_CORE), (index // N_CORE) % N_Z, index % N_CORE

    bases = jnp.stack(
        [((x ^ flip_x) * N_Z * N_CORE + (c ^ flip_c)) * width for flip_x, flip_c in PEERS] + [z]
    ).astype(jnp.int32)

    cotangents = jnp.concatenate([key_cotangent] + [with_peer(key_cotangent, p) for p in (1, 2, 3)])
    near, far = pack_columns(inputs, bases, width)
    far = [far[0]] + [with_peer(far[p], p) for p in (1, 2, 3)]
    near = [near[0]] + [with_peer(near[p], p) for p in (1, 2, 3)]
    positions = peer_positions(token_ids, x, z, c)
    weights = ring_gather(key_weight[0].astype(jnp.bfloat16))

    grads = unrotate(cotangents, positions.reshape(-1)).reshape(4, rows_here, -1)

    terms = dict(zip(FAR, weight_products(far, grads, len(FAR))))
    forward, backward = ring_reduce_far(terms)
    terms = dict(zip(NEAR, weight_products(near, grads, len(NEAR))))
    forward, backward, own = ring_reduce_near(forward, backward, terms)
    new_weight, new_m, new_v = adam(forward, backward, own, key_weight, adam_m, adam_v, seq_len)

    back = []
    for steps in (NEAR, FAR):
        part = back_products(grads, [weights[ahead] for ahead in steps])
        back.append([part[0]] + [with_peer(part[p], p) for p in (1, 2, 3)])
    input_cotangent = unpack_columns(*back, bases, width)

    synced, new_outer_mom = outer_sync(frag_local, frag_global, outer_mom, owner, fragment)
    return (input_cotangent, new_weight, new_m, new_v, synced, new_outer_mom)


def solution(mesh):
    in_specs = (
        P(("replica", "fsdp")),
        P(("replica", "fsdp"), None),
        P(("replica", "fsdp"), None),
        P("replica", "fsdp", None),
        P("replica", "fsdp", None),
        P("replica", "fsdp", None),
        P("replica", None, "fsdp", None),
        P("replica", "fsdp", None),
        P("replica", "fsdp", None),
        P("fsdp"),
        P("replica"),
    )
    out_specs = (
        P(("replica", "fsdp"), None),
        P("replica", "fsdp", None),
        P("replica", "fsdp", None),
        P("replica", "fsdp", None),
        P("replica", "fsdp", None),
        P("replica", "fsdp", None),
    )
    return jax.shard_map(
        on_device, mesh=mesh, in_specs=in_specs, out_specs=out_specs, check_vma=False
    )
```

time: 275 us -> 148 us (0.54); the launches traced: 271 us -> 147 us
  waiting for transfers between devices: 189 us -> 39.9 us
  starting transfers between devices: 0.13 us -> 57.8 us
  Pallas kernels: 0 us -> 26.6 us
  blocking collectives: 17.3 us -> 0 us
  matrix products: 16.7 us -> 0 us
  between operations: 17.1 us -> 2.51 us
  local copies, waits for them, and re-layouts: 17.3 us -> 8.32 us
    reduce_scatter x1 -> x0, waiting for transfers between devices: 106 us -> none  [on_device(): lax.psum_scatter(lax.dot_general(inputs, key_grad, (((0,), (0,)), ((), ()...]
    psum x1 -> x0, waiting for transfers between devices: 83.1 us -> none  [from_root(): return lax.psum(kept, axis)]
    ppermute x0 -> x40, starting transfers between devices: none -> 57.8 us  [the longest x18 25.8 us: with_peer(): return lax.ppermute(value, 'fsdp', pairs)]
    ppermute x0 -> x40, waiting for transfers between devices: none -> 39.9 us  [the longest x19 24.3 us: along_z(): return lax.ppermute(value, 'fsdp', pairs)]
    pallas_call x0 -> x7, Pallas kernels: none -> 26.6 us  [the longest x2 8.35 us: weight_products(): pl.pallas_call(kernel, out_shape=[jax.ShapeDtypeStruct((rows, depth), jnp...]
    unnamed x1 -> x0, blocking collectives: 17.3 us -> none
    dot_general x2 -> x0, matrix products: 16.7 us -> none  [the longest x1 10.3 us: on_device(): lax.dot_general(key_grad, lax.all_gather(weight_bf, 'fsdp', axis=0, tiled...]
    unnamed x18 -> x37, local copies, waits for them, and re-layouts: 14.9 us -> 3.23 us
  transfers between devices with their start and end apart: 3 -> 40, of which waited for: 2 -> 12; matrix products, arithmetic and copies ran while one was open for 11% -> 11% of each run, Pallas kernels for 0% -> 13%
where the time goes in v1:
time: 148 us; the launch traced here: 147 us
  starting transfers between devices  57.8 us (39%)
  waiting for transfers between devices  39.9 us (27%)
  Pallas kernels  26.6 us (18%)
  other arithmetic  12 us (8%)
  local copies, waits for them, and re-layouts  8.32 us (6%)
  between operations  2.51 us (2%)
    ppermute x18, starting transfers between devices, with_peer(): return lax.ppermute(value, 'fsdp', pairs)  25.8 us
    ppermute x19, starting transfers between devices, along_z(): return lax.ppermute(value, 'fsdp', pairs)  25.1 us
    ppermute x19, waiting for transfers between devices, along_z(): return lax.ppermute(value, 'fsdp', pairs)  24.3 us
    ppermute x18, waiting for transfers between devices, with_peer(): return lax.ppermute(value, 'fsdp', pairs)  13.1 us
    pallas_call x2, Pallas kernels, weight_products(): pl.pallas_call(kernel, out_shape=[jax.ShapeDtypeStruct((rows, depth), jnp...  8.35 us
    pallas_call x2, Pallas kernels, back_products(): pl.pallas_call(kernel, out_shape=[jax.ShapeDtypeStruct((tokens, count * r...  7.01 us
    ppermute x3, starting transfers between devices, outer_sync(): arrived = lax.ppermute(synced.astype(jnp.bfloat16), 'replica', pairs)  6.91 us
    convert_element_type x6, other arithmetic, added(): (arrived.astype(jnp.float32) + term.astype(jnp.float32)).astype(jnp.bfloa...  5.82 us
  transfers between devices with their start and end apart: 40, of which 12 were waited for; matrix products, arithmetic and copies ran while one was open for 11% of the time, Pallas kernels for 13%

profile of v1, /device:TPU:1, one launch (start us, length us, event | category | flops | bytes accessed | tf_op | source)
XLA Modules:
  0.0 147.3 jit_solution(16138192656622661492)
XLA Ops:
  1.7 2.7 %collective-permute-start.2 = (bf16[128,768]{0,1:T(8,128)(2,1)S(1)}, bf16[128,768]{0,1:T(8,128)(2,1)S(1)}, u32[]{:S(2)}, u32[]{:S(2)}) collective-permute-start(bf16[128,768]{0,1:T(8,128)(2,1)S(1)} %copy.25), channel_id=1, source_target_pairs={{0,17},{1,16},{2,19},{3,18},{4,21},{5,20},{6,23},{7,22},{8,25},{9,... | collective-permute-start | bytes 589832 | tf_op jit(solution)/shard_map/ppermute | solution.py:38
  4.4 2.0 %collective-permute-start.1 = (bf16[128,768]{0,1:T(8,128)(2,1)S(1)}, bf16[128,768]{0,1:T(8,128)(2,1)S(1)}, u32[]{:S(2)}, u32[]{:S(2)}) collective-permute-start(bf16[128,768]{0,1:T(8,128)(2,1)S(1)} %copy.25), channel_id=1, source_target_pairs={{0,16},{1,17},{2,18},{3,19},{4,20},{5,21},{6,22},{7,23},{8,24},{9,... | collective-permute-start | bytes 589832 | tf_op jit(solution)/shard_map/ppermute | solution.py:38
  6.8 1.8 %collective-permute-start.3 = (s32[128]{0:T(128)}, s32[128]{0:T(128)S(1)}, u32[]{:S(2)}, u32[]{:S(2)}) collective-permute-start(s32[128]{0:T(128)} %param.11), channel_id=1, source_target_pairs={{0,1},{1,0},{2,3},{3,2},{4,5},{5,4},{6,7},{7,6},{8,9},{9,8},{10,11... | collective-permute-start | bytes 1544 | tf_op jit(solution)/shard_map/ppermute | solution.py:38
  9.3 3.8 %shard_map.157 = (bf16[128,1280]{1,0:T(8,128)(2,1)}, bf16[128,1280]{1,0:T(8,128)(2,1)}, bf16[128,1280]{1,0:T(8,128)(2,1)}, bf16[128,1280]{1,0:T(8,128)(2,1)}, bf...) custom-call(s32[5]{0:T(128)} %stack.60.base_ref, ...), custom_call_target="tpu_custom_call" | custom-call | bytes 4194304 | tf_op jit(solution)/shard_map/pallas_call | solution.py:121
  13.2 1.6 %collective-permute-start = (bf16[128,768]{0,1:T(8,128)(2,1)S(1)}, bf16[128,768]{0,1:T(8,128)(2,1)S(1)}, u32[]{:S(2)}, u32[]{:S(2)}) collective-permute-start(bf16[128,768]{0,1:T(8,128)(2,1)S(1)} %copy.25), channel_id=1, source_target_pairs={{0,1},{1,0},{2,3},{3,2},{4,5},{5,4},{6,7},{7,6},{8,9},{9,8},{10,11... | collective-permute-start | bytes 589832 | tf_op jit(solution)/shard_map/ppermute | solution.py:38
  15.1 1.7 %collective-permute-start.6 = (s32[8,4]{0,1:T(4,128)S(1)}, s32[8,4]{0,1:T(4,128)S(1)}, u32[]{:S(2)}, u32[]{:S(2)}) collective-permute-start(s32[8,4]{0,1:T(4,128)S(1)} %broadcast_select_fusion), channel_id=1, source_target_pairs={{0,2},{1,3},{2,4},{3,5},{4,6},{5,7},{6,8},{7,9},{8,10},{9,11},{10,... | collective-permute-start | bytes 392 | tf_op jit(solution)/shard_map/ppermute | solution.py:32
  16.8 4.9 %collective-permute-done.6 = s32[8,4]{0,1:T(4,128)S(1)} collective-permute-done((s32[8,4]{0,1:T(4,128)S(1)}, s32[8,4]{0,1:T(4,128)S(1)}, u32[]{:S(2)}, u32[]{:S(2)}) %collective-permute-start.6) | collective-permute-done | bytes 160 | tf_op jit(solution)/shard_map/ppermute | solution.py:32
  21.8 4.5 %collective-permute-done.7 = s32[8,4]{0,1:T(4,128)S(1)} collective-permute-done((s32[8,4]{0,1:T(4,128)S(1)}, s32[8,4]{0,1:T(4,128)S(1)}, u32[]{:S(2)}, u32[]{:S(2)}) %collective-permute-start.7) | collective-permute-done | bytes 160 | tf_op jit(solution)/shard_map/ppermute | solution.py:32
  26.4 4.0 %collective-permute-start.8 = (s32[8,4]{0,1:T(4,128)S(1)}, s32[8,4]{0,1:T(4,128)S(1)}, u32[]{:S(2)}, u32[]{:S(2)}) collective-permute-start(s32[8,4]{0,1:T(4,128)S(1)} %fusion.21), channel_id=1, source_target_pairs={{0,8},{1,9},{2,10},{3,11},{4,12},{5,13},{6,14},{7,15},{8,0},{9,1},... | collective-permute-start | bytes 392 | tf_op jit(solution)/shard_map/ppermute | solution.py:32
  30.5 2.2 %collective-permute-done.8 = s32[8,4]{0,1:T(4,128)S(1)} collective-permute-done((s32[8,4]{0,1:T(4,128)S(1)}, s32[8,4]{0,1:T(4,128)S(1)}, u32[]{:S(2)}, u32[]{:S(2)}) %collective-permute-start.8) | collective-permute-done | bytes 160 | tf_op jit(solution)/shard_map/ppermute | solution.py:32
  32.7 1.2 collective-permute-start.24
  34.8 4.0 %collective-permute-start.25 = (bf16[128,768]{1,0:T(8,128)(2,1)}, bf16[128,768]{1,0:T(8,128)(2,1)S(1)}, u32[]{:S(2)}, u32[]{:S(2)}) collective-permute-start(bf16[128,768]{1,0:T(8,128)(2,1)} %get-tuple-element.44), channel_id=1, source_target_pairs={{0,17},{1,16},{2,19},{3,18},{4,21},{5,20},{6,23},{7,22},{8,25},{9,... | collective-permute-start | bytes 589832 | tf_op jit(solution)/shard_map/ppermute | solution.py:38
  39.5 1.3 copy.29.g_ref
  40.8 5.0 %collective-permute-done.25.refs_3_ = bf16[128,768]{1,0:T(8,128)(2,1)S(1)} collective-permute-done((bf16[128,768]{1,0:T(8,128)(2,1)}, bf16[128,768]{1,0:T(8,128)(2,1)S(1)}, u32[]{:S(2)}, u32[]{:S(2)}) %collective-permute-start.25) | collective-permute-done | bytes 196640 | tf_op jit(solution)/shard_map/ppermute | solution.py:38
  46.5 3.7 %shard_map.158 = (bf16[256,768]{1,0:T(8,128)(2,1)}, bf16[256,768]{1,0:T(8,128)(2,1)}, bf16[256,768]{1,0:T(8,128)(2,1)}) custom-call(bf16[4,128,768]{2,1,0:T(8,128)(2,1)} %copy.29.g_ref, bf16[128,768]{1,0:T(8,128)(2,1)} %get-tuple-element.41.refs_0_, bf16[128,768]{1,0:T(8,128)(2,1)} %copy-done.15, bf16[128,768]{1,0:T(8,128)(2,1)} %copy-done.16, ...), custom_call_target="tpu_custom_call" | custom-call | flops 603979776 | bytes 2752512 | tf_op jit(solution)/shard_map/pallas_call | solution.py:210
  50.2 1.1 fusion.20
  51.5 2.7 %collective-permute-start.9 = (bf16[256,768]{1,0:T(8,128)(2,1)S(1)}, bf16[256,768]{1,0:T(8,128)(2,1)}, u32[]{:S(2)}, u32[]{:S(2)}) collective-permute-start(bf16[256,768]{1,0:T(8,128)(2,1)S(1)} %convert_bitcast_fusion.refs_0_), channel_id=1, source_target_pairs={{0,14},{1,15},{2,0},{3,1},{4,2},{5,3},{6,4},{7,5},{8,6},{9,7},{10,... | collective-permute-start | bytes 1179656 | tf_op jit(solution)/shard_map/ppermute | solution.py:32
  56.8 1.9 %collective-permute-done.26 = bf16[128,768]{1,0:T(8,128)(2,1)S(1)} collective-permute-done((bf16[128,768]{1,0:T(8,128)(2,1)S(1)}, bf16[128,768]{1,0:T(8,128)(2,1)S(1)}, u32[]{:S(2)}, u32[]{:S(2)}) %collective-permute-start.26) | collective-permute-done | bytes 196640 | tf_op jit(solution)/shard_map/ppermute | solution.py:32
  59.9 6.4 %collective-permute-done.33 = bf16[128,768]{1,0:T(8,128)(2,1)S(1)} collective-permute-done((bf16[128,768]{1,0:T(8,128)(2,1)S(1)}, bf16[128,768]{1,0:T(8,128)(2,1)S(1)}, u32[]{:S(2)}, u32[]{:S(2)}) %collective-permute-start.33) | collective-permute-done | bytes 196640 | tf_op jit(solution)/shard_map/ppermute | solution.py:32
  66.2 2.5 %collective-permute-start.30 = (bf16[128,1280]{1,0:T(8,128)(2,1)}, bf16[128,1280]{1,0:T(8,128)(2,1)S(1)}, u32[]{:S(2)}, u32[]{:S(2)}) collective-permute-start(bf16[128,1280]{1,0:T(8,128)(2,1)} %get-tuple-element.50), channel_id=1, source_target_pairs={{0,17},{1,16},{2,19},{3,18},{4,21},{5,20},{6,23},{7,22},{8,25},{9,... | collective-permute-start | bytes 983048 | tf_op jit(solution)/shard_map/ppermute | solution.py:38
  69.2 3.3 %collective-permute-start.34 = (bf16[256,768]{1,0:T(8,128)(2,1)S(1)}, bf16[256,768]{1,0:T(8,128)(2,1)S(1)}, u32[]{:S(2)}, u32[]{:S(2)}) collective-permute-start(bf16[256,768]{1,0:T(8,128)(2,1)S(1)} %pad_maximum_fusion.3), channel_id=1, source_target_pairs={{0,14},{1,15},{2,0},{3,1},{4,2},{5,3},{6,4},{7,5},{8,6},{9,7},{10,... | collective-permute-start | bytes 1179656 | tf_op jit(solution)/shard_map/ppermute | solution.py:32
  72.5 1.4 collective-permute-start.11
  73.9 2.0 %fusion.16 = (bf16[256,512]{1,0:T(8,128)(2,1)}, f32[256,512]{1,0:T(8,128)S(1)}) fusion(f32[1,256,512]{2,1,0:T(8,128)S(1)} %copy-done.1, f32[1,256,512]{2,1,0:T(8,128)S(1)} %copy-done.2, pred[]{:T(512)S(6)} %eq.30, f32[1,3,256,512]{3,2,1,0:T(8,128)} %param.17, s32[]{:T(128)S(6)} %select_n.64), kind=kLoop, calls=%fused_computation.54 | loop fusion | flops 917504 | bytes 2359301 | tf_op jit(solution)/shard_map/convert_element_type | solution.py:302
  75.9 1.7 %collective-permute-done.30.refs_3_ = bf16[128,1280]{1,0:T(8,128)(2,1)S(1)} collective-permute-done((bf16[128,1280]{1,0:T(8,128)(2,1)}, bf16[128,1280]{1,0:T(8,128)(2,1)S(1)}, u32[]{:S(2)}, u32[]{:S(2)}) %collective-permute-start.30) | collective-permute-done | bytes 327712 | tf_op jit(solution)/shard_map/ppermute | solution.py:38
  78.3 2.3 %collective-permute-start.37 = (bf16[256,512]{1,0:T(8,128)(2,1)}, bf16[256,512]{1,0:T(8,128)(2,1)S(1)}, u32[]{:S(2)}, u32[]{:S(2)}) collective-permute-start(bf16[256,512]{1,0:T(8,128)(2,1)} %get-tuple-element.60), channel_id=1, source_target_pairs={{0,32},{32,0},{64,96},{96,64},{128,160},{160,128},{192,224},{224,1... | collective-permute-start | bytes 786440 | tf_op jit(solution)/shard_map/ppermute | solution.py:302
  80.6 4.6 %shard_map.159 = (bf16[256,768]{1,0:T(8,128)(2,1)}, bf16[256,768]{1,0:T(8,128)(2,1)}, bf16[256,768]{1,0:T(8,128)(2,1)}, bf16[256,768]{1,0:T(8,128)(2,1)}, bf16[256,768]{1,0:T(8,128)(2,1)}) custom-call(bf16[4,128,768]{2,1,0:T(8,128)(2,1)} %copy.29.g_ref, bf16[128,1280]{1,0:T(8,128)(2,1)} %get-tuple-element.47.refs_0_, ...), custom_call_target="tpu_custom_call" | custom-call | flops 1006632960 | bytes 4063232 | tf_op jit(solution)/shard_map/pallas_call | solution.py:210
  85.2 2.0 %add_convert_fusion.3 = bf16[256,768]{1,0:T(8,128)(2,1)} fusion(bf16[256,768]{1,0:T(8,128)(2,1)} %get-tuple-element.51, bf16[256,768]{1,0:T(8,128)(2,1)} %collective-permute-done.27), kind=kLoop, calls=%fused_computation.5 | loop fusion | flops 786432 | bytes 1179648 | tf_op jit(solution)/shard_map/convert_element_type | solution.py:269
  87.4 2.4 %collective-permute-done.11.refs_3_ = bf16[256,768]{1,0:T(8,128)(2,1)} collective-permute-done((bf16[256,768]{1,0:T(8,128)(2,1)}, bf16[256,768]{1,0:T(8,128)(2,1)}, u32[]{:S(2)}, u32[]{:S(2)}) %collective-permute-start.11) | collective-permute-done | bytes 393248 | tf_op jit(solution)/shard_map/ppermute | solution.py:32
  89.8 3.2 %collective-permute-start.16 = (bf16[256,768]{1,0:T(8,128)(2,1)}, bf16[256,768]{1,0:T(8,128)(2,1)}, u32[]{:S(2)}, u32[]{:S(2)}) collective-permute-start(bf16[256,768]{1,0:T(8,128)(2,1)} %collective-permute-done.11.refs_3_), channel_id=1, source_target_pairs={{0,14},{1,15},{2,0},{3,1},{4,2},{5,3},{6,4},{7,5},{8,6},{9,7},{10,... | collective-permute-start | bytes 1179656 | tf_op jit(solution)/shard_map/ppermute | solution.py:32
  93.0 1.8 %add_convert_fusion.1 = bf16[256,768]{1,0:T(8,128)(2,1)} fusion(bf16[256,768]{1,0:T(8,128)(2,1)} %get-tuple-element.54, bf16[256,768]{1,0:T(8,128)(2,1)S(1)} %collective-permute-done.34), kind=kLoop, calls=%fused_computation.3 | loop fusion | flops 786432 | bytes 1179648 | tf_op jit(solution)/shard_map/convert_element_type | solution.py:269
  94.9 2.7 %collective-permute-start.35 = (bf16[256,768]{1,0:T(8,128)(2,1)}, bf16[256,768]{1,0:T(8,128)(2,1)}, u32[]{:S(2)}, u32[]{:S(2)}) collective-permute-start(bf16[256,768]{1,0:T(8,128)(2,1)} %add_convert_fusion.1), channel_id=1, source_target_pairs={{0,14},{1,15},{2,0},{3,1},{4,2},{5,3},{6,4},{7,5},{8,6},{9,7},{10,... | collective-permute-start | bytes 1179656 | tf_op jit(solution)/shard_map/ppermute | solution.py:32
  97.6 1.6 %collective-permute-start.38 = (bf16[256,512]{1,0:T(8,128)(2,1)S(1)}, bf16[256,512]{1,0:T(8,128)(2,1)S(1)}, u32[]{:S(2)}, u32[]{:S(2)}) collective-permute-start(bf16[256,512]{1,0:T(8,128)(2,1)S(1)} %fusion.7), channel_id=1, source_target_pairs={{0,64},{32,96},{64,0},{96,32},{128,192},{160,224},{192,128},{224,1... | collective-permute-start | bytes 786440 | tf_op jit(solution)/shard_map/ppermute | solution.py:302
  99.2 3.9 %shard_map.154 = (bf16[128,1280]{1,0:T(8,128)(2,1)}, bf16[128,1280]{1,0:T(8,128)(2,1)}, bf16[128,1280]{1,0:T(8,128)(2,1)}, bf16[128,1280]{1,0:T(8,128)(2,1)}) custom-call(bf16[4,128,768]{2,1,0:T(8,128)(2,1)} %copy.29.g_ref, bf16[256,768]{1,0:T(8,128)(2,1)} %copy-done.7, bf16[256,768]{1,0:T(8,128)(2,1)} %collective-permute-done.9.refs_1_, ...), custom_call_target="tpu_custom_call" | custom-call | flops 1006632960 | bytes 4063232 | tf_op jit(solution)/shard_map/pallas_call | solution.py:179
  103.2 1.9 %collective-permute-start.13 = (bf16[128,1280]{1,0:T(8,128)(2,1)}, bf16[128,1280]{1,0:T(8,128)(2,1)}, u32[]{:S(2)}, u32[]{:S(2)}) collective-permute-start(bf16[128,1280]{1,0:T(8,128)(2,1)} %get-tuple-element.34), channel_id=1, source_target_pairs={{0,1},{1,0},{2,3},{3,2},{4,5},{5,4},{6,7},{7,6},{8,9},{9,8},{10,11... | collective-permute-start | bytes 983048 | tf_op jit(solution)/shard_map/ppermute | solution.py:38
  106.0 2.0 %collective-permute-done.17.refs_1_ = bf16[256,768]{1,0:T(8,128)(2,1)} collective-permute-done((bf16[256,768]{1,0:T(8,128)(2,1)}, bf16[256,768]{1,0:T(8,128)(2,1)}, u32[]{:S(2)}, u32[]{:S(2)}) %collective-permute-start.17) | collective-permute-done | bytes 393248 | tf_op jit(solution)/shard_map/ppermute | solution.py:32
  108.0 1.1 collective-permute-start.19
  111.5 1.8 %add_convert_fusion = bf16[256,768]{1,0:T(8,128)(2,1)} fusion(bf16[256,768]{1,0:T(8,128)(2,1)S(1)} %copy-done.8, bf16[256,768]{1,0:T(8,128)(2,1)} %collective-permute-done.35), kind=kLoop, calls=%fused_computation.2 | loop fusion | flops 786432 | bytes 1179648 | tf_op jit(solution)/shard_map/convert_element_type | solution.py:269
  113.3 1.9 %collective-permute-start.36 = (bf16[256,768]{1,0:T(8,128)(2,1)}, bf16[256,768]{1,0:T(8,128)(2,1)S(1)}, u32[]{:S(2)}, u32[]{:S(2)}) collective-permute-start(bf16[256,768]{1,0:T(8,128)(2,1)} %add_convert_fusion), channel_id=1, source_target_pairs={{0,14},{1,15},{2,0},{3,1},{4,2},{5,3},{6,4},{7,5},{8,6},{9,7},{10,... | collective-permute-start | bytes 1179656 | tf_op jit(solution)/shard_map/ppermute | solution.py:32
  115.3 3.0 %collective-permute-start.39 = (bf16[256,512]{1,0:T(8,128)(2,1)S(1)}, bf16[256,512]{1,0:T(8,128)(2,1)S(1)}, u32[]{:S(2)}, u32[]{:S(2)}) collective-permute-start(bf16[256,512]{1,0:T(8,128)(2,1)S(1)} %fusion.15), channel_id=1, source_target_pairs={{0,128},{32,160},{64,192},{96,224},{128,0},{160,32},{192,64},{224,... | collective-permute-start | bytes 786440 | tf_op jit(solution)/shard_map/ppermute | solution.py:302
  119.6 2.6 %collective-permute-done.39 = bf16[256,512]{1,0:T(8,128)(2,1)S(1)} collective-permute-done((bf16[256,512]{1,0:T(8,128)(2,1)S(1)}, bf16[256,512]{1,0:T(8,128)(2,1)S(1)}, u32[]{:S(2)}, u32[]{:S(2)}) %collective-permute-start.39) | collective-permute-done | bytes 262176 | tf_op jit(solution)/shard_map/ppermute | solution.py:302
  122.2 4.0 %collective-permute-start.15 = (bf16[128,1280]{1,0:T(8,128)(2,1)}, bf16[128,1280]{1,0:T(8,128)(2,1)}, u32[]{:S(2)}, u32[]{:S(2)}) collective-permute-start(bf16[128,1280]{1,0:T(8,128)(2,1)} %get-tuple-element.36), channel_id=1, source_target_pairs={{0,17},{1,16},{2,19},{3,18},{4,21},{5,20},{6,23},{7,22},{8,25},{9,... | collective-permute-start | bytes 983048 | tf_op jit(solution)/shard_map/ppermute | solution.py:38
  126.1 3.1 %shard_map.155 = (bf16[128,768]{1,0:T(8,128)(2,1)}, bf16[128,768]{1,0:T(8,128)(2,1)}, bf16[128,768]{1,0:T(8,128)(2,1)}, bf16[128,768]{1,0:T(8,128)(2,1)}) custom-call(bf16[4,128,768]{2,1,0:T(8,128)(2,1)} %copy.29.g_ref, bf16[256,768]{1,0:T(8,128)(2,1)} %collective-permute-done.16.refs_0_, bf16[256,768]{1,0:T(8,128)(2,1)} %collective-permute-done.17.refs_1_, ...), custom_call_target="tpu_custom_call" | custom-call | flops 603979776 | bytes 2752512 | tf_op jit(solution)/shard_map/pallas_call | solution.py:179
  129.2 1.1 collective-permute-start.21
  131.4 1.2 fusion.1
  132.6 4.3 %shard_map.160 = (f32[1,256,768]{2,1,0:T(8,128)}, f32[1,256,768]{2,1,0:T(8,128)}, f32[1,256,768]{2,1,0:T(8,128)}) custom-call(bf16[256,768]{1,0:T(8,128)(2,1)} %copy-done.3, bf16[256,768]{1,0:T(8,128)(2,1)} %copy-done.4, bf16[256,768]{1,0:T(8,128)(2,1)} %get-tuple-element.56.o_ref, f32[1,256,768]{2,1,0:T(8,128)} %w_ref.1, f32[1,256,768]{2,1,0:T(8,128)} %m_ref.1, ...), custom_call_target="tpu_custom_call" | custom-call | flops 3932160 | bytes 5898240 | tf_op jit(solution)/shard_map/pallas_call | solution.py:247
  137.0 2.6 %collective-permute-done.21.refs_6_ = bf16[128,768]{1,0:T(8,128)(2,1)S(1)} collective-permute-done((bf16[128,768]{1,0:T(8,128)(2,1)}, bf16[128,768]{1,0:T(8,128)(2,1)S(1)}, u32[]{:S(2)}, u32[]{:S(2)}) %collective-permute-start.21) | collective-permute-done | bytes 196640 | tf_op jit(solution)/shard_map/ppermute | solution.py:38
  139.6 3.7 %collective-permute-done.22.refs_7_ = bf16[128,768]{1,0:T(8,128)(2,1)S(1)} collective-permute-done((bf16[128,768]{1,0:T(8,128)(2,1)}, bf16[128,768]{1,0:T(8,128)(2,1)S(1)}, u32[]{:S(2)}, u32[]{:S(2)}) %collective-permute-start.22) | collective-permute-done | bytes 196640 | tf_op jit(solution)/shard_map/ppermute | solution.py:38
  144.0 3.1 %shard_map.156 = bf16[128,8192]{1,0:T(8,128)(2,1)} custom-call(s32[5]{0:T(128)} %stack.60.base_ref, bf16[128,1280]{1,0:T(8,128)(2,1)} %get-tuple-element.33.refs_0_, bf16[128,1280]{1,0:T(8,128)(2,1)} %collective-permute-done.13.refs_1_, bf16[128,1280]{1,0:T(8,128)(2,1)} %collective-permute-done.14.refs_2_, ...), custom_call_target="tpu_custom_call" | custom-call | bytes 4194304 | tf_op jit(solution)/shard_map/pallas_call | solution.py:154
  (117 shorter events, 15.3 us)
Async XLA Ops:
  0.6 14.2 %copy-start.12 = (s32[128]{0:T(128)S(1)}, s32[128]{0:T(128)}, u32[]{:S(2)}) copy-start(s32[128]{0:T(128)} %param.11) | copy-start | bytes 1540
  1.7 33.1 %collective-permute-start.2 = (bf16[128,768]{0,1:T(8,128)(2,1)S(1)}, bf16[128,768]{0,1:T(8,128)(2,1)S(1)}, u32[]{:S(2)}, u32[]{:S(2)}) collective-permute-start(bf16[128,768]{0,1:T(8,128)(2,1)S(1)} %copy.25), channel_id=1, source_target_pairs={{0,17},{1,16},{2,19},{3,18},{4,21},{5,20},{6,23},{7,22},{8,25},{9,... | collective-permute-start | bytes 589832 | tf_op jit(solution)/shard_map/ppermute | solution.py:38
  4.4 34.4 %collective-permute-start.1 = (bf16[128,768]{0,1:T(8,128)(2,1)S(1)}, bf16[128,768]{0,1:T(8,128)(2,1)S(1)}, u32[]{:S(2)}, u32[]{:S(2)}) collective-permute-start(bf16[128,768]{0,1:T(8,128)(2,1)S(1)} %copy.25), channel_id=1, source_target_pairs={{0,16},{1,17},{2,18},{3,19},{4,20},{5,21},{6,22},{7,23},{8,24},{9,... | collective-permute-start | bytes 589832 | tf_op jit(solution)/shard_map/ppermute | solution.py:38
  6.4 6.7 %collective-permute-start.5 = (s32[128]{0:T(128)}, s32[128]{0:T(128)S(1)}, u32[]{:S(2)}, u32[]{:S(2)}) collective-permute-start(s32[128]{0:T(128)} %param.11), channel_id=1, source_target_pairs={{0,17},{1,16},{2,19},{3,18},{4,21},{5,20},{6,23},{7,22},{8,25},{9,... | collective-permute-start | bytes 1544 | tf_op jit(solution)/shard_map/ppermute | solution.py:38
  6.8 8.0 %collective-permute-start.4 = (s32[128]{0:T(128)}, s32[128]{0:T(128)S(1)}, u32[]{:S(2)}, u32[]{:S(2)}) collective-permute-start(s32[128]{0:T(128)} %param.11), channel_id=1, source_target_pairs={{0,16},{1,17},{2,18},{3,19},{4,20},{5,21},{6,22},{7,23},{8,24},{9,... | collective-permute-start | bytes 1544 | tf_op jit(solution)/shard_map/ppermute | solution.py:38
  6.8 8.0 %collective-permute-start.3 = (s32[128]{0:T(128)}, s32[128]{0:T(128)S(1)}, u32[]{:S(2)}, u32[]{:S(2)}) collective-permute-start(s32[128]{0:T(128)} %param.11), channel_id=1, source_target_pairs={{0,1},{1,0},{2,3},{3,2},{4,5},{5,4},{6,7},{7,6},{8,9},{9,8},{10,11... | collective-permute-start | bytes 1544 | tf_op jit(solution)/shard_map/ppermute | solution.py:38
  13.2 25.7 %collective-permute-start = (bf16[128,768]{0,1:T(8,128)(2,1)S(1)}, bf16[128,768]{0,1:T(8,128)(2,1)S(1)}, u32[]{:S(2)}, u32[]{:S(2)}) collective-permute-start(bf16[128,768]{0,1:T(8,128)(2,1)S(1)} %copy.25), channel_id=1, source_target_pairs={{0,1},{1,0},{2,3},{3,2},{4,5},{5,4},{6,7},{7,6},{8,9},{9,8},{10,11... | collective-permute-start | bytes 589832 | tf_op jit(solution)/shard_map/ppermute | solution.py:38
  14.8 26.0 %collective-permute-start.23 = (bf16[128,768]{1,0:T(8,128)(2,1)}, bf16[128,768]{1,0:T(8,128)(2,1)S(1)}, u32[]{:S(2)}, u32[]{:S(2)}) collective-permute-start(bf16[128,768]{1,0:T(8,128)(2,1)} %get-tuple-element.42), channel_id=1, source_target_pairs={{0,1},{1,0},{2,3},{3,2},{4,5},{5,4},{6,7},{7,6},{8,9},{9,8},{10,11... | collective-permute-start | bytes 589832 | tf_op jit(solution)/shard_map/ppermute | solution.py:38
  15.1 6.6 %collective-permute-start.6 = (s32[8,4]{0,1:T(4,128)S(1)}, s32[8,4]{0,1:T(4,128)S(1)}, u32[]{:S(2)}, u32[]{:S(2)}) collective-permute-start(s32[8,4]{0,1:T(4,128)S(1)} %broadcast_select_fusion), channel_id=1, source_target_pairs={{0,2},{1,3},{2,4},{3,5},{4,6},{5,7},{6,8},{7,9},{8,10},{9,11},{10,... | collective-permute-start | bytes 392 | tf_op jit(solution)/shard_map/ppermute | solution.py:32
  21.8 4.5 %collective-permute-start.7 = (s32[8,4]{0,1:T(4,128)S(1)}, s32[8,4]{0,1:T(4,128)S(1)}, u32[]{:S(2)}, u32[]{:S(2)}) collective-permute-start(s32[8,4]{0,1:T(4,128)S(1)} %fusion.14), channel_id=1, source_target_pairs={{0,4},{1,5},{2,6},{3,7},{4,8},{5,9},{6,10},{7,11},{8,12},{9,13},{1... | collective-permute-start | bytes 392 | tf_op jit(solution)/shard_map/ppermute | solution.py:32
  26.4 6.4 %collective-permute-start.8 = (s32[8,4]{0,1:T(4,128)S(1)}, s32[8,4]{0,1:T(4,128)S(1)}, u32[]{:S(2)}, u32[]{:S(2)}) collective-permute-start(s32[8,4]{0,1:T(4,128)S(1)} %fusion.21), channel_id=1, source_target_pairs={{0,8},{1,9},{2,10},{3,11},{4,12},{5,13},{6,14},{7,15},{8,0},{9,1},... | collective-permute-start | bytes 392 | tf_op jit(solution)/shard_map/ppermute | solution.py:32
  32.7 8.1 %collective-permute-start.24 = (bf16[128,768]{1,0:T(8,128)(2,1)}, bf16[128,768]{1,0:T(8,128)(2,1)S(1)}, u32[]{:S(2)}, u32[]{:S(2)}) collective-permute-start(bf16[128,768]{1,0:T(8,128)(2,1)} %get-tuple-element.43), channel_id=1, source_target_pairs={{0,16},{1,17},{2,18},{3,19},{4,20},{5,21},{6,22},{7,23},{8,24},{9,... | collective-permute-start | bytes 589832 | tf_op jit(solution)/shard_map/ppermute | solution.py:38
  34.8 11.0 %collective-permute-start.25 = (bf16[128,768]{1,0:T(8,128)(2,1)}, bf16[128,768]{1,0:T(8,128)(2,1)S(1)}, u32[]{:S(2)}, u32[]{:S(2)}) collective-permute-start(bf16[128,768]{1,0:T(8,128)(2,1)} %get-tuple-element.44), channel_id=1, source_target_pairs={{0,17},{1,16},{2,19},{3,18},{4,21},{5,20},{6,23},{7,22},{8,25},{9,... | collective-permute-start | bytes 589832 | tf_op jit(solution)/shard_map/ppermute | solution.py:38
  40.8 10.7 %copy-start = (f32[1,256,768]{2,1,0:T(8,128)S(1)}, f32[1,256,768]{2,1,0:T(8,128)}, u32[]{:S(2)}) copy-start(f32[1,256,768]{2,1,0:T(8,128)} %w_ref.1) | copy-start | bytes 2359300
  46.5 8.7 %copy-start.13 = (bf16[128,1280]{1,0:T(8,128)(2,1)S(1)}, bf16[128,1280]{1,0:T(8,128)(2,1)}, u32[]{:S(2)}) copy-start(bf16[128,1280]{1,0:T(8,128)(2,1)} %get-tuple-element.49) | copy-start | bytes 983044
  51.3 7.4 %collective-permute-start.26 = (bf16[128,768]{1,0:T(8,128)(2,1)S(1)}, bf16[128,768]{1,0:T(8,128)(2,1)S(1)}, u32[]{:S(2)}, u32[]{:S(2)}) collective-permute-start(bf16[128,768]{1,0:T(8,128)(2,1)S(1)} %get-tuple-element.71), channel_id=1, source_target_pairs={{0,2},{1,3},{2,4},{3,5},{4,6},{5,7},{6,8},{7,9},{8,10},{9,11},{10,... | collective-permute-start | bytes 589832 | tf_op jit(solution)/shard_map/ppermute | solution.py:32
  51.5 17.7 %copy-start.7 = (bf16[256,768]{1,0:T(8,128)(2,1)}, bf16[256,768]{1,0:T(8,128)(2,1)S(1)}, u32[]{:S(2)}) copy-start(bf16[256,768]{1,0:T(8,128)(2,1)S(1)} %convert_bitcast_fusion.refs_0_) | copy-start | bytes 1179652
  51.5 20.9 %collective-permute-start.9 = (bf16[256,768]{1,0:T(8,128)(2,1)S(1)}, bf16[256,768]{1,0:T(8,128)(2,1)}, u32[]{:S(2)}, u32[]{:S(2)}) collective-permute-start(bf16[256,768]{1,0:T(8,128)(2,1)S(1)} %convert_bitcast_fusion.refs_0_), channel_id=1, source_target_pairs={{0,14},{1,15},{2,0},{3,1},{4,2},{5,3},{6,4},{7,5},{8,6},{9,7},{10,... | collective-permute-start | bytes 1179656 | tf_op jit(solution)/shard_map/ppermute | solution.py:32
  54.2 19.7 %collective-permute-start.10 = (bf16[256,768]{1,0:T(8,128)(2,1)S(1)}, bf16[256,768]{1,0:T(8,128)(2,1)}, u32[]{:S(2)}, u32[]{:S(2)}) collective-permute-start(bf16[256,768]{1,0:T(8,128)(2,1)S(1)} %convert_bitcast_fusion.refs_0_), channel_id=1, source_target_pairs={{0,2},{1,3},{2,4},{3,5},{4,6},{5,7},{6,8},{7,9},{8,10},{9,11},{10,... | collective-permute-start | bytes 1179656 | tf_op jit(solution)/shard_map/ppermute | solution.py:32
  54.2 14.6 %collective-permute-start.28 = (bf16[128,1280]{1,0:T(8,128)(2,1)}, bf16[128,1280]{1,0:T(8,128)(2,1)}, u32[]{:S(2)}, u32[]{:S(2)}) collective-permute-start(bf16[128,1280]{1,0:T(8,128)(2,1)} %get-tuple-element.48), channel_id=1, source_target_pairs={{0,1},{1,0},{2,3},{3,2},{4,5},{5,4},{6,7},{7,6},{8,9},{9,8},{10,11... | collective-permute-start | bytes 983048 | tf_op jit(solution)/shard_map/ppermute | solution.py:38
  55.2 14.0 %collective-permute-start.29 = (bf16[128,1280]{1,0:T(8,128)(2,1)S(1)}, bf16[128,1280]{1,0:T(8,128)(2,1)}, u32[]{:S(2)}, u32[]{:S(2)}) collective-permute-start(bf16[128,1280]{1,0:T(8,128)(2,1)S(1)} %copy-done.13), channel_id=1, source_target_pairs={{0,16},{1,17},{2,18},{3,19},{4,20},{5,21},{6,22},{7,23},{8,24},{9,... | collective-permute-start | bytes 983048 | tf_op jit(solution)/shard_map/ppermute | solution.py:38
  56.8 17.2 %copy-start.1 = (f32[1,256,512]{2,1,0:T(8,128)S(1)}, f32[1,256,512]{2,1,0:T(8,128)}, u32[]{:S(2)}) copy-start(f32[1,256,512]{2,1,0:T(8,128)} %param.19) | copy-start | bytes 1572868
  56.8 17.1 %copy-start.2 = (f32[1,256,512]{2,1,0:T(8,128)S(1)}, f32[1,256,512]{2,1,0:T(8,128)}, u32[]{:S(2)}) copy-start(f32[1,256,512]{2,1,0:T(8,128)} %param.18) | copy-start | bytes 1572868
  58.7 7.5 %collective-permute-start.33 = (bf16[128,768]{1,0:T(8,128)(2,1)S(1)}, bf16[128,768]{1,0:T(8,128)(2,1)S(1)}, u32[]{:S(2)}, u32[]{:S(2)}) collective-permute-start(bf16[128,768]{1,0:T(8,128)(2,1)S(1)} %get-tuple-element.70), channel_id=1, source_target_pairs={{0,14},{1,15},{2,0},{3,1},{4,2},{5,3},{6,4},{7,5},{8,6},{9,7},{10,... | collective-permute-start | bytes 589832 | tf_op jit(solution)/shard_map/ppermute | solution.py:32
  66.2 11.3 %collective-permute-start.30 = (bf16[128,1280]{1,0:T(8,128)(2,1)}, bf16[128,1280]{1,0:T(8,128)(2,1)S(1)}, u32[]{:S(2)}, u32[]{:S(2)}) collective-permute-start(bf16[128,1280]{1,0:T(8,128)(2,1)} %get-tuple-element.50), channel_id=1, source_target_pairs={{0,17},{1,16},{2,19},{3,18},{4,21},{5,20},{6,23},{7,22},{8,25},{9,... | collective-permute-start | bytes 983048 | tf_op jit(solution)/shard_map/ppermute | solution.py:38
  68.8 16.4 %collective-permute-start.27 = (bf16[256,768]{1,0:T(8,128)(2,1)S(1)}, bf16[256,768]{1,0:T(8,128)(2,1)}, u32[]{:S(2)}, u32[]{:S(2)}) collective-permute-start(bf16[256,768]{1,0:T(8,128)(2,1)S(1)} %pad_maximum_fusion.2), channel_id=1, source_target_pairs={{0,2},{1,3},{2,4},{3,5},{4,6},{5,7},{6,8},{7,9},{8,10},{9,11},{10,... | collective-permute-start | bytes 1179656 | tf_op jit(solution)/shard_map/ppermute | solution.py:32
  69.2 23.8 %collective-permute-start.34 = (bf16[256,768]{1,0:T(8,128)(2,1)S(1)}, bf16[256,768]{1,0:T(8,128)(2,1)S(1)}, u32[]{:S(2)}, u32[]{:S(2)}) collective-permute-start(bf16[256,768]{1,0:T(8,128)(2,1)S(1)} %pad_maximum_fusion.3), channel_id=1, source_target_pairs={{0,14},{1,15},{2,0},{3,1},{4,2},{5,3},{6,4},{7,5},{8,6},{9,7},{10,... | collective-permute-start | bytes 1179656 | tf_op jit(solution)/shard_map/ppermute | solution.py:32
  72.5 17.3 %collective-permute-start.11 = (bf16[256,768]{1,0:T(8,128)(2,1)}, bf16[256,768]{1,0:T(8,128)(2,1)}, u32[]{:S(2)}, u32[]{:S(2)}) collective-permute-start(bf16[256,768]{1,0:T(8,128)(2,1)} %collective-permute-done.9.refs_1_), channel_id=1, source_target_pairs={{0,14},{1,15},{2,0},{3,1},{4,2},{5,3},{6,4},{7,5},{8,6},{9,7},{10,... | collective-permute-start | bytes 1179656 | tf_op jit(solution)/shard_map/ppermute | solution.py:32
  73.9 19.1 %collective-permute-start.12 = (bf16[256,768]{1,0:T(8,128)(2,1)}, bf16[256,768]{1,0:T(8,128)(2,1)}, u32[]{:S(2)}, u32[]{:S(2)}) collective-permute-start(bf16[256,768]{1,0:T(8,128)(2,1)} %collective-permute-done.10.refs_2_), channel_id=1, source_target_pairs={{0,2},{1,3},{2,4},{3,5},{4,6},{5,7},{6,8},{7,9},{8,10},{9,11},{10,... | collective-permute-start | bytes 1179656 | tf_op jit(solution)/shard_map/ppermute | solution.py:32
  78.3 19.3 %collective-permute-start.37 = (bf16[256,512]{1,0:T(8,128)(2,1)}, bf16[256,512]{1,0:T(8,128)(2,1)S(1)}, u32[]{:S(2)}, u32[]{:S(2)}) collective-permute-start(bf16[256,512]{1,0:T(8,128)(2,1)} %get-tuple-element.60), channel_id=1, source_target_pairs={{0,32},{32,0},{64,96},{96,64},{128,160},{160,128},{192,224},{224,1... | collective-permute-start | bytes 786440 | tf_op jit(solution)/shard_map/ppermute | solution.py:302
  87.2 22.9 %collective-permute-start.31 = (bf16[256,768]{1,0:T(8,128)(2,1)}, bf16[256,768]{1,0:T(8,128)(2,1)S(1)}, u32[]{:S(2)}, u32[]{:S(2)}) collective-permute-start(bf16[256,768]{1,0:T(8,128)(2,1)} %add_convert_fusion.3), channel_id=1, source_target_pairs={{0,2},{1,3},{2,4},{3,5},{4,6},{5,7},{6,8},{7,9},{8,10},{9,11},{10,... | collective-permute-start | bytes 1179656 | tf_op jit(solution)/shard_map/ppermute | solution.py:32
  89.8 13.4 %collective-permute-start.16 = (bf16[256,768]{1,0:T(8,128)(2,1)}, bf16[256,768]{1,0:T(8,128)(2,1)}, u32[]{:S(2)}, u32[]{:S(2)}) collective-permute-start(bf16[256,768]{1,0:T(8,128)(2,1)} %collective-permute-done.11.refs_3_), channel_id=1, source_target_pairs={{0,14},{1,15},{2,0},{3,1},{4,2},{5,3},{6,4},{7,5},{8,6},{9,7},{10,... | collective-permute-start | bytes 1179656 | tf_op jit(solution)/shard_map/ppermute | solution.py:32
  93.0 15.0 %collective-permute-start.17 = (bf16[256,768]{1,0:T(8,128)(2,1)}, bf16[256,768]{1,0:T(8,128)(2,1)}, u32[]{:S(2)}, u32[]{:S(2)}) collective-permute-start(bf16[256,768]{1,0:T(8,128)(2,1)} %collective-permute-done.12.refs_4_), channel_id=1, source_target_pairs={{0,2},{1,3},{2,4},{3,5},{4,6},{5,7},{6,8},{7,9},{8,10},{9,11},{10,... | collective-permute-start | bytes 1179656 | tf_op jit(solution)/shard_map/ppermute | solution.py:32
  94.9 15.7 %collective-permute-start.35 = (bf16[256,768]{1,0:T(8,128)(2,1)}, bf16[256,768]{1,0:T(8,128)(2,1)}, u32[]{:S(2)}, u32[]{:S(2)}) collective-permute-start(bf16[256,768]{1,0:T(8,128)(2,1)} %add_convert_fusion.1), channel_id=1, source_target_pairs={{0,14},{1,15},{2,0},{3,1},{4,2},{5,3},{6,4},{7,5},{8,6},{9,7},{10,... | collective-permute-start | bytes 1179656 | tf_op jit(solution)/shard_map/ppermute | solution.py:32
  97.6 12.9 %copy-start.9 = (bf16[256,768]{1,0:T(8,128)(2,1)S(1)}, bf16[256,768]{1,0:T(8,128)(2,1)}, u32[]{:S(2)}) copy-start(bf16[256,768]{1,0:T(8,128)(2,1)} %get-tuple-element.52) | copy-start | bytes 1179652
  97.6 15.7 %collective-permute-start.38 = (bf16[256,512]{1,0:T(8,128)(2,1)S(1)}, bf16[256,512]{1,0:T(8,128)(2,1)S(1)}, u32[]{:S(2)}, u32[]{:S(2)}) collective-permute-start(bf16[256,512]{1,0:T(8,128)(2,1)S(1)} %fusion.7), channel_id=1, source_target_pairs={{0,64},{32,96},{64,0},{96,32},{128,192},{160,224},{192,128},{224,1... | collective-permute-start | bytes 786440 | tf_op jit(solution)/shard_map/ppermute | solution.py:302
  103.2 8.3 %copy-start.8 = (bf16[256,768]{1,0:T(8,128)(2,1)S(1)}, bf16[256,768]{1,0:T(8,128)(2,1)}, u32[]{:S(2)}) copy-start(bf16[256,768]{1,0:T(8,128)(2,1)} %get-tuple-element.55) | copy-start | bytes 1179652
  103.2 26.0 %collective-permute-start.13 = (bf16[128,1280]{1,0:T(8,128)(2,1)}, bf16[128,1280]{1,0:T(8,128)(2,1)}, u32[]{:S(2)}, u32[]{:S(2)}) collective-permute-start(bf16[128,1280]{1,0:T(8,128)(2,1)} %get-tuple-element.34), channel_id=1, source_target_pairs={{0,1},{1,0},{2,3},{3,2},{4,5},{5,4},{6,7},{7,6},{8,9},{9,8},{10,11... | collective-permute-start | bytes 983048 | tf_op jit(solution)/shard_map/ppermute | solution.py:38
  108.0 7.3 %collective-permute-start.19 = (bf16[128,768]{1,0:T(8,128)(2,1)S(1)}, bf16[128,768]{1,0:T(8,128)(2,1)S(1)}, u32[]{:S(2)}, u32[]{:S(2)}) collective-permute-start(bf16[128,768]{1,0:T(8,128)(2,1)S(1)} %slice.43), channel_id=1, source_target_pairs={{0,14},{1,15},{2,0},{3,1},{4,2},{5,3},{6,4},{7,5},{8,6},{9,7},{10,... | collective-permute-start | bytes 589832 | tf_op jit(solution)/shard_map/ppermute | solution.py:32
  110.1 8.2 %collective-permute-start.18 = (bf16[128,768]{1,0:T(8,128)(2,1)S(1)}, bf16[128,768]{1,0:T(8,128)(2,1)S(1)}, u32[]{:S(2)}, u32[]{:S(2)}) collective-permute-start(bf16[128,768]{1,0:T(8,128)(2,1)S(1)} %slice.42), channel_id=1, source_target_pairs={{0,2},{1,3},{2,4},{3,5},{4,6},{5,7},{6,8},{7,9},{8,10},{9,11},{10,... | collective-permute-start | bytes 589832 | tf_op jit(solution)/shard_map/ppermute | solution.py:32
  110.6 18.6 %collective-permute-start.32 = (bf16[256,768]{1,0:T(8,128)(2,1)S(1)}, bf16[256,768]{1,0:T(8,128)(2,1)S(1)}, u32[]{:S(2)}, u32[]{:S(2)}) collective-permute-start(bf16[256,768]{1,0:T(8,128)(2,1)S(1)} %add_convert_fusion.2), channel_id=1, source_target_pairs={{0,2},{1,3},{2,4},{3,5},{4,6},{5,7},{6,8},{7,9},{8,10},{9,11},{10,... | collective-permute-start | bytes 1179656 | tf_op jit(solution)/shard_map/ppermute | solution.py:32
  113.3 17.0 %collective-permute-start.36 = (bf16[256,768]{1,0:T(8,128)(2,1)}, bf16[256,768]{1,0:T(8,128)(2,1)S(1)}, u32[]{:S(2)}, u32[]{:S(2)}) collective-permute-start(bf16[256,768]{1,0:T(8,128)(2,1)} %add_convert_fusion), channel_id=1, source_target_pairs={{0,14},{1,15},{2,0},{3,1},{4,2},{5,3},{6,4},{7,5},{8,6},{9,7},{10,... | collective-permute-start | bytes 1179656 | tf_op jit(solution)/shard_map/ppermute | solution.py:32
  115.3 6.8 %collective-permute-start.39 = (bf16[256,512]{1,0:T(8,128)(2,1)S(1)}, bf16[256,512]{1,0:T(8,128)(2,1)S(1)}, u32[]{:S(2)}, u32[]{:S(2)}) collective-permute-start(bf16[256,512]{1,0:T(8,128)(2,1)S(1)} %fusion.15), channel_id=1, source_target_pairs={{0,128},{32,160},{64,192},{96,224},{128,0},{160,32},{192,64},{224,... | collective-permute-start | bytes 786440 | tf_op jit(solution)/shard_map/ppermute | solution.py:302
  118.3 18.6 %collective-permute-start.14 = (bf16[128,1280]{1,0:T(8,128)(2,1)}, bf16[128,1280]{1,0:T(8,128)(2,1)}, u32[]{:S(2)}, u32[]{:S(2)}) collective-permute-start(bf16[128,1280]{1,0:T(8,128)(2,1)} %get-tuple-element.35), channel_id=1, source_target_pairs={{0,16},{1,17},{2,18},{3,19},{4,20},{5,21},{6,22},{7,23},{8,24},{9,... | collective-permute-start | bytes 983048 | tf_op jit(solution)/shard_map/ppermute | solution.py:38
  122.2 14.8 %collective-permute-start.15 = (bf16[128,1280]{1,0:T(8,128)(2,1)}, bf16[128,1280]{1,0:T(8,128)(2,1)}, u32[]{:S(2)}, u32[]{:S(2)}) collective-permute-start(bf16[128,1280]{1,0:T(8,128)(2,1)} %get-tuple-element.36), channel_id=1, source_target_pairs={{0,17},{1,16},{2,19},{3,18},{4,21},{5,20},{6,23},{7,22},{8,25},{9,... | collective-permute-start | bytes 983048 | tf_op jit(solution)/shard_map/ppermute | solution.py:38
  129.2 7.7 %collective-permute-start.20 = (bf16[128,768]{1,0:T(8,128)(2,1)}, bf16[128,768]{1,0:T(8,128)(2,1)}, u32[]{:S(2)}, u32[]{:S(2)}) collective-permute-start(bf16[128,768]{1,0:T(8,128)(2,1)} %get-tuple-element.38), channel_id=1, source_target_pairs={{0,1},{1,0},{2,3},{3,2},{4,5},{5,4},{6,7},{7,6},{8,9},{9,8},{10,11... | collective-permute-start | bytes 589832 | tf_op jit(solution)/shard_map/ppermute | solution.py:38
  129.2 10.4 %collective-permute-start.21 = (bf16[128,768]{1,0:T(8,128)(2,1)}, bf16[128,768]{1,0:T(8,128)(2,1)S(1)}, u32[]{:S(2)}, u32[]{:S(2)}) collective-permute-start(bf16[128,768]{1,0:T(8,128)(2,1)} %get-tuple-element.39), channel_id=1, source_target_pairs={{0,16},{1,17},{2,18},{3,19},{4,20},{5,21},{6,22},{7,23},{8,24},{9,... | collective-permute-start | bytes 589832 | tf_op jit(solution)/shard_map/ppermute | solution.py:38
  130.4 13.0 %collective-permute-start.22 = (bf16[128,768]{1,0:T(8,128)(2,1)}, bf16[128,768]{1,0:T(8,128)(2,1)S(1)}, u32[]{:S(2)}, u32[]{:S(2)}) collective-permute-start(bf16[128,768]{1,0:T(8,128)(2,1)} %get-tuple-element.40), channel_id=1, source_target_pairs={{0,17},{1,16},{2,19},{3,18},{4,21},{5,20},{6,23},{7,22},{8,25},{9,... | collective-permute-start | bytes 589832 | tf_op jit(solution)/shard_map/ppermute | solution.py:38
  (10 other events, 34.5 us)

commit v2 on v1

v2 whole, which is shorter than its diff:
```python
import jax
import jax.numpy as jnp
from jax import lax
from jax.experimental import pallas as pl
from jax.experimental.pallas import tpu as pltpu
from jax.sharding import PartitionSpec as P

HEAD = 128
N_X, N_Z, N_CORE = 2, 8, 2

begin_token = 128000
rope_base = 500000.0
beta_one = 0.9
beta_two = 0.95
adam_lr = 0.001
adam_eps = 1e-08
adam_step = 10.0
weight_decay = 0.1
outer_lr = 0.7
outer_momentum = 0.9

PLACES = [(x, z, c) for x in range(N_X) for z in range(N_Z) for c in range(N_CORE)]
PEERS = [(0, 0), (0, 1), (1, 0), (1, 1)]


def place(x, z, c):
    return (x * N_Z + z % N_Z) * N_CORE + c


def along_z(value, distance):
    pairs = [(place(x, z, c), place(x, z + distance, c)) for x, z, c in PLACES]
    return lax.ppermute(value, "fsdp", pairs)


def with_peer(value, peer):
    flip_x, flip_c = PEERS[peer]
    pairs = [(place(x, z, c), place(x ^ flip_x, z, c ^ flip_c)) for x, z, c in PLACES]
    return lax.ppermute(value, "fsdp", pairs)


def turn_tables(positions):
    half_head = HEAD // 2
    lane = jnp.arange(HEAD, dtype=jnp.int32)
    frequency = jnp.float32(rope_base) ** (
        -((lane % half_head).astype(jnp.float32) * (2.0 / HEAD))
    )
    angles = positions.astype(jnp.float32)[:, None] * frequency[None, :]
    sign = jnp.where(lane < half_head, 1.0, -1.0).astype(jnp.float32)
    return jnp.cos(angles), jnp.sin(angles) * sign[None, :]


def place_index(x, z, c, peer):
    flip_x, flip_c = PEERS[peer]
    return ((x ^ flip_x) * N_Z + z) * N_CORE + (c ^ flip_c)


def tie(value, *others):
    return lax.optimization_barrier((value, *others))[0]


FAR = (4, 3, -3)
NEAR = (2, -2, 1, -1, 0)
RING = (0, 1, -1, 2, -2, 3, -3, 4)


def room(mebibytes):
    return pltpu.CompilerParams(vmem_limit_bytes=mebibytes * 2**20)


def run_copies(copies):
    for copy in copies:
        copy.start()
    for copy in copies:
        copy.wait()


def vmem(count):
    return [pl.BlockSpec(memory_space=pltpu.VMEM)] * count


def pack_columns(inputs, cotangent, bases, width):
    tokens, depth = cotangent.shape
    steps = FAR + NEAR
    cut = len(FAR)

    def kernel(base_ref, in_ref, cot_ref, own, beside, far_2, far_3, near_2, near_3, sem):
        copies = []
        for peer in range(4):
            for at, ahead in enumerate(steps):
                step = lax.rem(base_ref[4] + (ahead + N_Z), N_Z)
                column = pl.multiple_of(base_ref[peer] + step * (N_CORE * width), width)
                if peer < 2:
                    out, first = (own, beside)[peer], at
                elif at < cut:
                    out, first = (far_2, far_3)[peer - 2], at
                else:
                    out, first = (near_2, near_3)[peer - 2], at - cut
                copies.append(
                    pltpu.make_async_copy(
                        in_ref.at[:, pl.ds(column, width)],
                        out.at[:, pl.ds(first * width, width)],
                        sem.at[len(copies)],
                    )
                )
        last = len(steps) * width
        copies.append(pltpu.make_async_copy(cot_ref, beside.at[:, pl.ds(last, depth)], sem.at[len(copies)]))
        run_copies(copies)

    widths = [len(steps) * width, len(steps) * width + depth]
    widths += [cut * width] * 2 + [len(NEAR) * width] * 2
    return pl.pallas_call(
        kernel,
        out_shape=[jax.ShapeDtypeStruct((tokens, columns), inputs.dtype) for columns in widths],
        in_specs=[pl.BlockSpec(memory_space=pltpu.SMEM)] + [pl.BlockSpec(memory_space=pl.ANY)] * 2,
        out_specs=vmem(6),
        scratch_shapes=[pltpu.SemaphoreType.DMA((4 * N_Z + 1,))],
        compiler_params=room(8),
        cost_estimate=pl.CostEstimate(flops=0, bytes_accessed=4 * inputs.size, transcendentals=0),
    )(bases, inputs, cotangent)


def unpack_columns(parts, bases, width):
    tokens = parts[0].shape[0]
    columns = 4 * N_Z * width

    def kernel(base_ref, *refs):
        ins, out_ref, sem = refs[:4], refs[4], refs[5]
        copies = []
        for peer in range(4):
            for at, ahead in enumerate(RING):
                step = lax.rem(base_ref[4] + (ahead + N_Z), N_Z)
                column = pl.multiple_of(base_ref[peer] + step * (N_CORE * width), width)
                copies.append(
                    pltpu.make_async_copy(
                        ins[peer].at[:, pl.ds(at * width, width)],
                        out_ref.at[:, pl.ds(column, width)],
                        sem.at[len(copies)],
                    )
                )
        run_copies(copies)

    return pl.pallas_call(
        kernel,
        out_shape=jax.ShapeDtypeStruct((tokens, columns), parts[0].dtype),
        in_specs=[pl.BlockSpec(memory_space=pltpu.SMEM)] + vmem(4),
        out_specs=pl.BlockSpec(memory_space=pl.ANY),
        scratch_shapes=[pltpu.SemaphoreType.DMA((4 * N_Z,))],
        compiler_params=room(8),
        cost_estimate=pl.CostEstimate(flops=0, bytes_accessed=4 * tokens * columns, transcendentals=0),
    )(bases, *parts)


def back_products(grads, weights):
    tokens, depth = grads.shape[0] // 4, grads.shape[1]
    rows = weights[0].shape[0]
    count = len(weights)

    def kernel(g_ref, *refs):
        w_refs, outs = refs[:count], refs[count:]
        grad = g_ref[...]
        for at, w_ref in enumerate(w_refs):
            product = lax.dot_general(
                grad, w_ref[...], (((1,), (1,)), ((), ())), preferred_element_type=jnp.float32
            ).astype(jnp.bfloat16)
            for peer in range(4):
                outs[peer][:, at * rows : (at + 1) * rows] = product[peer * tokens : (peer + 1) * tokens]

    return pl.pallas_call(
        kernel,
        out_shape=[jax.ShapeDtypeStruct((tokens, count * rows), jnp.bfloat16)] * 4,
        in_specs=vmem(1 + count),
        out_specs=vmem(4),
        compiler_params=room(16),
        cost_estimate=pl.CostEstimate(
            flops=8 * tokens * depth * count * rows,
            bytes_accessed=2 * (4 * tokens * depth + count * rows * depth + 4 * tokens * count * rows),
            transcendentals=0,
        ),
    )(grads, *weights)


def turn_and_multiply(cotangents, whole, far, tables, width):
    tokens, depth = cotangents[0].shape
    half = width // 2

    def kernel(c_ref, s_ref, cot, cot_2, cot_3, own, beside, far_2, far_3, turned, first, second):
        for peer, (ref, at_column) in enumerate(
            ((cot, 0), (beside, beside.shape[1] - depth), (cot_2, 0), (cot_3, 0))
        ):
            at = slice(peer * tokens, (peer + 1) * tokens)
            cosine, sine_part = c_ref[at, :], s_ref[at, :]
            for head in range(depth // HEAD):
                lane = at_column + head * HEAD
                value = ref[:, lane : lane + HEAD].astype(jnp.float32)
                other = pltpu.roll(value, HEAD // 2, 1)
                turned[at, head * HEAD : (head + 1) * HEAD] = (
                    value * cosine + other * sine_part
                ).astype(jnp.bfloat16)
        product = block_product((own, beside, far_2, far_3), 0, 0, width, turned[...])
        first[...] = product[:half]
        second[...] = product[half:]

    return pl.pallas_call(
        kernel,
        out_shape=[jax.ShapeDtypeStruct((4 * tokens, depth), jnp.bfloat16)]
        + [jax.ShapeDtypeStruct((half, depth), jnp.bfloat16)] * 2,
        in_specs=vmem(9),
        out_specs=vmem(3),
        compiler_params=room(12),
        cost_estimate=product_cost(tokens, depth, width, 1),
    )(*tables, *cotangents, *whole, *far)


def multiply(whole, part, grads, width, steps, part_steps):
    tokens, depth = grads.shape[0] // 4, grads.shape[1]
    order = FAR + NEAR

    def kernel(g_ref, *refs):
        ins, outs = refs[:4], refs[4:]
        grad = g_ref[...]
        for ahead, out in zip(steps, outs):
            out[...] = block_product(ins, order.index(ahead), part_steps.index(ahead), width, grad)

    return pl.pallas_call(
        kernel,
        out_shape=[jax.ShapeDtypeStruct((width, depth), jnp.bfloat16)] * len(steps),
        in_specs=vmem(5),
        out_specs=vmem(len(steps)),
        compiler_params=room(12),
        cost_estimate=product_cost(tokens, depth, width, len(steps)),
    )(grads, *whole, *part)


def block_product(ins, at_whole, at_part, width, grad):
    places = [at_whole * width] * 2 + [at_part * width] * 2
    block = jnp.concatenate([ref[:, p : p + width] for ref, p in zip(ins, places)], axis=0)
    return lax.dot_general(
        block, grad, (((0,), (0,)), ((), ())), preferred_element_type=jnp.float32
    ).astype(jnp.bfloat16)


def product_cost(tokens, depth, width, blocks):
    return pl.CostEstimate(
        flops=8 * tokens * depth * blocks * width,
        bytes_accessed=2 * (4 * tokens * depth + blocks * width * depth + 4 * tokens * blocks * width),
        transcendentals=0,
    )


def added(arrived, term):
    return (arrived.astype(jnp.float32) + term.astype(jnp.float32)).astype(jnp.bfloat16)


def add_halves(forward, backward, up, down):
    half = forward.shape[0]

    def kernel(f_ref, b_ref, u_ref, d_ref, f_out, b_out):
        f_out[:half] = added(f_ref[...], u_ref[:half])
        f_out[half:] = u_ref[half:]
        b_out[:half] = d_ref[:half]
        b_out[half:] = added(b_ref[...], d_ref[half:])

    return pl.pallas_call(
        kernel,
        out_shape=[jax.ShapeDtypeStruct(up.shape, up.dtype)] * 2,
        in_specs=vmem(4),
        out_specs=vmem(2),
        compiler_params=room(6),
        cost_estimate=pl.CostEstimate(flops=2 * up.size, bytes_accessed=10 * up.size, transcendentals=0),
    )(forward, backward, up, down)


def add_pair(forward, backward, up, down):
    def kernel(f_ref, b_ref, u_ref, d_ref, f_out, b_out):
        f_out[...] = added(f_ref[...], u_ref[...])
        b_out[...] = added(b_ref[...], d_ref[...])

    return pl.pallas_call(
        kernel,
        out_shape=[jax.ShapeDtypeStruct(up.shape, up.dtype)] * 2,
        in_specs=vmem(4),
        out_specs=vmem(2),
        compiler_params=room(6),
        cost_estimate=pl.CostEstimate(flops=2 * up.size, bytes_accessed=12 * up.size, transcendentals=0),
    )(forward, backward, up, down)


def adam(forward, backward, own, key_weight, adam_m, adam_v, seq_len):
    rows, columns = own.shape
    step_rows = rows // 4

    def kernel(f_ref, b_ref, o_ref, w_ref, m_ref, v_ref, nw_ref, nm_ref, nv_ref):
        total = (
            f_ref[...].astype(jnp.float32)
            + b_ref[...].astype(jnp.float32)
            + o_ref[...].astype(jnp.float32)
        )
        grad = total * (1.0 / seq_len)
        weight = w_ref[0]
        mean = beta_one * m_ref[0] + (1.0 - beta_one) * grad
        square = beta_two * v_ref[0] + (1.0 - beta_two) * grad * grad
        mean_hat = mean * (1.0 / (1.0 - beta_one**adam_step))
        square_hat = square * (1.0 / (1.0 - beta_two**adam_step))
        nm_ref[0] = mean
        nv_ref[0] = square
        nw_ref[0] = weight - adam_lr * (
            mean_hat / (jnp.sqrt(square_hat) + adam_eps) + weight_decay * weight
        )

    flat = pl.BlockSpec((step_rows, columns), lambda i: (i, 0))
    deep = pl.BlockSpec((1, step_rows, columns), lambda i: (0, i, 0))
    return pl.pallas_call(
        kernel,
        grid=(4,),
        out_shape=[jax.ShapeDtypeStruct((1, rows, columns), jnp.float32)] * 3,
        in_specs=[flat] * 3 + [deep] * 3,
        out_specs=[deep] * 3,
        compiler_params=room(12),
        cost_estimate=pl.CostEstimate(flops=20 * own.size, bytes_accessed=30 * own.size, transcendentals=own.size),
    )(forward, backward, own, key_weight, adam_m, adam_v)


def outer_sync(frag_local, frag_global, outer_mom, owner, fragment, after, before_swap):
    replica_count = lax.axis_size("replica")
    is_owner = tie(lax.axis_index("replica") == owner[0], after)
    gain = outer_lr * (1.0 + outer_momentum)
    mom_gain = outer_lr * outer_momentum * outer_momentum
    local_slot = lax.dynamic_index_in_dim(frag_local[0], fragment[0], 0, keepdims=False)
    state_global, state_mom = frag_global[0], outer_mom[0]
    synced = (gain / replica_count) * local_slot + jnp.where(
        is_owner, (1.0 - gain) * state_global - mom_gain * state_mom, 0.0
    )
    synced = tie(synced, before_swap)
    for flip in (1, 2, 4):
        pairs = [(r, r ^ flip) for r in range(replica_count)]
        arrived = lax.ppermute(synced.astype(jnp.bfloat16), "replica", pairs)
        synced = synced + arrived.astype(jnp.float32)
    outer_grad = (state_global - mom_gain * state_mom - synced) / gain
    mom_next = outer_momentum * state_mom + outer_grad
    return synced[None], jnp.where(is_owner, mom_next, state_mom)[None]


def on_device(
    token_ids,
    inputs,
    key_cotangent,
    key_weight,
    adam_m,
    adam_v,
    frag_local,
    frag_global,
    outer_mom,
    owner,
    fragment,
):
    rows_here = inputs.shape[0]
    width = key_weight.shape[1]
    seq_len = rows_here * lax.axis_size("fsdp")
    index = lax.axis_index("fsdp")
    x, z, c = index // (N_Z * N_CORE), (index // N_CORE) % N_Z, index % N_CORE

    bases = jnp.stack(
        [((x ^ flip_x) * N_Z * N_CORE + (c ^ flip_c)) * width for flip_x, flip_c in PEERS] + [z]
    ).astype(jnp.int32)

    ids = [token_ids] + [with_peer(token_ids, p) for p in (1, 2, 3)]
    across = with_peer(key_cotangent, 2)

    half = width // 2
    held = {0: tie(key_weight[0].astype(jnp.bfloat16), *ids[1:])}
    held[-1], held[1] = along_z(held[0], 1), along_z(held[0], -1)

    own, *packed = pack_columns(inputs, key_cotangent, tie(bases, *ids[1:]), width)
    far = [with_peer(packed[1], 2), with_peer(packed[2], 3)]
    whole = [own, with_peer(packed[0], 1)]
    cotangents = [key_cotangent, across, with_peer(tie(across, packed[0]), 1)]

    ids = jnp.stack(ids)
    indices = jnp.stack([place_index(x, z, c, p) for p in range(4)])
    token_index = indices[:, None] * rows_here + jnp.arange(rows_here, dtype=jnp.int32)[None, :]
    starts = jnp.where(ids == begin_token, token_index, -1)
    rank = jnp.arange(N_Z, dtype=jnp.int32)
    newest = jnp.where((rank == z)[:, None], jnp.max(starts, axis=1)[None, :], -1)
    newest = jnp.maximum(newest, jnp.maximum(along_z(newest, 1), along_z(newest, -1)))
    newest = tie(newest, packed[0], held[1], held[-1])
    newest = jnp.maximum(newest, jnp.maximum(along_z(newest, 3), along_z(newest, -3)))
    held[-2], held[2] = along_z(held[-1], 1), along_z(held[1], -1)
    all_indices = jnp.stack([place_index(x, rank, c, p) for p in range(4)], axis=1)
    before = all_indices[None, :, :] < indices[:, None, None]
    earlier = jnp.max(jnp.where(before, newest[None], -1), axis=(1, 2))
    lane = jnp.arange(rows_here, dtype=jnp.int32)
    upto = lane[None, :] <= lane[:, None]
    latest = jnp.max(jnp.where(upto[None], starts[:, None, :], -1), axis=2)
    positions = token_index - jnp.maximum(latest, earlier[:, None])
    tables = turn_tables(tie(positions, whole[1], far[0], far[1]).reshape(-1))

    near = [with_peer(tie(packed[3], newest), 2), with_peer(tie(packed[4], newest), 3)]

    grads, first, second = turn_and_multiply(cotangents, whole, far, tables, width)
    forward, backward = along_z(first, 1), along_z(second, -1)
    up, down = multiply(whole, far, grads, width, (3, -3), FAR)
    up = tie(up, held[2], held[-2])
    held[-3], held[3] = along_z(held[-2], 1), along_z(held[2], -1)
    summed = add_halves(forward, backward, up, down)
    forward, backward = along_z(summed[0], 1), along_z(summed[1], -1)
    up, down, up_1, down_1, term = multiply(whole, near, tie(grads, summed[0]), width, NEAR, NEAR)
    opposite = along_z(held[-3][:half], 1), along_z(held[3][half:], -1)
    forward, backward = add_pair(forward, backward, tie(up, held[3], held[-3]), down)
    forward, backward = along_z(forward, 1), along_z(backward, -1)

    synced, new_outer_mom = outer_sync(frag_local, frag_global, outer_mom, owner, fragment, newest, term)
    held[4] = jnp.concatenate(opposite)
    back = back_products(grads, [held[ahead] for ahead in RING])
    parts = [back[0]] + [with_peer(back[p], p) for p in (1, 2, 3)]

    forward, backward = add_pair(forward, backward, tie(up_1, back[0]), down_1)
    forward, backward = along_z(forward, 1), along_z(backward, -1)
    input_cotangent = unpack_columns(parts, bases, width)
    term = tie(term, input_cotangent)
    new_weight, new_m, new_v = adam(forward, backward, term, key_weight, adam_m, adam_v, seq_len)
    return (input_cotangent, new_weight, new_m, new_v, synced, new_outer_mom)


def solution(mesh):
    in_specs = (
        P(("replica", "fsdp")),
        P(("replica", "fsdp"), None),
        P(("replica", "fsdp"), None),
        P("replica", "fsdp", None),
        P("replica", "fsdp", None),
        P("replica", "fsdp", None),
        P("replica", None, "fsdp", None),
        P("replica", "fsdp", None),
        P("replica", "fsdp", None),
        P("fsdp"),
        P("replica"),
    )
    out_specs = (
        P(("replica", "fsdp"), None),
        P("replica", "fsdp", None),
        P("replica", "fsdp", None),
        P("replica", "fsdp", None),
        P("replica", "fsdp", None),
        P("replica", "fsdp", None),
    )
    return jax.shard_map(
        on_device, mesh=mesh, in_specs=in_specs, out_specs=out_specs, check_vma=False
    )
```

time: 148 us -> 112 us (0.76)
  Pallas kernels: 26.6 us -> 10.5 us
  starting transfers between devices: 57.8 us -> 50.5 us
  local copies, waits for them, and re-layouts: 8.32 us -> 2.66 us
  other arithmetic: 12 us -> 6.43 us
    ppermute x19 -> x20, waiting for transfers between devices: 24.3 us -> 15.9 us  [along_z(): return lax.ppermute(value, 'fsdp', pairs)]
    pallas_call x3 -> x7, Pallas kernels: 12.2 us -> 4.38 us  [the longest x2 1.82 us: multiply(): pl.pallas_call(kernel, out_shape=[jax.ShapeDtypeStruct((width, depth), jn...]
    ppermute x18 -> x13, waiting for transfers between devices: 13.1 us -> 20.7 us  [with_peer(): return lax.ppermute(value, 'fsdp', pairs)]
    ppermute x18 -> x13, starting transfers between devices: 25.8 us -> 18.7 us  [with_peer(): return lax.ppermute(value, 'fsdp', pairs)]
    pallas_call x2 -> x1, Pallas kernels: 7.01 us -> 1.82 us  [back_products(): pl.pallas_call(kernel, out_shape=[jax.ShapeDtypeStruct((tokens, count * r...]
    convert_element_type x9 -> x2, other arithmetic: 6.05 us -> 1.18 us  [the longest x1 1.18 us: on_device(): held = {0: tie(key_weight[0].astype(jnp.bfloat16), *ids[1:])}]
    slice x5 -> x2, local copies, waits for them, and re-layouts: 3.03 us -> 0.03 us  [on_device(): opposite = (along_z(held[-3][:half], 1), along_z(held[3][half:], -1))]
    pallas_call x1, Pallas kernels: 4.34 us -> 2.19 us  [adam(): pl.pallas_call(kernel, grid=(4,), out_shape=[jax.ShapeDtypeStruct((1, row...]
  transfers between devices with their start and end apart: 40 -> 36, of which waited for: 12 -> 14; matrix products, arithmetic and copies ran while one was open for 11% -> 6% of each run, Pallas kernels for 13% -> 7%
where the time goes in v2:
time: 112 us
  starting transfers between devices  50.5 us (45%)
  waiting for transfers between devices  39.2 us (35%)
  Pallas kernels  10.5 us (9%)
  other arithmetic  6.43 us (6%)
  local copies, waits for them, and re-layouts  2.66 us (2%)
  between operations  2.32 us (2%)
    ppermute x20, starting transfers between devices, along_z(): return lax.ppermute(value, 'fsdp', pairs)  25.1 us
    ppermute x13, waiting for transfers between devices, with_peer(): return lax.ppermute(value, 'fsdp', pairs)  20.7 us
    ppermute x13, starting transfers between devices, with_peer(): return lax.ppermute(value, 'fsdp', pairs)  18.7 us
    ppermute x20, waiting for transfers between devices, along_z(): return lax.ppermute(value, 'fsdp', pairs)  15.9 us
    ppermute x3, starting transfers between devices, outer_sync(): arrived = lax.ppermute(synced.astype(jnp.bfloat16), 'replica', pairs)  6.62 us
    ppermute x3, waiting for transfers between devices, outer_sync(): arrived = lax.ppermute(synced.astype(jnp.bfloat16), 'replica', pairs)  2.63 us
    unnamed x16, local copies, waits for them, and re-layouts  2.54 us
  transfers between devices with their start and end apart: 36, of which 14 were waited for; matrix products, arithmetic and copies ran while one was open for 6% of the time, Pallas kernels for 7%

profile of v2, /device:TPU:1, one launch (start us, length us, event | category | flops | bytes accessed | tf_op | source)
XLA Modules:
  0.0 111.6 jit_solution(14128142961855420504)
XLA Ops:
  0.6 3.3 %collective-permute-start = (s32[128]{0:T(128)}, s32[128]{0:T(128)S(1)}, u32[]{:S(2)}, u32[]{:S(2)}) collective-permute-start(s32[128]{0:T(128)} %param.11), channel_id=1, source_target_pairs={{0,1},{1,0},{2,3},{3,2},{4,5},{5,4},{6,7},{7,6},{8,9},{9,8},{10,11... | collective-permute-start | bytes 1544 | tf_op jit(solution)/shard_map/ppermute | solution.py:38
  4.0 1.5 %collective-permute-start.1 = (s32[128]{0:T(128)}, s32[128]{0:T(128)S(1)}, u32[]{:S(2)}, u32[]{:S(2)}) collective-permute-start(s32[128]{0:T(128)} %param.11), channel_id=1, source_target_pairs={{0,16},{1,17},{2,18},{3,19},{4,20},{5,21},{6,22},{7,23},{8,24},{9,... | collective-permute-start | bytes 1544 | tf_op jit(solution)/shard_map/ppermute | solution.py:38
  6.9 1.2 %convert_bitcast_fusion.refs_0_ = bf16[256,768]{1,0:T(8,128)(2,1)S(1)} fusion(f32[1,256,768]{2,1,0:T(8,128)} %w_ref.1), kind=kLoop, calls=%fused_computation.16 | loop fusion | flops 196608 | bytes 1179648 | tf_op jit(solution)/shard_map/convert_element_type | solution.py:370
  8.3 1.1 %collective-permute-start.6 = (bf16[256,768]{1,0:T(8,128)(2,1)S(1)}, bf16[256,768]{1,0:T(8,128)(2,1)S(1)}, u32[]{:S(2)}, u32[]{:S(2)}) collective-permute-start(bf16[256,768]{1,0:T(8,128)(2,1)S(1)} %convert_bitcast_fusion.refs_0_), channel_id=1, source_target_pairs={{0,2},{1,3},{2,4},{3,5},{4,6},{5,7},{6,8},{7,9},{8,10},{9,11},{10,... | collective-permute-start | bytes 1179656 | tf_op jit(solution)/shard_map/ppermute | solution.py:32
  9.4 4.0 %collective-permute-start.5 = (bf16[256,768]{1,0:T(8,128)(2,1)S(1)}, bf16[256,768]{1,0:T(8,128)(2,1)S(1)}, u32[]{:S(2)}, u32[]{:S(2)}) collective-permute-start(bf16[256,768]{1,0:T(8,128)(2,1)S(1)} %convert_bitcast_fusion.refs_0_), channel_id=1, source_target_pairs={{0,14},{1,15},{2,0},{3,1},{4,2},{5,3},{6,4},{7,5},{8,6},{9,7},{10,... | collective-permute-start | bytes 1179656 | tf_op jit(solution)/shard_map/ppermute | solution.py:32
  13.4 0.8 fusion.20
  14.3 1.4 %collective-permute-start.4 = (s32[8,4]{0,1:T(4,128)S(1)}, s32[8,4]{0,1:T(4,128)S(1)}, u32[]{:S(2)}, u32[]{:S(2)}) collective-permute-start(s32[8,4]{0,1:T(4,128)S(1)} %broadcast_select_fusion), channel_id=1, source_target_pairs={{0,14},{1,15},{2,0},{3,1},{4,2},{5,3},{6,4},{7,5},{8,6},{9,7},{10,... | collective-permute-start | bytes 392 | tf_op jit(solution)/shard_map/ppermute | solution.py:32
  16.0 1.6 %copy-done.1 = bf16[128,8192]{1,0:T(8,128)(2,1)S(1)} copy-done((bf16[128,8192]{1,0:T(8,128)(2,1)S(1)}, bf16[128,8192]{1,0:T(8,128)(2,1)}, u32[]{:S(2)}) %copy-start.1) | copy-done | bytes 2097176
  17.6 0.9 copy-done.4
  18.5 1.3 %shard_map.154 = (bf16[128,2048]{1,0:T(8,128)(2,1)S(1)}, bf16[128,2816]{1,0:T(8,128)(2,1)S(1)}, bf16[128,768]{1,0:T(8,128)(2,1)S(1)}, bf16[128,768]{1,0:T(8,128)...) custom-call(s32[5]{0:T(128)S(1)} %stack.60.base_ref, bf16[128,8192]{1,0:T(8,128)(2,1)S(1)} %copy-done.1, ...), custom_call_target="tpu_custom_call" | custom-call | bytes 4194304 | tf_op jit(solution)/shard_map/pallas_call | solution.py:111
  19.9 1.0 collective-permute-done.4
  21.9 1.6 %collective-permute-start.9 = (bf16[128,2816]{1,0:T(8,128)(2,1)S(1)}, bf16[128,2816]{1,0:T(8,128)(2,1)S(1)}, u32[]{:S(2)}, u32[]{:S(2)}) collective-permute-start(bf16[128,2816]{1,0:T(8,128)(2,1)S(1)} %get-tuple-element.50), channel_id=1, source_target_pairs={{0,1},{1,0},{2,3},{3,2},{4,5},{5,4},{6,7},{7,6},{8,9},{9,8},{10,11... | collective-permute-start | bytes 2162696 | tf_op jit(solution)/shard_map/ppermute | solution.py:38
  23.5 1.0 collective-permute-start.11
  24.6 3.7 %collective-permute-start.8 = (s32[8,4]{0,1:T(4,128)S(1)}, s32[8,4]{0,1:T(4,128)S(1)}, u32[]{:S(2)}, u32[]{:S(2)}) collective-permute-start(s32[8,4]{0,1:T(4,128)S(1)} %maximum_maximum_fusion.1), channel_id=1, source_target_pairs={{0,10},{1,11},{2,12},{3,13},{4,14},{5,15},{6,0},{7,1},{8,2},{9,3},... | collective-permute-start | bytes 392 | tf_op jit(solution)/shard_map/ppermute | solution.py:32
  28.3 1.3 %collective-permute-start.7 = (s32[8,4]{0,1:T(4,128)S(1)}, s32[8,4]{0,1:T(4,128)S(1)}, u32[]{:S(2)}, u32[]{:S(2)}) collective-permute-start(s32[8,4]{0,1:T(4,128)S(1)} %maximum_maximum_fusion.1), channel_id=1, source_target_pairs={{0,6},{1,7},{2,8},{3,9},{4,10},{5,11},{6,12},{7,13},{8,14},{9,15},... | collective-permute-start | bytes 392 | tf_op jit(solution)/shard_map/ppermute | solution.py:32
  29.6 0.9 collective-permute-done.8
  30.5 1.4 %collective-permute-start.13 = (bf16[128,768]{1,0:T(8,128)(2,1)S(1)}, bf16[128,768]{1,0:T(8,128)(2,1)S(1)}, u32[]{:S(2)}, u32[]{:S(2)}) collective-permute-start(bf16[128,768]{1,0:T(8,128)(2,1)S(1)} %collective-permute-done.12.cot_2), channel_id=1, source_target_pairs={{0,1},{1,0},{2,3},{3,2},{4,5},{5,4},{6,7},{7,6},{8,9},{9,8},{10,11... | collective-permute-start | bytes 589832 | tf_op jit(solution)/shard_map/ppermute | solution.py:38
  31.8 1.9 %collective-permute-done.7 = s32[8,4]{0,1:T(4,128)S(1)} collective-permute-done((s32[8,4]{0,1:T(4,128)S(1)}, s32[8,4]{0,1:T(4,128)S(1)}, u32[]{:S(2)}, u32[]{:S(2)}) %collective-permute-start.7) | collective-permute-done | bytes 160 | tf_op jit(solution)/shard_map/ppermute | solution.py:32
  33.7 0.7 collective-permute-start.15
  34.8 2.0 %collective-permute-start.14 = (bf16[256,768]{1,0:T(8,128)(2,1)S(1)}, bf16[256,768]{1,0:T(8,128)(2,1)S(1)}, u32[]{:S(2)}, u32[]{:S(2)}) collective-permute-start(bf16[256,768]{1,0:T(8,128)(2,1)S(1)} %collective-permute-done.5.refs_1_), channel_id=1, source_target_pairs={{0,14},{1,15},{2,0},{3,1},{4,2},{5,3},{6,4},{7,5},{8,6},{9,7},{10,... | collective-permute-start | bytes 1179656 | tf_op jit(solution)/shard_map/ppermute | solution.py:32
  37.0 3.9 %collective-permute-start.28 = (bf16[128,1280]{1,0:T(8,128)(2,1)S(1)}, bf16[128,1280]{1,0:T(8,128)(2,1)S(1)}, u32[]{:S(2)}, u32[]{:S(2)}) collective-permute-start(bf16[128,1280]{1,0:T(8,128)(2,1)S(1)} %get-tuple-element.74), channel_id=1, source_target_pairs={{0,17},{1,16},{2,19},{3,18},{4,21},{5,20},{6,23},{7,22},{8,25},{9,... | collective-permute-start | bytes 983048 | tf_op jit(solution)/shard_map/ppermute | solution.py:38
  40.9 1.0 fusion.9
  41.9 0.8 shard_map.155
  42.8 0.9 collective-permute-done.15.refs_4_
  43.6 1.8 %collective-permute-start.24 = (bf16[128,768]{1,0:T(8,128)(2,1)S(1)}, bf16[128,768]{1,0:T(8,128)(2,1)S(1)}, u32[]{:S(2)}, u32[]{:S(2)}) collective-permute-start(bf16[128,768]{1,0:T(8,128)(2,1)S(1)} %get-tuple-element.64), channel_id=1, source_target_pairs={{0,14},{1,15},{2,0},{3,1},{4,2},{5,3},{6,4},{7,5},{8,6},{9,7},{10,... | collective-permute-start | bytes 589832 | tf_op jit(solution)/shard_map/ppermute | solution.py:32
  45.4 1.2 %fusion.4 = f32[256,512]{1,0:T(8,128)S(1)} fusion(f32[1,256,512]{2,1,0:T(8,128)S(1)} %copy-done.7, f32[1,3,256,512]{3,2,1,0:T(8,128)} %param.17, s32[]{:T(128)S(6)} %select_n.84, f32[1,256,512]{2,1,0:T(8,128)S(1)} %copy-done.6, pred[]{:T(512)S(6)} %eq.32), kind=kLoop, calls=%fused_computation.9 | loop fusion | flops 786432 | bytes 2097157 | tf_op jit(solution)/shard_map/add | solution.py:330
  46.8 3.2 %collective-permute-done.23.f_ref = bf16[128,768]{1,0:T(8,128)(2,1)S(1)} collective-permute-done((bf16[128,768]{1,0:T(8,128)(2,1)S(1)}, bf16[128,768]{1,0:T(8,128)(2,1)S(1)}, u32[]{:S(2)}, u32[]{:S(2)}) %collective-permute-start.23) | collective-permute-done | bytes 196640 | tf_op jit(solution)/shard_map/ppermute | solution.py:32
  50.0 1.0 collective-permute-start.16
  51.8 1.7 %collective-permute-done.28.refs_3_ = bf16[128,1280]{1,0:T(8,128)(2,1)S(1)} collective-permute-done((bf16[128,1280]{1,0:T(8,128)(2,1)S(1)}, bf16[128,1280]{1,0:T(8,128)(2,1)S(1)}, u32[]{:S(2)}, u32[]{:S(2)}) %collective-permute-start.28) | collective-permute-done | bytes 327712 | tf_op jit(solution)/shard_map/ppermute | solution.py:38
  53.5 1.2 %shard_map.160 = (bf16[256,768]{1,0:T(8,128)(2,1)S(1)}, bf16[256,768]{1,0:T(8,128)(2,1)S(1)}, bf16[256,768]{1,0:T(8,128)(2,1)S(1)}, bf16[256,768]{1,0:T(8,128)(2,1)S(1)}, bf16[256,768]{1,0:T(8,128)(2,1)S(1)}) custom-call(bf16[512,768]{1,0:T(8,128)(2,1)S(1)} %get-tuple-element.70.g_ref, bf16[128,2048]{1,0:T(8,128)(2,1)S(1)} %get-tuple-element.57.own.refs_0_, ...), custom_call_target="tpu_custom_call" | custom-call | flops 1006632960 | bytes 4063232 | tf_op jit(solution)/shard_map/pallas_call | solution.py:224
  54.8 2.2 %collective-permute-start.33 = (bf16[256,512]{1,0:T(8,128)(2,1)S(1)}, bf16[256,512]{1,0:T(8,128)(2,1)S(1)}, u32[]{:S(2)}, u32[]{:S(2)}) collective-permute-start(bf16[256,512]{1,0:T(8,128)(2,1)S(1)} %convert_element_type.46), channel_id=1, source_target_pairs={{0,32},{32,0},{64,96},{96,64},{128,160},{160,128},{192,224},{224,1... | collective-permute-start | bytes 786440 | tf_op jit(solution)/shard_map/ppermute | solution.py:336
  57.0 1.5 %collective-permute-start.26 = (bf16[256,768]{1,0:T(8,128)(2,1)S(1)}, bf16[256,768]{1,0:T(8,128)(2,1)S(1)}, u32[]{:S(2)}, u32[]{:S(2)}) collective-permute-start(bf16[256,768]{1,0:T(8,128)(2,1)S(1)} %get-tuple-element.69), channel_id=1, source_target_pairs={{0,14},{1,15},{2,0},{3,1},{4,2},{5,3},{6,4},{7,5},{8,6},{9,7},{10,... | collective-permute-start | bytes 1179656 | tf_op jit(solution)/shard_map/ppermute | solution.py:32
  58.6 2.1 %collective-permute-done.16.refs_5_ = bf16[256,768]{1,0:T(8,128)(2,1)S(1)} collective-permute-done((bf16[256,768]{1,0:T(8,128)(2,1)S(1)}, bf16[256,768]{1,0:T(8,128)(2,1)S(1)}, u32[]{:S(2)}, u32[]{:S(2)}) %collective-permute-start.16) | collective-permute-done | bytes 393248 | tf_op jit(solution)/shard_map/ppermute | solution.py:32
  61.4 2.6 %collective-permute-done.33 = bf16[256,512]{1,0:T(8,128)(2,1)S(1)} collective-permute-done((bf16[256,512]{1,0:T(8,128)(2,1)S(1)}, bf16[256,512]{1,0:T(8,128)(2,1)S(1)}, u32[]{:S(2)}, u32[]{:S(2)}) %collective-permute-start.33) | collective-permute-done | bytes 262176 | tf_op jit(solution)/shard_map/ppermute | solution.py:336
  64.1 1.4 %collective-permute-start.34 = (bf16[256,512]{1,0:T(8,128)(2,1)S(1)}, bf16[256,512]{1,0:T(8,128)(2,1)S(1)}, u32[]{:S(2)}, u32[]{:S(2)}) collective-permute-start(bf16[256,512]{1,0:T(8,128)(2,1)S(1)} %fusion.7), channel_id=1, source_target_pairs={{0,64},{32,96},{64,0},{96,32},{128,192},{160,224},{192,128},{224,1... | collective-permute-start | bytes 786440 | tf_op jit(solution)/shard_map/ppermute | solution.py:336
  65.5 3.6 %collective-permute-done.26.b_ref = bf16[256,768]{1,0:T(8,128)(2,1)S(1)} collective-permute-done((bf16[256,768]{1,0:T(8,128)(2,1)S(1)}, bf16[256,768]{1,0:T(8,128)(2,1)S(1)}, u32[]{:S(2)}, u32[]{:S(2)}) %collective-permute-start.26) | collective-permute-done | bytes 393248 | tf_op jit(solution)/shard_map/ppermute | solution.py:32
  69.6 2.7 %collective-permute-start.30 = (bf16[256,768]{1,0:T(8,128)(2,1)S(1)}, bf16[256,768]{1,0:T(8,128)(2,1)S(1)}, u32[]{:S(2)}, u32[]{:S(2)}) collective-permute-start(bf16[256,768]{1,0:T(8,128)(2,1)S(1)} %get-tuple-element.79), channel_id=1, source_target_pairs={{0,14},{1,15},{2,0},{3,1},{4,2},{5,3},{6,4},{7,5},{8,6},{9,7},{10,... | collective-permute-start | bytes 1179656 | tf_op jit(solution)/shard_map/ppermute | solution.py:32
  72.3 1.3 %collective-permute-done.18 = bf16[128,768]{1,0:T(8,128)(2,1)S(1)} collective-permute-done((bf16[128,768]{1,0:T(8,128)(2,1)S(1)}, bf16[128,768]{1,0:T(8,128)(2,1)S(1)}, u32[]{:S(2)}, u32[]{:S(2)}) %collective-permute-start.18) | collective-permute-done | bytes 196640 | tf_op jit(solution)/shard_map/ppermute | solution.py:32
  73.7 3.0 %collective-permute-start.35 = (bf16[256,512]{1,0:T(8,128)(2,1)S(1)}, bf16[256,512]{1,0:T(8,128)(2,1)S(1)}, u32[]{:S(2)}, u32[]{:S(2)}) collective-permute-start(bf16[256,512]{1,0:T(8,128)(2,1)S(1)} %fusion.19), channel_id=1, source_target_pairs={{0,128},{32,160},{64,192},{96,224},{128,0},{160,32},{192,64},{224,... | collective-permute-start | bytes 786440 | tf_op jit(solution)/shard_map/ppermute | solution.py:336
  76.7 1.8 %shard_map.156 = (bf16[128,2048]{1,0:T(8,128)(2,1)S(1)}, bf16[128,2048]{1,0:T(8,128)(2,1)S(1)}, bf16[128,2048]{1,0:T(8,128)(2,1)S(1)}, bf16[128,2048]{1,0:T(8,128)(2,1)S(1)}) custom-call(bf16[512,768]{1,0:T(8,128)(2,1)S(1)} %get-tuple-element.70.g_ref, bf16[256,768]{1,0:T(8,128)(2,1)S(1)} %convert_bitcast_fusion.refs_0_, ...), custom_call_target="tpu_custom_call" | custom-call | flops 1610612736 | bytes 6029312 | tf_op jit(solution)/shard_map/pallas_call | solution.py:168
  78.6 3.8 %collective-permute-start.20 = (bf16[128,2048]{1,0:T(8,128)(2,1)S(1)}, bf16[128,2048]{1,0:T(8,128)(2,1)S(1)}, u32[]{:S(2)}, u32[]{:S(2)}) collective-permute-start(bf16[128,2048]{1,0:T(8,128)(2,1)S(1)} %get-tuple-element.60), channel_id=1, source_target_pairs={{0,1},{1,0},{2,3},{3,2},{4,5},{5,4},{6,7},{7,6},{8,9},{9,8},{10,11... | collective-permute-start | bytes 1572872 | tf_op jit(solution)/shard_map/ppermute | solution.py:38
  82.4 1.7 %collective-permute-start.22 = (bf16[128,2048]{1,0:T(8,128)(2,1)S(1)}, bf16[128,2048]{1,0:T(8,128)(2,1)S(1)}, u32[]{:S(2)}, u32[]{:S(2)}) collective-permute-start(bf16[128,2048]{1,0:T(8,128)(2,1)S(1)} %get-tuple-element.62), channel_id=1, source_target_pairs={{0,17},{1,16},{2,19},{3,18},{4,21},{5,20},{6,23},{7,22},{8,25},{9,... | collective-permute-start | bytes 1572872 | tf_op jit(solution)/shard_map/ppermute | solution.py:38
  84.4 2.7 %collective-permute-start.32 = (bf16[256,768]{1,0:T(8,128)(2,1)S(1)}, bf16[256,768]{1,0:T(8,128)(2,1)S(1)}, u32[]{:S(2)}, u32[]{:S(2)}) collective-permute-start(bf16[256,768]{1,0:T(8,128)(2,1)S(1)} %get-tuple-element.84), channel_id=1, source_target_pairs={{0,14},{1,15},{2,0},{3,1},{4,2},{5,3},{6,4},{7,5},{8,6},{9,7},{10,... | collective-permute-start | bytes 1179656 | tf_op jit(solution)/shard_map/ppermute | solution.py:32
  87.0 1.2 %fusion.1 = (f32[1,256,512]{2,1,0:T(8,128)}, f32[1,256,512]{2,1,0:T(8,128)}) fusion(f32[1,256,512]{2,1,0:T(8,128)S(1)} %copy-done.6, f32[1,256,512]{2,1,0:T(8,128)S(1)} %copy-done.7, bf16[256,512]{1,0:T(8,128)(2,1)S(1)} %collective-permute-done.35, pred[]{:T(512)S(6)} %eq.32, bf16[256,512]{1,0:T(8,128)(2,1)S(1)} %collective-permute-done.34, ...), kind=kLoop, calls=%fused_computation.4 | loop fusion | flops 1703936 | bytes 3407873 | tf_op jit(solution)/shard_map/broadcast_in_dim | solution.py:340
  88.3 7.6 %collective-permute-done.21.refs_2_ = bf16[128,2048]{1,0:T(8,128)(2,1)S(1)} collective-permute-done((bf16[128,2048]{1,0:T(8,128)(2,1)S(1)}, bf16[128,2048]{1,0:T(8,128)(2,1)S(1)}, u32[]{:S(2)}, u32[]{:S(2)}) %collective-permute-start.21) | collective-permute-done | bytes 524320 | tf_op jit(solution)/shard_map/ppermute | solution.py:38
  95.8 11.4 %collective-permute-done.22.refs_3_ = bf16[128,2048]{1,0:T(8,128)(2,1)S(1)} collective-permute-done((bf16[128,2048]{1,0:T(8,128)(2,1)S(1)}, bf16[128,2048]{1,0:T(8,128)(2,1)S(1)}, u32[]{:S(2)}, u32[]{:S(2)}) %collective-permute-start.22) | collective-permute-done | bytes 524320 | tf_op jit(solution)/shard_map/ppermute | solution.py:38
  107.3 2.1 %shard_map.157 = bf16[128,8192]{1,0:T(8,128)(2,1)} custom-call(s32[5]{0:T(128)S(1)} %stack.60.base_ref, bf16[128,2048]{1,0:T(8,128)(2,1)S(1)} %get-tuple-element.59.refs_0_, bf16[128,2048]{1,0:T(8,128)(2,1)S(1)} %collective-permute-done.20.refs_1_, bf16[128,2048]{1,0:T(8,128)(2,1)S(1)} %collective-permute-done.21.refs_2_, ...), custom_call_target="tpu_custom_call" | custom-call | bytes 4194304 | tf_op jit(solution)/shard_map/pallas_call | solution.py:142
  109.4 2.2 %shard_map.163 = (f32[1,256,768]{2,1,0:T(8,128)}, f32[1,256,768]{2,1,0:T(8,128)}, f32[1,256,768]{2,1,0:T(8,128)}) custom-call(bf16[256,768]{1,0:T(8,128)(2,1)S(1)} %collective-permute-done.31.f_ref, bf16[256,768]{1,0:T(8,128)(2,1)S(1)} %collective-permute-done.32.b_ref, bf16[256,768]{1,0:T(8,128)(2,1)S(1)} %get-tuple-element.86.o_ref, ...), custom_call_target="tpu_custom_call" | custom-call | flops 3932160 | bytes 5898240 | tf_op jit(solution)/shard_map/pallas_call | solution.py:312
  (76 shorter events, 5.0 us)
Async XLA Ops:
  0.6 7.6 %collective-permute-start = (s32[128]{0:T(128)}, s32[128]{0:T(128)S(1)}, u32[]{:S(2)}, u32[]{:S(2)}) collective-permute-start(s32[128]{0:T(128)} %param.11), channel_id=1, source_target_pairs={{0,1},{1,0},{2,3},{3,2},{4,5},{5,4},{6,7},{7,6},{8,9},{9,8},{10,11... | collective-permute-start | bytes 1544 | tf_op jit(solution)/shard_map/ppermute | solution.py:38
  4.0 4.3 %collective-permute-start.2 = (s32[128]{0:T(128)}, s32[128]{0:T(128)S(1)}, u32[]{:S(2)}, u32[]{:S(2)}) collective-permute-start(s32[128]{0:T(128)} %param.11), channel_id=1, source_target_pairs={{0,17},{1,16},{2,19},{3,18},{4,21},{5,20},{6,23},{7,22},{8,25},{9,... | collective-permute-start | bytes 1544 | tf_op jit(solution)/shard_map/ppermute | solution.py:38
  4.0 4.3 %collective-permute-start.1 = (s32[128]{0:T(128)}, s32[128]{0:T(128)S(1)}, u32[]{:S(2)}, u32[]{:S(2)}) collective-permute-start(s32[128]{0:T(128)} %param.11), channel_id=1, source_target_pairs={{0,16},{1,17},{2,18},{3,19},{4,20},{5,21},{6,22},{7,23},{8,24},{9,... | collective-permute-start | bytes 1544 | tf_op jit(solution)/shard_map/ppermute | solution.py:38
  5.4 18.1 %collective-permute-start.12 = (bf16[128,768]{1,0:T(8,128)(2,1)}, bf16[128,768]{1,0:T(8,128)(2,1)S(1)}, u32[]{:S(2)}, u32[]{:S(2)}) collective-permute-start(bf16[128,768]{1,0:T(8,128)(2,1)} %cot.1), channel_id=1, source_target_pairs={{0,16},{1,17},{2,18},{3,19},{4,20},{5,21},{6,22},{7,23},{8,24},{9,... | collective-permute-start | bytes 589832 | tf_op jit(solution)/shard_map/ppermute | solution.py:38
  5.5 36.4 %copy-start.5 = (bf16[128,768]{1,0:T(8,128)(2,1)S(1)}, bf16[128,768]{1,0:T(8,128)(2,1)}, u32[]{:S(2)}) copy-start(bf16[128,768]{1,0:T(8,128)(2,1)} %cot.1) | copy-start | bytes 589828
  8.3 16.3 %collective-permute-start.6 = (bf16[256,768]{1,0:T(8,128)(2,1)S(1)}, bf16[256,768]{1,0:T(8,128)(2,1)S(1)}, u32[]{:S(2)}, u32[]{:S(2)}) collective-permute-start(bf16[256,768]{1,0:T(8,128)(2,1)S(1)} %convert_bitcast_fusion.refs_0_), channel_id=1, source_target_pairs={{0,2},{1,3},{2,4},{3,5},{4,6},{5,7},{6,8},{7,9},{8,10},{9,11},{10,... | collective-permute-start | bytes 1179656 | tf_op jit(solution)/shard_map/ppermute | solution.py:32
  9.4 15.2 %collective-permute-start.5 = (bf16[256,768]{1,0:T(8,128)(2,1)S(1)}, bf16[256,768]{1,0:T(8,128)(2,1)S(1)}, u32[]{:S(2)}, u32[]{:S(2)}) collective-permute-start(bf16[256,768]{1,0:T(8,128)(2,1)S(1)} %convert_bitcast_fusion.refs_0_), channel_id=1, source_target_pairs={{0,14},{1,15},{2,0},{3,1},{4,2},{5,3},{6,4},{7,5},{8,6},{9,7},{10,... | collective-permute-start | bytes 1179656 | tf_op jit(solution)/shard_map/ppermute | solution.py:32
  14.3 6.6 %collective-permute-start.4 = (s32[8,4]{0,1:T(4,128)S(1)}, s32[8,4]{0,1:T(4,128)S(1)}, u32[]{:S(2)}, u32[]{:S(2)}) collective-permute-start(s32[8,4]{0,1:T(4,128)S(1)} %broadcast_select_fusion), channel_id=1, source_target_pairs={{0,14},{1,15},{2,0},{3,1},{4,2},{5,3},{6,4},{7,5},{8,6},{9,7},{10,... | collective-permute-start | bytes 392 | tf_op jit(solution)/shard_map/ppermute | solution.py:32
  15.7 6.1 %collective-permute-start.3 = (s32[8,4]{0,1:T(4,128)S(1)}, s32[8,4]{0,1:T(4,128)S(1)}, u32[]{:S(2)}, u32[]{:S(2)}) collective-permute-start(s32[8,4]{0,1:T(4,128)S(1)} %broadcast_select_fusion), channel_id=1, source_target_pairs={{0,2},{1,3},{2,4},{3,5},{4,6},{5,7},{6,8},{7,9},{8,10},{9,11},{10,... | collective-permute-start | bytes 392 | tf_op jit(solution)/shard_map/ppermute | solution.py:32
  16.0 1.6 %copy-start.1 = (bf16[128,8192]{1,0:T(8,128)(2,1)S(1)}, bf16[128,8192]{1,0:T(8,128)(2,1)}, u32[]{:S(2)}) copy-start(bf16[128,8192]{1,0:T(8,128)(2,1)} %in_ref.1) | copy-start | bytes 6291460
  17.6 0.9 copy-start.4
  19.8 25.6 %copy-start.6 = (f32[1,256,512]{2,1,0:T(8,128)S(1)}, f32[1,256,512]{2,1,0:T(8,128)}, u32[]{:S(2)}) copy-start(f32[1,256,512]{2,1,0:T(8,128)} %param.19) | copy-start | bytes 1572868
  19.9 25.6 %copy-start.7 = (f32[1,256,512]{2,1,0:T(8,128)S(1)}, f32[1,256,512]{2,1,0:T(8,128)}, u32[]{:S(2)}) copy-start(f32[1,256,512]{2,1,0:T(8,128)} %param.18) | copy-start | bytes 1572868
  20.9 13.9 %collective-permute-start.10 = (bf16[128,768]{1,0:T(8,128)(2,1)S(1)}, bf16[128,768]{1,0:T(8,128)(2,1)S(1)}, u32[]{:S(2)}, u32[]{:S(2)}) collective-permute-start(bf16[128,768]{1,0:T(8,128)(2,1)S(1)} %get-tuple-element.53), channel_id=1, source_target_pairs={{0,16},{1,17},{2,18},{3,19},{4,20},{5,21},{6,22},{7,23},{8,24},{9,... | collective-permute-start | bytes 589832 | tf_op jit(solution)/shard_map/ppermute | solution.py:38
  21.9 15.2 %collective-permute-start.9 = (bf16[128,2816]{1,0:T(8,128)(2,1)S(1)}, bf16[128,2816]{1,0:T(8,128)(2,1)S(1)}, u32[]{:S(2)}, u32[]{:S(2)}) collective-permute-start(bf16[128,2816]{1,0:T(8,128)(2,1)S(1)} %get-tuple-element.50), channel_id=1, source_target_pairs={{0,1},{1,0},{2,3},{3,2},{4,5},{5,4},{6,7},{7,6},{8,9},{9,8},{10,11... | collective-permute-start | bytes 2162696 | tf_op jit(solution)/shard_map/ppermute | solution.py:38
  23.5 13.2 %collective-permute-start.11 = (bf16[128,768]{1,0:T(8,128)(2,1)S(1)}, bf16[128,768]{1,0:T(8,128)(2,1)S(1)}, u32[]{:S(2)}, u32[]{:S(2)}) collective-permute-start(bf16[128,768]{1,0:T(8,128)(2,1)S(1)} %get-tuple-element.54), channel_id=1, source_target_pairs={{0,17},{1,16},{2,19},{3,18},{4,21},{5,20},{6,23},{7,22},{8,25},{9,... | collective-permute-start | bytes 589832 | tf_op jit(solution)/shard_map/ppermute | solution.py:38
  24.6 5.9 %collective-permute-start.8 = (s32[8,4]{0,1:T(4,128)S(1)}, s32[8,4]{0,1:T(4,128)S(1)}, u32[]{:S(2)}, u32[]{:S(2)}) collective-permute-start(s32[8,4]{0,1:T(4,128)S(1)} %maximum_maximum_fusion.1), channel_id=1, source_target_pairs={{0,10},{1,11},{2,12},{3,13},{4,14},{5,15},{6,0},{7,1},{8,2},{9,3},... | collective-permute-start | bytes 392 | tf_op jit(solution)/shard_map/ppermute | solution.py:32
  28.3 5.4 %collective-permute-start.7 = (s32[8,4]{0,1:T(4,128)S(1)}, s32[8,4]{0,1:T(4,128)S(1)}, u32[]{:S(2)}, u32[]{:S(2)}) collective-permute-start(s32[8,4]{0,1:T(4,128)S(1)} %maximum_maximum_fusion.1), channel_id=1, source_target_pairs={{0,6},{1,7},{2,8},{3,9},{4,10},{5,11},{6,12},{7,13},{8,14},{9,15},... | collective-permute-start | bytes 392 | tf_op jit(solution)/shard_map/ppermute | solution.py:32
  30.5 11.4 %collective-permute-start.13 = (bf16[128,768]{1,0:T(8,128)(2,1)S(1)}, bf16[128,768]{1,0:T(8,128)(2,1)S(1)}, u32[]{:S(2)}, u32[]{:S(2)}) collective-permute-start(bf16[128,768]{1,0:T(8,128)(2,1)S(1)} %collective-permute-done.12.cot_2), channel_id=1, source_target_pairs={{0,1},{1,0},{2,3},{3,2},{4,5},{5,4},{6,7},{7,6},{8,9},{9,8},{10,11... | collective-permute-start | bytes 589832 | tf_op jit(solution)/shard_map/ppermute | solution.py:38
  33.7 9.9 %collective-permute-start.15 = (bf16[256,768]{1,0:T(8,128)(2,1)S(1)}, bf16[256,768]{1,0:T(8,128)(2,1)S(1)}, u32[]{:S(2)}, u32[]{:S(2)}) collective-permute-start(bf16[256,768]{1,0:T(8,128)(2,1)S(1)} %collective-permute-done.6.refs_2_), channel_id=1, source_target_pairs={{0,2},{1,3},{2,4},{3,5},{4,6},{5,7},{6,8},{7,9},{8,10},{9,11},{10,... | collective-permute-start | bytes 1179656 | tf_op jit(solution)/shard_map/ppermute | solution.py:32
  34.8 11.9 %collective-permute-start.14 = (bf16[256,768]{1,0:T(8,128)(2,1)S(1)}, bf16[256,768]{1,0:T(8,128)(2,1)S(1)}, u32[]{:S(2)}, u32[]{:S(2)}) collective-permute-start(bf16[256,768]{1,0:T(8,128)(2,1)S(1)} %collective-permute-done.5.refs_1_), channel_id=1, source_target_pairs={{0,14},{1,15},{2,0},{3,1},{4,2},{5,3},{6,4},{7,5},{8,6},{9,7},{10,... | collective-permute-start | bytes 1179656 | tf_op jit(solution)/shard_map/ppermute | solution.py:32
  36.8 15.0 %collective-permute-start.27 = (bf16[128,1280]{1,0:T(8,128)(2,1)S(1)}, bf16[128,1280]{1,0:T(8,128)(2,1)S(1)}, u32[]{:S(2)}, u32[]{:S(2)}) collective-permute-start(bf16[128,1280]{1,0:T(8,128)(2,1)S(1)} %get-tuple-element.72), channel_id=1, source_target_pairs={{0,16},{1,17},{2,18},{3,19},{4,20},{5,21},{6,22},{7,23},{8,24},{9,... | collective-permute-start | bytes 983048 | tf_op jit(solution)/shard_map/ppermute | solution.py:38
  37.0 16.5 %collective-permute-start.28 = (bf16[128,1280]{1,0:T(8,128)(2,1)S(1)}, bf16[128,1280]{1,0:T(8,128)(2,1)S(1)}, u32[]{:S(2)}, u32[]{:S(2)}) collective-permute-start(bf16[128,1280]{1,0:T(8,128)(2,1)S(1)} %get-tuple-element.74), channel_id=1, source_target_pairs={{0,17},{1,16},{2,19},{3,18},{4,21},{5,20},{6,23},{7,22},{8,25},{9,... | collective-permute-start | bytes 983048 | tf_op jit(solution)/shard_map/ppermute | solution.py:38
  42.7 7.3 %collective-permute-start.23 = (bf16[128,768]{1,0:T(8,128)(2,1)S(1)}, bf16[128,768]{1,0:T(8,128)(2,1)S(1)}, u32[]{:S(2)}, u32[]{:S(2)}) collective-permute-start(bf16[128,768]{1,0:T(8,128)(2,1)S(1)} %get-tuple-element.63), channel_id=1, source_target_pairs={{0,2},{1,3},{2,4},{3,5},{4,6},{5,7},{6,8},{7,9},{8,10},{9,11},{10,... | collective-permute-start | bytes 589832 | tf_op jit(solution)/shard_map/ppermute | solution.py:32
  43.6 8.0 %collective-permute-start.24 = (bf16[128,768]{1,0:T(8,128)(2,1)S(1)}, bf16[128,768]{1,0:T(8,128)(2,1)S(1)}, u32[]{:S(2)}, u32[]{:S(2)}) collective-permute-start(bf16[128,768]{1,0:T(8,128)(2,1)S(1)} %get-tuple-element.64), channel_id=1, source_target_pairs={{0,14},{1,15},{2,0},{3,1},{4,2},{5,3},{6,4},{7,5},{8,6},{9,7},{10,... | collective-permute-start | bytes 589832 | tf_op jit(solution)/shard_map/ppermute | solution.py:32
  46.7 11.9 %collective-permute-start.17 = (bf16[256,768]{1,0:T(8,128)(2,1)S(1)}, bf16[256,768]{1,0:T(8,128)(2,1)S(1)}, u32[]{:S(2)}, u32[]{:S(2)}) collective-permute-start(bf16[256,768]{1,0:T(8,128)(2,1)S(1)} %collective-permute-done.15.refs_4_), channel_id=1, source_target_pairs={{0,2},{1,3},{2,4},{3,5},{4,6},{5,7},{6,8},{7,9},{8,10},{9,11},{10,... | collective-permute-start | bytes 1179656 | tf_op jit(solution)/shard_map/ppermute | solution.py:32
  50.0 10.7 %collective-permute-start.16 = (bf16[256,768]{1,0:T(8,128)(2,1)S(1)}, bf16[256,768]{1,0:T(8,128)(2,1)S(1)}, u32[]{:S(2)}, u32[]{:S(2)}) collective-permute-start(bf16[256,768]{1,0:T(8,128)(2,1)S(1)} %collective-permute-done.14.refs_3_), channel_id=1, source_target_pairs={{0,14},{1,15},{2,0},{3,1},{4,2},{5,3},{6,4},{7,5},{8,6},{9,7},{10,... | collective-permute-start | bytes 1179656 | tf_op jit(solution)/shard_map/ppermute | solution.py:32
  54.8 9.3 %collective-permute-start.33 = (bf16[256,512]{1,0:T(8,128)(2,1)S(1)}, bf16[256,512]{1,0:T(8,128)(2,1)S(1)}, u32[]{:S(2)}, u32[]{:S(2)}) collective-permute-start(bf16[256,512]{1,0:T(8,128)(2,1)S(1)} %convert_element_type.46), channel_id=1, source_target_pairs={{0,32},{32,0},{64,96},{96,64},{128,160},{160,128},{192,224},{224,1... | collective-permute-start | bytes 786440 | tf_op jit(solution)/shard_map/ppermute | solution.py:336
  57.0 12.1 %collective-permute-start.26 = (bf16[256,768]{1,0:T(8,128)(2,1)S(1)}, bf16[256,768]{1,0:T(8,128)(2,1)S(1)}, u32[]{:S(2)}, u32[]{:S(2)}) collective-permute-start(bf16[256,768]{1,0:T(8,128)(2,1)S(1)} %get-tuple-element.69), channel_id=1, source_target_pairs={{0,14},{1,15},{2,0},{3,1},{4,2},{5,3},{6,4},{7,5},{8,6},{9,7},{10,... | collective-permute-start | bytes 1179656 | tf_op jit(solution)/shard_map/ppermute | solution.py:32
  58.5 10.8 %collective-permute-start.25 = (bf16[256,768]{1,0:T(8,128)(2,1)S(1)}, bf16[256,768]{1,0:T(8,128)(2,1)S(1)}, u32[]{:S(2)}, u32[]{:S(2)}) collective-permute-start(bf16[256,768]{1,0:T(8,128)(2,1)S(1)} %get-tuple-element.68), channel_id=1, source_target_pairs={{0,2},{1,3},{2,4},{3,5},{4,6},{5,7},{6,8},{7,9},{8,10},{9,11},{10,... | collective-permute-start | bytes 1179656 | tf_op jit(solution)/shard_map/ppermute | solution.py:32
  58.6 15.0 %collective-permute-start.18 = (bf16[128,768]{1,0:T(8,128)(2,1)S(1)}, bf16[128,768]{1,0:T(8,128)(2,1)S(1)}, u32[]{:S(2)}, u32[]{:S(2)}) collective-permute-start(bf16[128,768]{1,0:T(8,128)(2,1)S(1)} %slice.8), channel_id=1, source_target_pairs={{0,2},{1,3},{2,4},{3,5},{4,6},{5,7},{6,8},{7,9},{8,10},{9,11},{10,... | collective-permute-start | bytes 589832 | tf_op jit(solution)/shard_map/ppermute | solution.py:32
  60.7 12.9 %collective-permute-start.19 = (bf16[128,768]{1,0:T(8,128)(2,1)S(1)}, bf16[128,768]{1,0:T(8,128)(2,1)S(1)}, u32[]{:S(2)}, u32[]{:S(2)}) collective-permute-start(bf16[128,768]{1,0:T(8,128)(2,1)S(1)} %slice.9), channel_id=1, source_target_pairs={{0,14},{1,15},{2,0},{3,1},{4,2},{5,3},{6,4},{7,5},{8,6},{9,7},{10,... | collective-permute-start | bytes 589832 | tf_op jit(solution)/shard_map/ppermute | solution.py:32
  64.1 9.5 %collective-permute-start.34 = (bf16[256,512]{1,0:T(8,128)(2,1)S(1)}, bf16[256,512]{1,0:T(8,128)(2,1)S(1)}, u32[]{:S(2)}, u32[]{:S(2)}) collective-permute-start(bf16[256,512]{1,0:T(8,128)(2,1)S(1)} %fusion.7), channel_id=1, source_target_pairs={{0,64},{32,96},{64,0},{96,32},{128,192},{160,224},{192,128},{224,1... | collective-permute-start | bytes 786440 | tf_op jit(solution)/shard_map/ppermute | solution.py:336
  69.5 12.8 %collective-permute-start.29 = (bf16[256,768]{1,0:T(8,128)(2,1)S(1)}, bf16[256,768]{1,0:T(8,128)(2,1)S(1)}, u32[]{:S(2)}, u32[]{:S(2)}) collective-permute-start(bf16[256,768]{1,0:T(8,128)(2,1)S(1)} %get-tuple-element.78), channel_id=1, source_target_pairs={{0,2},{1,3},{2,4},{3,5},{4,6},{5,7},{6,8},{7,9},{8,10},{9,11},{10,... | collective-permute-start | bytes 1179656 | tf_op jit(solution)/shard_map/ppermute | solution.py:32
  69.6 14.5 %collective-permute-start.30 = (bf16[256,768]{1,0:T(8,128)(2,1)S(1)}, bf16[256,768]{1,0:T(8,128)(2,1)S(1)}, u32[]{:S(2)}, u32[]{:S(2)}) collective-permute-start(bf16[256,768]{1,0:T(8,128)(2,1)S(1)} %get-tuple-element.79), channel_id=1, source_target_pairs={{0,14},{1,15},{2,0},{3,1},{4,2},{5,3},{6,4},{7,5},{8,6},{9,7},{10,... | collective-permute-start | bytes 1179656 | tf_op jit(solution)/shard_map/ppermute | solution.py:32
  73.7 10.6 %collective-permute-start.35 = (bf16[256,512]{1,0:T(8,128)(2,1)S(1)}, bf16[256,512]{1,0:T(8,128)(2,1)S(1)}, u32[]{:S(2)}, u32[]{:S(2)}) collective-permute-start(bf16[256,512]{1,0:T(8,128)(2,1)S(1)} %fusion.19), channel_id=1, source_target_pairs={{0,128},{32,160},{64,192},{96,224},{128,0},{160,32},{192,64},{224,... | collective-permute-start | bytes 786440 | tf_op jit(solution)/shard_map/ppermute | solution.py:336
  78.6 9.7 %collective-permute-start.20 = (bf16[128,2048]{1,0:T(8,128)(2,1)S(1)}, bf16[128,2048]{1,0:T(8,128)(2,1)S(1)}, u32[]{:S(2)}, u32[]{:S(2)}) collective-permute-start(bf16[128,2048]{1,0:T(8,128)(2,1)S(1)} %get-tuple-element.60), channel_id=1, source_target_pairs={{0,1},{1,0},{2,3},{3,2},{4,5},{5,4},{6,7},{7,6},{8,9},{9,8},{10,11... | collective-permute-start | bytes 1572872 | tf_op jit(solution)/shard_map/ppermute | solution.py:38
  82.4 13.5 %collective-permute-start.21 = (bf16[128,2048]{1,0:T(8,128)(2,1)S(1)}, bf16[128,2048]{1,0:T(8,128)(2,1)S(1)}, u32[]{:S(2)}, u32[]{:S(2)}) collective-permute-start(bf16[128,2048]{1,0:T(8,128)(2,1)S(1)} %get-tuple-element.61), channel_id=1, source_target_pairs={{0,16},{1,17},{2,18},{3,19},{4,20},{5,21},{6,22},{7,23},{8,24},{9,... | collective-permute-start | bytes 1572872 | tf_op jit(solution)/shard_map/ppermute | solution.py:38
  82.4 24.9 %collective-permute-start.22 = (bf16[128,2048]{1,0:T(8,128)(2,1)S(1)}, bf16[128,2048]{1,0:T(8,128)(2,1)S(1)}, u32[]{:S(2)}, u32[]{:S(2)}) collective-permute-start(bf16[128,2048]{1,0:T(8,128)(2,1)S(1)} %get-tuple-element.62), channel_id=1, source_target_pairs={{0,17},{1,16},{2,19},{3,18},{4,21},{5,20},{6,23},{7,22},{8,25},{9,... | collective-permute-start | bytes 1572872 | tf_op jit(solution)/shard_map/ppermute | solution.py:38
  84.3 25.1 %collective-permute-start.31 = (bf16[256,768]{1,0:T(8,128)(2,1)S(1)}, bf16[256,768]{1,0:T(8,128)(2,1)S(1)}, u32[]{:S(2)}, u32[]{:S(2)}) collective-permute-start(bf16[256,768]{1,0:T(8,128)(2,1)S(1)} %get-tuple-element.83), channel_id=1, source_target_pairs={{0,2},{1,3},{2,4},{3,5},{4,6},{5,7},{6,8},{7,9},{8,10},{9,11},{10,... | collective-permute-start | bytes 1179656 | tf_op jit(solution)/shard_map/ppermute | solution.py:32
  84.4 25.0 %collective-permute-start.32 = (bf16[256,768]{1,0:T(8,128)(2,1)S(1)}, bf16[256,768]{1,0:T(8,128)(2,1)S(1)}, u32[]{:S(2)}, u32[]{:S(2)}) collective-permute-start(bf16[256,768]{1,0:T(8,128)(2,1)S(1)} %get-tuple-element.84), channel_id=1, source_target_pairs={{0,14},{1,15},{2,0},{3,1},{4,2},{5,3},{6,4},{7,5},{8,6},{9,7},{10,... | collective-permute-start | bytes 1179656 | tf_op jit(solution)/shard_map/ppermute | solution.py:32
  88.3 21.1 %copy-start = (f32[1,256,768]{2,1,0:T(8,128)S(1)}, f32[1,256,768]{2,1,0:T(8,128)}, u32[]{:S(2)}) copy-start(f32[1,256,768]{2,1,0:T(8,128)} %w_ref.1) | copy-start | bytes 2359300
  88.3 21.2 %copy-start.2 = (f32[1,256,768]{2,1,0:T(8,128)S(1)}, f32[1,256,768]{2,1,0:T(8,128)}, u32[]{:S(2)}) copy-start(f32[1,256,768]{2,1,0:T(8,128)} %m_ref.1) | copy-start | bytes 2359300
  88.3 21.2 %copy-start.3 = (f32[1,256,768]{2,1,0:T(8,128)S(1)}, f32[1,256,768]{2,1,0:T(8,128)}, u32[]{:S(2)}) copy-start(f32[1,256,768]{2,1,0:T(8,128)} %v_ref.1) | copy-start | bytes 2359300

commit v3 on v2

--- a/solution.py
+++ b/solution.py
@@ -320,7 +320,7 @@
     )(forward, backward, own, key_weight, adam_m, adam_v)
 
 
-def outer_sync(frag_local, frag_global, outer_mom, owner, fragment, after, before_swap):
+def outer_sync(frag_local, frag_global, outer_mom, owner, fragment, after, before_swap, before_last):
     replica_count = lax.axis_size("replica")
     is_owner = tie(lax.axis_index("replica") == owner[0], after)
     gain = outer_lr * (1.0 + outer_momentum)
@@ -332,6 +332,7 @@
     )
     synced = tie(synced, before_swap)
     for flip in (1, 2, 4):
+        synced = tie(synced, before_last) if flip == 4 else synced
         pairs = [(r, r ^ flip) for r in range(replica_count)]
         arrived = lax.ppermute(synced.astype(jnp.bfloat16), "replica", pairs)
         synced = synced + arrived.astype(jnp.float32)
@@ -367,7 +368,7 @@
     across = with_peer(key_cotangent, 2)
 
     half = width // 2
-    held = {0: tie(key_weight[0].astype(jnp.bfloat16), *ids[1:])}
+    held = {0: key_weight[0].astype(jnp.bfloat16)}
     held[-1], held[1] = along_z(held[0], 1), along_z(held[0], -1)
 
     own, *packed = pack_columns(inputs, key_cotangent, tie(bases, *ids[1:]), width)
@@ -408,9 +409,11 @@
     forward, backward = add_pair(forward, backward, tie(up, held[3], held[-3]), down)
     forward, backward = along_z(forward, 1), along_z(backward, -1)
 
-    synced, new_outer_mom = outer_sync(frag_local, frag_global, outer_mom, owner, fragment, newest, term)
     held[4] = jnp.concatenate(opposite)
     back = back_products(grads, [held[ahead] for ahead in RING])
+    synced, new_outer_mom = outer_sync(
+        frag_local, frag_global, outer_mom, owner, fragment, newest, term, back[0]
+    )
     parts = [back[0]] + [with_peer(back[p], p) for p in (1, 2, 3)]
 
     forward, backward = add_pair(forward, backward, tie(up_1, back[0]), down_1)

time: 112 us -> 109 us (0.973)
  waiting for transfers between devices: 39.2 us -> 37.6 us
  starting transfers between devices: 50.5 us -> 49.3 us
    ppermute x20, starting transfers between devices: 25.1 us -> 21.7 us  [along_z(): return lax.ppermute(value, 'fsdp', pairs)]
    ppermute x13, starting transfers between devices: 18.7 us -> 20.8 us  [with_peer(): return lax.ppermute(value, 'fsdp', pairs)]
    ppermute x20, waiting for transfers between devices: 15.9 us -> 14 us  [along_z(): return lax.ppermute(value, 'fsdp', pairs)]
  transfers between devices with their start and end apart: 36 -> 36, of which waited for: 14 -> 12; matrix products, arithmetic and copies ran while one was open for 6% -> 6% of each run, Pallas kernels for 7% -> 8%
where the time goes in v3:
time: 109 us
  starting transfers between devices  49.3 us (45%)
  waiting for transfers between devices  37.6 us (34%)
  Pallas kernels  10.5 us (10%)
  other arithmetic  6.4 us (6%)
  local copies, waits for them, and re-layouts  2.66 us (2%)
  between operations  2.31 us (2%)
    ppermute x20, starting transfers between devices, along_z(): return lax.ppermute(value, 'fsdp', pairs)  21.7 us
    ppermute x13, waiting for transfers between devices, with_peer(): return lax.ppermute(value, 'fsdp', pairs)  21.2 us
    ppermute x13, starting transfers between devices, with_peer(): return lax.ppermute(value, 'fsdp', pairs)  20.8 us
    ppermute x20, waiting for transfers between devices, along_z(): return lax.ppermute(value, 'fsdp', pairs)  14 us
    ppermute x3, starting transfers between devices, outer_sync(): arrived = lax.ppermute(synced.astype(jnp.bfloat16), 'replica', pairs)  6.92 us
    unnamed x16, local copies, waits for them, and re-layouts  2.54 us
    ppermute x3, waiting for transfers between devices, outer_sync(): arrived = lax.ppermute(synced.astype(jnp.bfloat16), 'replica', pairs)  2.48 us
  transfers between devices with their start and end apart: 36, of which 12 were waited for; matrix products, arithmetic and copies ran while one was open for 6% of the time, Pallas kernels for 8%

profile of v3, /device:TPU:1, one launch (start us, length us, event | category | flops | bytes accessed | tf_op | source)
XLA Modules:
  0.0 108.8 jit_solution(1885991488743675147)
XLA Ops:
  0.6 3.3 %collective-permute-start = (s32[128]{0:T(128)}, s32[128]{0:T(128)S(1)}, u32[]{:S(2)}, u32[]{:S(2)}) collective-permute-start(s32[128]{0:T(128)} %param.11), channel_id=1, source_target_pairs={{0,1},{1,0},{2,3},{3,2},{4,5},{5,4},{6,7},{7,6},{8,9},{9,8},{10,11... | collective-permute-start | bytes 1544 | tf_op jit(solution)/shard_map/ppermute | solution.py:38
  4.0 1.5 %collective-permute-start.1 = (s32[128]{0:T(128)}, s32[128]{0:T(128)S(1)}, u32[]{:S(2)}, u32[]{:S(2)}) collective-permute-start(s32[128]{0:T(128)} %param.11), channel_id=1, source_target_pairs={{0,16},{1,17},{2,18},{3,19},{4,20},{5,21},{6,22},{7,23},{8,24},{9,... | collective-permute-start | bytes 1544 | tf_op jit(solution)/shard_map/ppermute | solution.py:38
  5.4 1.2 %convert_bitcast_fusion.refs_0_ = bf16[256,768]{1,0:T(8,128)(2,1)S(1)} fusion(f32[1,256,768]{2,1,0:T(8,128)} %w_ref.1), kind=kLoop, calls=%fused_computation.16 | loop fusion | flops 196608 | bytes 1179648 | tf_op jit(solution)/shard_map/convert_element_type | solution.py:371
  6.7 3.9 %collective-permute-start.5 = (bf16[256,768]{1,0:T(8,128)(2,1)S(1)}, bf16[256,768]{1,0:T(8,128)(2,1)S(1)}, u32[]{:S(2)}, u32[]{:S(2)}) collective-permute-start(bf16[256,768]{1,0:T(8,128)(2,1)S(1)} %convert_bitcast_fusion.refs_0_), channel_id=1, source_target_pairs={{0,14},{1,15},{2,0},{3,1},{4,2},{5,3},{6,4},{7,5},{8,6},{9,7},{10,... | collective-permute-start | bytes 1179656 | tf_op jit(solution)/shard_map/ppermute | solution.py:32
  12.2 1.2 %collective-permute-start.12 = (bf16[128,768]{1,0:T(8,128)(2,1)}, bf16[128,768]{1,0:T(8,128)(2,1)S(1)}, u32[]{:S(2)}, u32[]{:S(2)}) collective-permute-start(bf16[128,768]{1,0:T(8,128)(2,1)} %cot.1), channel_id=1, source_target_pairs={{0,16},{1,17},{2,18},{3,19},{4,20},{5,21},{6,22},{7,23},{8,24},{9,... | collective-permute-start | bytes 589832 | tf_op jit(solution)/shard_map/ppermute | solution.py:38
  13.4 0.8 fusion.19
  14.3 1.4 %collective-permute-start.4 = (s32[8,4]{0,1:T(4,128)S(1)}, s32[8,4]{0,1:T(4,128)S(1)}, u32[]{:S(2)}, u32[]{:S(2)}) collective-permute-start(s32[8,4]{0,1:T(4,128)S(1)} %broadcast_select_fusion), channel_id=1, source_target_pairs={{0,14},{1,15},{2,0},{3,1},{4,2},{5,3},{6,4},{7,5},{8,6},{9,7},{10,... | collective-permute-start | bytes 392 | tf_op jit(solution)/shard_map/ppermute | solution.py:32
  16.0 1.6 %copy-done.1 = bf16[128,8192]{1,0:T(8,128)(2,1)S(1)} copy-done((bf16[128,8192]{1,0:T(8,128)(2,1)S(1)}, bf16[128,8192]{1,0:T(8,128)(2,1)}, u32[]{:S(2)}) %copy-start.1) | copy-done | bytes 2097176
  17.6 0.9 copy-done.4
  18.5 1.3 %shard_map.154 = (bf16[128,2048]{1,0:T(8,128)(2,1)S(1)}, bf16[128,2816]{1,0:T(8,128)(2,1)S(1)}, bf16[128,768]{1,0:T(8,128)(2,1)S(1)}, bf16[128,768]{1,0:T(8,128)...) custom-call(s32[5]{0:T(128)S(1)} %stack.60.base_ref, bf16[128,8192]{1,0:T(8,128)(2,1)S(1)} %copy-done.1, ...), custom_call_target="tpu_custom_call" | custom-call | bytes 4194304 | tf_op jit(solution)/shard_map/pallas_call | solution.py:111
  20.2 2.1 %collective-permute-start.9 = (bf16[128,2816]{1,0:T(8,128)(2,1)S(1)}, bf16[128,2816]{1,0:T(8,128)(2,1)S(1)}, u32[]{:S(2)}, u32[]{:S(2)}) collective-permute-start(bf16[128,2816]{1,0:T(8,128)(2,1)S(1)} %get-tuple-element.50), channel_id=1, source_target_pairs={{0,1},{1,0},{2,3},{3,2},{4,5},{5,4},{6,7},{7,6},{8,9},{9,8},{10,11... | collective-permute-start | bytes 2162696 | tf_op jit(solution)/shard_map/ppermute | solution.py:38
  22.4 1.1 %collective-permute-start.11 = (bf16[128,768]{1,0:T(8,128)(2,1)S(1)}, bf16[128,768]{1,0:T(8,128)(2,1)S(1)}, u32[]{:S(2)}, u32[]{:S(2)}) collective-permute-start(bf16[128,768]{1,0:T(8,128)(2,1)S(1)} %get-tuple-element.53), channel_id=1, source_target_pairs={{0,17},{1,16},{2,19},{3,18},{4,21},{5,20},{6,23},{7,22},{8,25},{9,... | collective-permute-start | bytes 589832 | tf_op jit(solution)/shard_map/ppermute | solution.py:38
  23.5 2.7 %collective-permute-start.8 = (s32[8,4]{0,1:T(4,128)S(1)}, s32[8,4]{0,1:T(4,128)S(1)}, u32[]{:S(2)}, u32[]{:S(2)}) collective-permute-start(s32[8,4]{0,1:T(4,128)S(1)} %maximum_maximum_fusion.1), channel_id=1, source_target_pairs={{0,10},{1,11},{2,12},{3,13},{4,14},{5,15},{6,0},{7,1},{8,2},{9,3},... | collective-permute-start | bytes 392 | tf_op jit(solution)/shard_map/ppermute | solution.py:32
  26.3 0.5 collective-permute-start.7
  26.8 1.0 collective-permute-done.8
  27.8 1.7 %collective-permute-start.13 = (bf16[128,768]{1,0:T(8,128)(2,1)S(1)}, bf16[128,768]{1,0:T(8,128)(2,1)S(1)}, u32[]{:S(2)}, u32[]{:S(2)}) collective-permute-start(bf16[128,768]{1,0:T(8,128)(2,1)S(1)} %collective-permute-done.12.cot_2), channel_id=1, source_target_pairs={{0,1},{1,0},{2,3},{3,2},{4,5},{5,4},{6,7},{7,6},{8,9},{9,8},{10,11... | collective-permute-start | bytes 589832 | tf_op jit(solution)/shard_map/ppermute | solution.py:38
  29.4 2.3 %collective-permute-done.7 = s32[8,4]{0,1:T(4,128)S(1)} collective-permute-done((s32[8,4]{0,1:T(4,128)S(1)}, s32[8,4]{0,1:T(4,128)S(1)}, u32[]{:S(2)}, u32[]{:S(2)}) %collective-permute-start.7) | collective-permute-done | bytes 160 | tf_op jit(solution)/shard_map/ppermute | solution.py:32
  31.7 0.5 collective-permute-start.15
  32.6 2.2 %collective-permute-start.14 = (bf16[256,768]{1,0:T(8,128)(2,1)S(1)}, bf16[256,768]{1,0:T(8,128)(2,1)S(1)}, u32[]{:S(2)}, u32[]{:S(2)}) collective-permute-start(bf16[256,768]{1,0:T(8,128)(2,1)S(1)} %collective-permute-done.5.refs_1_), channel_id=1, source_target_pairs={{0,14},{1,15},{2,0},{3,1},{4,2},{5,3},{6,4},{7,5},{8,6},{9,7},{10,... | collective-permute-start | bytes 1179656 | tf_op jit(solution)/shard_map/ppermute | solution.py:32
  35.2 3.7 %collective-permute-start.28 = (bf16[128,1280]{1,0:T(8,128)(2,1)S(1)}, bf16[128,1280]{1,0:T(8,128)(2,1)S(1)}, u32[]{:S(2)}, u32[]{:S(2)}) collective-permute-start(bf16[128,1280]{1,0:T(8,128)(2,1)S(1)} %get-tuple-element.73), channel_id=1, source_target_pairs={{0,17},{1,16},{2,19},{3,18},{4,21},{5,20},{6,23},{7,22},{8,25},{9,... | collective-permute-start | bytes 983048 | tf_op jit(solution)/shard_map/ppermute | solution.py:38
  38.9 1.0 fusion.9
  39.9 0.8 shard_map.155
  40.8 0.9 collective-permute-done.15.refs_4_
  41.6 1.8 %collective-permute-start.24 = (bf16[128,768]{1,0:T(8,128)(2,1)S(1)}, bf16[128,768]{1,0:T(8,128)(2,1)S(1)}, u32[]{:S(2)}, u32[]{:S(2)}) collective-permute-start(bf16[128,768]{1,0:T(8,128)(2,1)S(1)} %get-tuple-element.63), channel_id=1, source_target_pairs={{0,14},{1,15},{2,0},{3,1},{4,2},{5,3},{6,4},{7,5},{8,6},{9,7},{10,... | collective-permute-start | bytes 589832 | tf_op jit(solution)/shard_map/ppermute | solution.py:32
  43.4 1.2 %fusion.4 = f32[256,512]{1,0:T(8,128)S(1)} fusion(f32[1,256,512]{2,1,0:T(8,128)S(1)} %copy-done.7, f32[1,3,256,512]{3,2,1,0:T(8,128)} %param.17, s32[]{:T(128)S(6)} %select_n.84, f32[1,256,512]{2,1,0:T(8,128)S(1)} %copy-done.6, pred[]{:T(512)S(6)} %eq.32), kind=kLoop, calls=%fused_computation.9 | loop fusion | flops 786432 | bytes 2097157 | tf_op jit(solution)/shard_map/add | solution.py:330
  44.8 3.3 %collective-permute-done.23.f_ref = bf16[128,768]{1,0:T(8,128)(2,1)S(1)} collective-permute-done((bf16[128,768]{1,0:T(8,128)(2,1)S(1)}, bf16[128,768]{1,0:T(8,128)(2,1)S(1)}, u32[]{:S(2)}, u32[]{:S(2)}) %collective-permute-start.23) | collective-permute-done | bytes 196640 | tf_op jit(solution)/shard_map/ppermute | solution.py:32
  48.1 0.6 shard_map.158
  48.9 2.4 %collective-permute-done.28.refs_3_ = bf16[128,1280]{1,0:T(8,128)(2,1)S(1)} collective-permute-done((bf16[128,1280]{1,0:T(8,128)(2,1)S(1)}, bf16[128,1280]{1,0:T(8,128)(2,1)S(1)}, u32[]{:S(2)}, u32[]{:S(2)}) %collective-permute-start.28) | collective-permute-done | bytes 327712 | tf_op jit(solution)/shard_map/ppermute | solution.py:38
  51.2 1.2 %shard_map.160 = (bf16[256,768]{1,0:T(8,128)(2,1)S(1)}, bf16[256,768]{1,0:T(8,128)(2,1)S(1)}, bf16[256,768]{1,0:T(8,128)(2,1)S(1)}, bf16[256,768]{1,0:T(8,128)(2,1)S(1)}, bf16[256,768]{1,0:T(8,128)(2,1)S(1)}) custom-call(bf16[512,768]{1,0:T(8,128)(2,1)S(1)} %get-tuple-element.69.g_ref, bf16[128,2048]{1,0:T(8,128)(2,1)S(1)} %get-tuple-element.56.own.refs_0_, ...), custom_call_target="tpu_custom_call" | custom-call | flops 1006632960 | bytes 4063232 | tf_op jit(solution)/shard_map/pallas_call | solution.py:224
  52.5 2.5 %collective-permute-start.33 = (bf16[256,512]{1,0:T(8,128)(2,1)S(1)}, bf16[256,512]{1,0:T(8,128)(2,1)S(1)}, u32[]{:S(2)}, u32[]{:S(2)}) collective-permute-start(bf16[256,512]{1,0:T(8,128)(2,1)S(1)} %convert_element_type.45), channel_id=1, source_target_pairs={{0,32},{32,0},{64,96},{96,64},{128,160},{160,128},{192,224},{224,1... | collective-permute-start | bytes 786440 | tf_op jit(solution)/shard_map/ppermute | solution.py:337
  55.0 1.0 collective-permute-start.26
  57.0 1.6 %collective-permute-done.16.refs_5_ = bf16[256,768]{1,0:T(8,128)(2,1)S(1)} collective-permute-done((bf16[256,768]{1,0:T(8,128)(2,1)S(1)}, bf16[256,768]{1,0:T(8,128)(2,1)S(1)}, u32[]{:S(2)}, u32[]{:S(2)}) %collective-permute-start.16) | collective-permute-done | bytes 393248 | tf_op jit(solution)/shard_map/ppermute | solution.py:32
  58.6 0.8 collective-permute-start.19
  59.4 2.5 %collective-permute-done.33 = bf16[256,512]{1,0:T(8,128)(2,1)S(1)} collective-permute-done((bf16[256,512]{1,0:T(8,128)(2,1)S(1)}, bf16[256,512]{1,0:T(8,128)(2,1)S(1)}, u32[]{:S(2)}, u32[]{:S(2)}) %collective-permute-start.33) | collective-permute-done | bytes 262176 | tf_op jit(solution)/shard_map/ppermute | solution.py:337
  61.9 1.4 %collective-permute-start.34 = (bf16[256,512]{1,0:T(8,128)(2,1)S(1)}, bf16[256,512]{1,0:T(8,128)(2,1)S(1)}, u32[]{:S(2)}, u32[]{:S(2)}) collective-permute-start(bf16[256,512]{1,0:T(8,128)(2,1)S(1)} %fusion.7), channel_id=1, source_target_pairs={{0,64},{32,96},{64,0},{96,32},{128,192},{160,224},{192,128},{224,1... | collective-permute-start | bytes 786440 | tf_op jit(solution)/shard_map/ppermute | solution.py:337
  63.3 3.7 %collective-permute-done.26.b_ref = bf16[256,768]{1,0:T(8,128)(2,1)S(1)} collective-permute-done((bf16[256,768]{1,0:T(8,128)(2,1)S(1)}, bf16[256,768]{1,0:T(8,128)(2,1)S(1)}, u32[]{:S(2)}, u32[]{:S(2)}) %collective-permute-start.26) | collective-permute-done | bytes 393248 | tf_op jit(solution)/shard_map/ppermute | solution.py:32
  67.2 2.7 %collective-permute-start.30 = (bf16[256,768]{1,0:T(8,128)(2,1)S(1)}, bf16[256,768]{1,0:T(8,128)(2,1)S(1)}, u32[]{:S(2)}, u32[]{:S(2)}) collective-permute-start(bf16[256,768]{1,0:T(8,128)(2,1)S(1)} %get-tuple-element.78), channel_id=1, source_target_pairs={{0,14},{1,15},{2,0},{3,1},{4,2},{5,3},{6,4},{7,5},{8,6},{9,7},{10,... | collective-permute-start | bytes 1179656 | tf_op jit(solution)/shard_map/ppermute | solution.py:32
  69.9 1.1 %collective-permute-done.18 = bf16[128,768]{1,0:T(8,128)(2,1)S(1)} collective-permute-done((bf16[128,768]{1,0:T(8,128)(2,1)S(1)}, bf16[128,768]{1,0:T(8,128)(2,1)S(1)}, u32[]{:S(2)}, u32[]{:S(2)}) %collective-permute-start.18) | collective-permute-done | bytes 196640 | tf_op jit(solution)/shard_map/ppermute | solution.py:32
  71.2 1.8 %shard_map.156 = (bf16[128,2048]{1,0:T(8,128)(2,1)S(1)}, bf16[128,2048]{1,0:T(8,128)(2,1)S(1)}, bf16[128,2048]{1,0:T(8,128)(2,1)S(1)}, bf16[128,2048]{1,0:T(8,128)(2,1)S(1)}) custom-call(bf16[512,768]{1,0:T(8,128)(2,1)S(1)} %get-tuple-element.69.g_ref, bf16[256,768]{1,0:T(8,128)(2,1)S(1)} %convert_bitcast_fusion.refs_0_, ...), custom_call_target="tpu_custom_call" | custom-call | flops 1610612736 | bytes 6029312 | tf_op jit(solution)/shard_map/pallas_call | solution.py:168
  73.2 3.0 %collective-permute-start.35 = (bf16[256,512]{1,0:T(8,128)(2,1)S(1)}, bf16[256,512]{1,0:T(8,128)(2,1)S(1)}, u32[]{:S(2)}, u32[]{:S(2)}) collective-permute-start(bf16[256,512]{1,0:T(8,128)(2,1)S(1)} %convert_element_type.49), channel_id=1, source_target_pairs={{0,128},{32,160},{64,192},{96,224},{128,0},{160,32},{192,64},{224,... | collective-permute-start | bytes 786440 | tf_op jit(solution)/shard_map/ppermute | solution.py:337
  76.2 3.4 %collective-permute-start.20 = (bf16[128,2048]{1,0:T(8,128)(2,1)S(1)}, bf16[128,2048]{1,0:T(8,128)(2,1)S(1)}, u32[]{:S(2)}, u32[]{:S(2)}) collective-permute-start(bf16[128,2048]{1,0:T(8,128)(2,1)S(1)} %get-tuple-element.59), channel_id=1, source_target_pairs={{0,1},{1,0},{2,3},{3,2},{4,5},{5,4},{6,7},{7,6},{8,9},{9,8},{10,11... | collective-permute-start | bytes 1572872 | tf_op jit(solution)/shard_map/ppermute | solution.py:38
  79.8 1.8 %collective-permute-start.22 = (bf16[128,2048]{1,0:T(8,128)(2,1)S(1)}, bf16[128,2048]{1,0:T(8,128)(2,1)S(1)}, u32[]{:S(2)}, u32[]{:S(2)}) collective-permute-start(bf16[128,2048]{1,0:T(8,128)(2,1)S(1)} %get-tuple-element.61), channel_id=1, source_target_pairs={{0,17},{1,16},{2,19},{3,18},{4,21},{5,20},{6,23},{7,22},{8,25},{9,... | collective-permute-start | bytes 1572872 | tf_op jit(solution)/shard_map/ppermute | solution.py:38
  81.9 2.7 %collective-permute-start.32 = (bf16[256,768]{1,0:T(8,128)(2,1)S(1)}, bf16[256,768]{1,0:T(8,128)(2,1)S(1)}, u32[]{:S(2)}, u32[]{:S(2)}) collective-permute-start(bf16[256,768]{1,0:T(8,128)(2,1)S(1)} %get-tuple-element.83), channel_id=1, source_target_pairs={{0,14},{1,15},{2,0},{3,1},{4,2},{5,3},{6,4},{7,5},{8,6},{9,7},{10,... | collective-permute-start | bytes 1179656 | tf_op jit(solution)/shard_map/ppermute | solution.py:32
  84.5 1.2 %fusion.1 = (f32[1,256,512]{2,1,0:T(8,128)}, f32[1,256,512]{2,1,0:T(8,128)}) fusion(f32[1,256,512]{2,1,0:T(8,128)S(1)} %copy-done.6, f32[1,256,512]{2,1,0:T(8,128)S(1)} %copy-done.7, f32[256,512]{1,0:T(8,128)S(1)} %convert_add_fusion.1, bf16[256,512]{1,0:T(8,128)(2,1)S(1)} %collective-permute-done.35, pred[]{:T(512)S(6)} %eq.32), kind=kLoop, calls=%fused_computation.4 | loop fusion | flops 1179648 | bytes 2883585 | tf_op jit(solution)/shard_map/broadcast_in_dim | solution.py:341
  85.7 7.4 %collective-permute-done.21.refs_2_ = bf16[128,2048]{1,0:T(8,128)(2,1)S(1)} collective-permute-done((bf16[128,2048]{1,0:T(8,128)(2,1)S(1)}, bf16[128,2048]{1,0:T(8,128)(2,1)S(1)}, u32[]{:S(2)}, u32[]{:S(2)}) %collective-permute-start.21) | collective-permute-done | bytes 524320 | tf_op jit(solution)/shard_map/ppermute | solution.py:38
  93.2 11.3 %collective-permute-done.22.refs_3_ = bf16[128,2048]{1,0:T(8,128)(2,1)S(1)} collective-permute-done((bf16[128,2048]{1,0:T(8,128)(2,1)S(1)}, bf16[128,2048]{1,0:T(8,128)(2,1)S(1)}, u32[]{:S(2)}, u32[]{:S(2)}) %collective-permute-start.22) | collective-permute-done | bytes 524320 | tf_op jit(solution)/shard_map/ppermute | solution.py:38
  104.5 2.1 %shard_map.157 = bf16[128,8192]{1,0:T(8,128)(2,1)} custom-call(s32[5]{0:T(128)S(1)} %stack.60.base_ref, bf16[128,2048]{1,0:T(8,128)(2,1)S(1)} %get-tuple-element.58.refs_0_, bf16[128,2048]{1,0:T(8,128)(2,1)S(1)} %collective-permute-done.20.refs_1_, bf16[128,2048]{1,0:T(8,128)(2,1)S(1)} %collective-permute-done.21.refs_2_, ...), custom_call_target="tpu_custom_call" | custom-call | bytes 4194304 | tf_op jit(solution)/shard_map/pallas_call | solution.py:142
  106.7 2.2 %shard_map.163 = (f32[1,256,768]{2,1,0:T(8,128)}, f32[1,256,768]{2,1,0:T(8,128)}, f32[1,256,768]{2,1,0:T(8,128)}) custom-call(bf16[256,768]{1,0:T(8,128)(2,1)S(1)} %collective-permute-done.31.f_ref, bf16[256,768]{1,0:T(8,128)(2,1)S(1)} %collective-permute-done.32.b_ref, bf16[256,768]{1,0:T(8,128)(2,1)S(1)} %get-tuple-element.85.o_ref, ...), custom_call_target="tpu_custom_call" | custom-call | flops 3932160 | bytes 5898240 | tf_op jit(solution)/shard_map/pallas_call | solution.py:312
  (77 shorter events, 4.2 us)
Async XLA Ops:
  0.6 39.3 %copy-start.5 = (bf16[128,768]{1,0:T(8,128)(2,1)S(1)}, bf16[128,768]{1,0:T(8,128)(2,1)}, u32[]{:S(2)}) copy-start(bf16[128,768]{1,0:T(8,128)(2,1)} %cot.1) | copy-start | bytes 589828
  0.6 11.5 %collective-permute-start = (s32[128]{0:T(128)}, s32[128]{0:T(128)S(1)}, u32[]{:S(2)}, u32[]{:S(2)}) collective-permute-start(s32[128]{0:T(128)} %param.11), channel_id=1, source_target_pairs={{0,1},{1,0},{2,3},{3,2},{4,5},{5,4},{6,7},{7,6},{8,9},{9,8},{10,11... | collective-permute-start | bytes 1544 | tf_op jit(solution)/shard_map/ppermute | solution.py:38
  4.0 9.5 %collective-permute-start.2 = (s32[128]{0:T(128)}, s32[128]{0:T(128)S(1)}, u32[]{:S(2)}, u32[]{:S(2)}) collective-permute-start(s32[128]{0:T(128)} %param.11), channel_id=1, source_target_pairs={{0,17},{1,16},{2,19},{3,18},{4,21},{5,20},{6,23},{7,22},{8,25},{9,... | collective-permute-start | bytes 1544 | tf_op jit(solution)/shard_map/ppermute | solution.py:38
  4.0 9.5 %collective-permute-start.1 = (s32[128]{0:T(128)}, s32[128]{0:T(128)S(1)}, u32[]{:S(2)}, u32[]{:S(2)}) collective-permute-start(s32[128]{0:T(128)} %param.11), channel_id=1, source_target_pairs={{0,16},{1,17},{2,18},{3,19},{4,20},{5,21},{6,22},{7,23},{8,24},{9,... | collective-permute-start | bytes 1544 | tf_op jit(solution)/shard_map/ppermute | solution.py:38
  6.6 16.9 %collective-permute-start.6 = (bf16[256,768]{1,0:T(8,128)(2,1)S(1)}, bf16[256,768]{1,0:T(8,128)(2,1)S(1)}, u32[]{:S(2)}, u32[]{:S(2)}) collective-permute-start(bf16[256,768]{1,0:T(8,128)(2,1)S(1)} %convert_bitcast_fusion.refs_0_), channel_id=1, source_target_pairs={{0,2},{1,3},{2,4},{3,5},{4,6},{5,7},{6,8},{7,9},{8,10},{9,11},{10,... | collective-permute-start | bytes 1179656 | tf_op jit(solution)/shard_map/ppermute | solution.py:32
  6.7 16.9 %collective-permute-start.5 = (bf16[256,768]{1,0:T(8,128)(2,1)S(1)}, bf16[256,768]{1,0:T(8,128)(2,1)S(1)}, u32[]{:S(2)}, u32[]{:S(2)}) collective-permute-start(bf16[256,768]{1,0:T(8,128)(2,1)S(1)} %convert_bitcast_fusion.refs_0_), channel_id=1, source_target_pairs={{0,14},{1,15},{2,0},{3,1},{4,2},{5,3},{6,4},{7,5},{8,6},{9,7},{10,... | collective-permute-start | bytes 1179656 | tf_op jit(solution)/shard_map/ppermute | solution.py:32
  12.2 10.2 %collective-permute-start.12 = (bf16[128,768]{1,0:T(8,128)(2,1)}, bf16[128,768]{1,0:T(8,128)(2,1)S(1)}, u32[]{:S(2)}, u32[]{:S(2)}) collective-permute-start(bf16[128,768]{1,0:T(8,128)(2,1)} %cot.1), channel_id=1, source_target_pairs={{0,16},{1,17},{2,18},{3,19},{4,20},{5,21},{6,22},{7,23},{8,24},{9,... | collective-permute-start | bytes 589832 | tf_op jit(solution)/shard_map/ppermute | solution.py:38
  14.3 5.5 %collective-permute-start.4 = (s32[8,4]{0,1:T(4,128)S(1)}, s32[8,4]{0,1:T(4,128)S(1)}, u32[]{:S(2)}, u32[]{:S(2)}) collective-permute-start(s32[8,4]{0,1:T(4,128)S(1)} %broadcast_select_fusion), channel_id=1, source_target_pairs={{0,14},{1,15},{2,0},{3,1},{4,2},{5,3},{6,4},{7,5},{8,6},{9,7},{10,... | collective-permute-start | bytes 392 | tf_op jit(solution)/shard_map/ppermute | solution.py:32
  15.7 4.5 %collective-permute-start.3 = (s32[8,4]{0,1:T(4,128)S(1)}, s32[8,4]{0,1:T(4,128)S(1)}, u32[]{:S(2)}, u32[]{:S(2)}) collective-permute-start(s32[8,4]{0,1:T(4,128)S(1)} %broadcast_select_fusion), channel_id=1, source_target_pairs={{0,2},{1,3},{2,4},{3,5},{4,6},{5,7},{6,8},{7,9},{8,10},{9,11},{10,... | collective-permute-start | bytes 392 | tf_op jit(solution)/shard_map/ppermute | solution.py:32
  16.0 1.6 %copy-start.1 = (bf16[128,8192]{1,0:T(8,128)(2,1)S(1)}, bf16[128,8192]{1,0:T(8,128)(2,1)}, u32[]{:S(2)}) copy-start(bf16[128,8192]{1,0:T(8,128)(2,1)} %in_ref.1) | copy-start | bytes 6291460
  17.6 0.9 copy-start.4
  19.8 23.6 %copy-start.6 = (f32[1,256,512]{2,1,0:T(8,128)S(1)}, f32[1,256,512]{2,1,0:T(8,128)}, u32[]{:S(2)}) copy-start(f32[1,256,512]{2,1,0:T(8,128)} %param.19) | copy-start | bytes 1572868
  19.9 23.6 %copy-start.7 = (f32[1,256,512]{2,1,0:T(8,128)S(1)}, f32[1,256,512]{2,1,0:T(8,128)}, u32[]{:S(2)}) copy-start(f32[1,256,512]{2,1,0:T(8,128)} %param.18) | copy-start | bytes 1572868
  19.9 12.7 %collective-permute-start.10 = (bf16[128,768]{1,0:T(8,128)(2,1)S(1)}, bf16[128,768]{1,0:T(8,128)(2,1)S(1)}, u32[]{:S(2)}, u32[]{:S(2)}) collective-permute-start(bf16[128,768]{1,0:T(8,128)(2,1)S(1)} %get-tuple-element.52), channel_id=1, source_target_pairs={{0,16},{1,17},{2,18},{3,19},{4,20},{5,21},{6,22},{7,23},{8,24},{9,... | collective-permute-start | bytes 589832 | tf_op jit(solution)/shard_map/ppermute | solution.py:38
  20.2 14.9 %collective-permute-start.9 = (bf16[128,2816]{1,0:T(8,128)(2,1)S(1)}, bf16[128,2816]{1,0:T(8,128)(2,1)S(1)}, u32[]{:S(2)}, u32[]{:S(2)}) collective-permute-start(bf16[128,2816]{1,0:T(8,128)(2,1)S(1)} %get-tuple-element.50), channel_id=1, source_target_pairs={{0,1},{1,0},{2,3},{3,2},{4,5},{5,4},{6,7},{7,6},{8,9},{9,8},{10,11... | collective-permute-start | bytes 2162696 | tf_op jit(solution)/shard_map/ppermute | solution.py:38
  22.4 12.3 %collective-permute-start.11 = (bf16[128,768]{1,0:T(8,128)(2,1)S(1)}, bf16[128,768]{1,0:T(8,128)(2,1)S(1)}, u32[]{:S(2)}, u32[]{:S(2)}) collective-permute-start(bf16[128,768]{1,0:T(8,128)(2,1)S(1)} %get-tuple-element.53), channel_id=1, source_target_pairs={{0,17},{1,16},{2,19},{3,18},{4,21},{5,20},{6,23},{7,22},{8,25},{9,... | collective-permute-start | bytes 589832 | tf_op jit(solution)/shard_map/ppermute | solution.py:38
  23.5 4.2 %collective-permute-start.8 = (s32[8,4]{0,1:T(4,128)S(1)}, s32[8,4]{0,1:T(4,128)S(1)}, u32[]{:S(2)}, u32[]{:S(2)}) collective-permute-start(s32[8,4]{0,1:T(4,128)S(1)} %maximum_maximum_fusion.1), channel_id=1, source_target_pairs={{0,10},{1,11},{2,12},{3,13},{4,14},{5,15},{6,0},{7,1},{8,2},{9,3},... | collective-permute-start | bytes 392 | tf_op jit(solution)/shard_map/ppermute | solution.py:32
  26.3 5.4 %collective-permute-start.7 = (s32[8,4]{0,1:T(4,128)S(1)}, s32[8,4]{0,1:T(4,128)S(1)}, u32[]{:S(2)}, u32[]{:S(2)}) collective-permute-start(s32[8,4]{0,1:T(4,128)S(1)} %maximum_maximum_fusion.1), channel_id=1, source_target_pairs={{0,6},{1,7},{2,8},{3,9},{4,10},{5,11},{6,12},{7,13},{8,14},{9,15},... | collective-permute-start | bytes 392 | tf_op jit(solution)/shard_map/ppermute | solution.py:32
  27.8 12.1 %collective-permute-start.13 = (bf16[128,768]{1,0:T(8,128)(2,1)S(1)}, bf16[128,768]{1,0:T(8,128)(2,1)S(1)}, u32[]{:S(2)}, u32[]{:S(2)}) collective-permute-start(bf16[128,768]{1,0:T(8,128)(2,1)S(1)} %collective-permute-done.12.cot_2), channel_id=1, source_target_pairs={{0,1},{1,0},{2,3},{3,2},{4,5},{5,4},{6,7},{7,6},{8,9},{9,8},{10,11... | collective-permute-start | bytes 589832 | tf_op jit(solution)/shard_map/ppermute | solution.py:38
  31.7 9.9 %collective-permute-start.15 = (bf16[256,768]{1,0:T(8,128)(2,1)S(1)}, bf16[256,768]{1,0:T(8,128)(2,1)S(1)}, u32[]{:S(2)}, u32[]{:S(2)}) collective-permute-start(bf16[256,768]{1,0:T(8,128)(2,1)S(1)} %collective-permute-done.6.refs_2_), channel_id=1, source_target_pairs={{0,2},{1,3},{2,4},{3,5},{4,6},{5,7},{6,8},{7,9},{8,10},{9,11},{10,... | collective-permute-start | bytes 1179656 | tf_op jit(solution)/shard_map/ppermute | solution.py:32
  32.6 12.1 %collective-permute-start.14 = (bf16[256,768]{1,0:T(8,128)(2,1)S(1)}, bf16[256,768]{1,0:T(8,128)(2,1)S(1)}, u32[]{:S(2)}, u32[]{:S(2)}) collective-permute-start(bf16[256,768]{1,0:T(8,128)(2,1)S(1)} %collective-permute-done.5.refs_1_), channel_id=1, source_target_pairs={{0,14},{1,15},{2,0},{3,1},{4,2},{5,3},{6,4},{7,5},{8,6},{9,7},{10,... | collective-permute-start | bytes 1179656 | tf_op jit(solution)/shard_map/ppermute | solution.py:32
  34.8 14.1 %collective-permute-start.27 = (bf16[128,1280]{1,0:T(8,128)(2,1)S(1)}, bf16[128,1280]{1,0:T(8,128)(2,1)S(1)}, u32[]{:S(2)}, u32[]{:S(2)}) collective-permute-start(bf16[128,1280]{1,0:T(8,128)(2,1)S(1)} %get-tuple-element.71), channel_id=1, source_target_pairs={{0,16},{1,17},{2,18},{3,19},{4,20},{5,21},{6,22},{7,23},{8,24},{9,... | collective-permute-start | bytes 983048 | tf_op jit(solution)/shard_map/ppermute | solution.py:38
  35.2 16.1 %collective-permute-start.28 = (bf16[128,1280]{1,0:T(8,128)(2,1)S(1)}, bf16[128,1280]{1,0:T(8,128)(2,1)S(1)}, u32[]{:S(2)}, u32[]{:S(2)}) collective-permute-start(bf16[128,1280]{1,0:T(8,128)(2,1)S(1)} %get-tuple-element.73), channel_id=1, source_target_pairs={{0,17},{1,16},{2,19},{3,18},{4,21},{5,20},{6,23},{7,22},{8,25},{9,... | collective-permute-start | bytes 983048 | tf_op jit(solution)/shard_map/ppermute | solution.py:38
  40.7 7.4 %collective-permute-start.23 = (bf16[128,768]{1,0:T(8,128)(2,1)S(1)}, bf16[128,768]{1,0:T(8,128)(2,1)S(1)}, u32[]{:S(2)}, u32[]{:S(2)}) collective-permute-start(bf16[128,768]{1,0:T(8,128)(2,1)S(1)} %get-tuple-element.62), channel_id=1, source_target_pairs={{0,2},{1,3},{2,4},{3,5},{4,6},{5,7},{6,8},{7,9},{8,10},{9,11},{10,... | collective-permute-start | bytes 589832 | tf_op jit(solution)/shard_map/ppermute | solution.py:32
  41.6 7.1 %collective-permute-start.24 = (bf16[128,768]{1,0:T(8,128)(2,1)S(1)}, bf16[128,768]{1,0:T(8,128)(2,1)S(1)}, u32[]{:S(2)}, u32[]{:S(2)}) collective-permute-start(bf16[128,768]{1,0:T(8,128)(2,1)S(1)} %get-tuple-element.63), channel_id=1, source_target_pairs={{0,14},{1,15},{2,0},{3,1},{4,2},{5,3},{6,4},{7,5},{8,6},{9,7},{10,... | collective-permute-start | bytes 589832 | tf_op jit(solution)/shard_map/ppermute | solution.py:32
  44.7 11.8 %collective-permute-start.17 = (bf16[256,768]{1,0:T(8,128)(2,1)S(1)}, bf16[256,768]{1,0:T(8,128)(2,1)S(1)}, u32[]{:S(2)}, u32[]{:S(2)}) collective-permute-start(bf16[256,768]{1,0:T(8,128)(2,1)S(1)} %collective-permute-done.15.refs_4_), channel_id=1, source_target_pairs={{0,2},{1,3},{2,4},{3,5},{4,6},{5,7},{6,8},{7,9},{8,10},{9,11},{10,... | collective-permute-start | bytes 1179656 | tf_op jit(solution)/shard_map/ppermute | solution.py:32
  48.1 10.4 %collective-permute-start.16 = (bf16[256,768]{1,0:T(8,128)(2,1)S(1)}, bf16[256,768]{1,0:T(8,128)(2,1)S(1)}, u32[]{:S(2)}, u32[]{:S(2)}) collective-permute-start(bf16[256,768]{1,0:T(8,128)(2,1)S(1)} %collective-permute-done.14.refs_3_), channel_id=1, source_target_pairs={{0,14},{1,15},{2,0},{3,1},{4,2},{5,3},{6,4},{7,5},{8,6},{9,7},{10,... | collective-permute-start | bytes 1179656 | tf_op jit(solution)/shard_map/ppermute | solution.py:32
  52.5 9.4 %collective-permute-start.33 = (bf16[256,512]{1,0:T(8,128)(2,1)S(1)}, bf16[256,512]{1,0:T(8,128)(2,1)S(1)}, u32[]{:S(2)}, u32[]{:S(2)}) collective-permute-start(bf16[256,512]{1,0:T(8,128)(2,1)S(1)} %convert_element_type.45), channel_id=1, source_target_pairs={{0,32},{32,0},{64,96},{96,64},{128,160},{160,128},{192,224},{224,1... | collective-permute-start | bytes 786440 | tf_op jit(solution)/shard_map/ppermute | solution.py:337
  55.0 11.9 %collective-permute-start.26 = (bf16[256,768]{1,0:T(8,128)(2,1)S(1)}, bf16[256,768]{1,0:T(8,128)(2,1)S(1)}, u32[]{:S(2)}, u32[]{:S(2)}) collective-permute-start(bf16[256,768]{1,0:T(8,128)(2,1)S(1)} %get-tuple-element.68), channel_id=1, source_target_pairs={{0,14},{1,15},{2,0},{3,1},{4,2},{5,3},{6,4},{7,5},{8,6},{9,7},{10,... | collective-permute-start | bytes 1179656 | tf_op jit(solution)/shard_map/ppermute | solution.py:32
  56.0 11.0 %collective-permute-start.25 = (bf16[256,768]{1,0:T(8,128)(2,1)S(1)}, bf16[256,768]{1,0:T(8,128)(2,1)S(1)}, u32[]{:S(2)}, u32[]{:S(2)}) collective-permute-start(bf16[256,768]{1,0:T(8,128)(2,1)S(1)} %get-tuple-element.67), channel_id=1, source_target_pairs={{0,2},{1,3},{2,4},{3,5},{4,6},{5,7},{6,8},{7,9},{8,10},{9,11},{10,... | collective-permute-start | bytes 1179656 | tf_op jit(solution)/shard_map/ppermute | solution.py:32
  56.5 14.5 %collective-permute-start.18 = (bf16[128,768]{1,0:T(8,128)(2,1)S(1)}, bf16[128,768]{1,0:T(8,128)(2,1)S(1)}, u32[]{:S(2)}, u32[]{:S(2)}) collective-permute-start(bf16[128,768]{1,0:T(8,128)(2,1)S(1)} %slice.8), channel_id=1, source_target_pairs={{0,2},{1,3},{2,4},{3,5},{4,6},{5,7},{6,8},{7,9},{8,10},{9,11},{10,... | collective-permute-start | bytes 589832 | tf_op jit(solution)/shard_map/ppermute | solution.py:32
  58.6 12.6 %collective-permute-start.19 = (bf16[128,768]{1,0:T(8,128)(2,1)S(1)}, bf16[128,768]{1,0:T(8,128)(2,1)S(1)}, u32[]{:S(2)}, u32[]{:S(2)}) collective-permute-start(bf16[128,768]{1,0:T(8,128)(2,1)S(1)} %slice.9), channel_id=1, source_target_pairs={{0,14},{1,15},{2,0},{3,1},{4,2},{5,3},{6,4},{7,5},{8,6},{9,7},{10,... | collective-permute-start | bytes 589832 | tf_op jit(solution)/shard_map/ppermute | solution.py:32
  61.9 11.1 %collective-permute-start.34 = (bf16[256,512]{1,0:T(8,128)(2,1)S(1)}, bf16[256,512]{1,0:T(8,128)(2,1)S(1)}, u32[]{:S(2)}, u32[]{:S(2)}) collective-permute-start(bf16[256,512]{1,0:T(8,128)(2,1)S(1)} %fusion.7), channel_id=1, source_target_pairs={{0,64},{32,96},{64,0},{96,32},{128,192},{160,224},{192,128},{224,1... | collective-permute-start | bytes 786440 | tf_op jit(solution)/shard_map/ppermute | solution.py:337
  67.1 12.7 %collective-permute-start.29 = (bf16[256,768]{1,0:T(8,128)(2,1)S(1)}, bf16[256,768]{1,0:T(8,128)(2,1)S(1)}, u32[]{:S(2)}, u32[]{:S(2)}) collective-permute-start(bf16[256,768]{1,0:T(8,128)(2,1)S(1)} %get-tuple-element.77), channel_id=1, source_target_pairs={{0,2},{1,3},{2,4},{3,5},{4,6},{5,7},{6,8},{7,9},{8,10},{9,11},{10,... | collective-permute-start | bytes 1179656 | tf_op jit(solution)/shard_map/ppermute | solution.py:32
  67.2 14.3 %collective-permute-start.30 = (bf16[256,768]{1,0:T(8,128)(2,1)S(1)}, bf16[256,768]{1,0:T(8,128)(2,1)S(1)}, u32[]{:S(2)}, u32[]{:S(2)}) collective-permute-start(bf16[256,768]{1,0:T(8,128)(2,1)S(1)} %get-tuple-element.78), channel_id=1, source_target_pairs={{0,14},{1,15},{2,0},{3,1},{4,2},{5,3},{6,4},{7,5},{8,6},{9,7},{10,... | collective-permute-start | bytes 1179656 | tf_op jit(solution)/shard_map/ppermute | solution.py:32
  73.2 8.7 %collective-permute-start.35 = (bf16[256,512]{1,0:T(8,128)(2,1)S(1)}, bf16[256,512]{1,0:T(8,128)(2,1)S(1)}, u32[]{:S(2)}, u32[]{:S(2)}) collective-permute-start(bf16[256,512]{1,0:T(8,128)(2,1)S(1)} %convert_element_type.49), channel_id=1, source_target_pairs={{0,128},{32,160},{64,192},{96,224},{128,0},{160,32},{192,64},{224,... | collective-permute-start | bytes 786440 | tf_op jit(solution)/shard_map/ppermute | solution.py:337
  76.2 9.5 %collective-permute-start.20 = (bf16[128,2048]{1,0:T(8,128)(2,1)S(1)}, bf16[128,2048]{1,0:T(8,128)(2,1)S(1)}, u32[]{:S(2)}, u32[]{:S(2)}) collective-permute-start(bf16[128,2048]{1,0:T(8,128)(2,1)S(1)} %get-tuple-element.59), channel_id=1, source_target_pairs={{0,1},{1,0},{2,3},{3,2},{4,5},{5,4},{6,7},{7,6},{8,9},{9,8},{10,11... | collective-permute-start | bytes 1572872 | tf_op jit(solution)/shard_map/ppermute | solution.py:38
  79.6 13.6 %collective-permute-start.21 = (bf16[128,2048]{1,0:T(8,128)(2,1)S(1)}, bf16[128,2048]{1,0:T(8,128)(2,1)S(1)}, u32[]{:S(2)}, u32[]{:S(2)}) collective-permute-start(bf16[128,2048]{1,0:T(8,128)(2,1)S(1)} %get-tuple-element.60), channel_id=1, source_target_pairs={{0,16},{1,17},{2,18},{3,19},{4,20},{5,21},{6,22},{7,23},{8,24},{9,... | collective-permute-start | bytes 1572872 | tf_op jit(solution)/shard_map/ppermute | solution.py:38
  79.8 24.7 %collective-permute-start.22 = (bf16[128,2048]{1,0:T(8,128)(2,1)S(1)}, bf16[128,2048]{1,0:T(8,128)(2,1)S(1)}, u32[]{:S(2)}, u32[]{:S(2)}) collective-permute-start(bf16[128,2048]{1,0:T(8,128)(2,1)S(1)} %get-tuple-element.61), channel_id=1, source_target_pairs={{0,17},{1,16},{2,19},{3,18},{4,21},{5,20},{6,23},{7,22},{8,25},{9,... | collective-permute-start | bytes 1572872 | tf_op jit(solution)/shard_map/ppermute | solution.py:38
  81.8 24.9 %collective-permute-start.31 = (bf16[256,768]{1,0:T(8,128)(2,1)S(1)}, bf16[256,768]{1,0:T(8,128)(2,1)S(1)}, u32[]{:S(2)}, u32[]{:S(2)}) collective-permute-start(bf16[256,768]{1,0:T(8,128)(2,1)S(1)} %get-tuple-element.82), channel_id=1, source_target_pairs={{0,2},{1,3},{2,4},{3,5},{4,6},{5,7},{6,8},{7,9},{8,10},{9,11},{10,... | collective-permute-start | bytes 1179656 | tf_op jit(solution)/shard_map/ppermute | solution.py:32
  81.9 24.8 %collective-permute-start.32 = (bf16[256,768]{1,0:T(8,128)(2,1)S(1)}, bf16[256,768]{1,0:T(8,128)(2,1)S(1)}, u32[]{:S(2)}, u32[]{:S(2)}) collective-permute-start(bf16[256,768]{1,0:T(8,128)(2,1)S(1)} %get-tuple-element.83), channel_id=1, source_target_pairs={{0,14},{1,15},{2,0},{3,1},{4,2},{5,3},{6,4},{7,5},{8,6},{9,7},{10,... | collective-permute-start | bytes 1179656 | tf_op jit(solution)/shard_map/ppermute | solution.py:32
  85.7 20.9 %copy-start = (f32[1,256,768]{2,1,0:T(8,128)S(1)}, f32[1,256,768]{2,1,0:T(8,128)}, u32[]{:S(2)}) copy-start(f32[1,256,768]{2,1,0:T(8,128)} %w_ref.1) | copy-start | bytes 2359300
  85.7 20.9 %copy-start.2 = (f32[1,256,768]{2,1,0:T(8,128)S(1)}, f32[1,256,768]{2,1,0:T(8,128)}, u32[]{:S(2)}) copy-start(f32[1,256,768]{2,1,0:T(8,128)} %m_ref.1) | copy-start | bytes 2359300
  85.7 21.0 %copy-start.3 = (f32[1,256,768]{2,1,0:T(8,128)S(1)}, f32[1,256,768]{2,1,0:T(8,128)}, u32[]{:S(2)}) copy-start(f32[1,256,768]{2,1,0:T(8,128)} %v_ref.1) | copy-start | bytes 2359300
